TPU v7x, 32 devices: a whole 2x2x4 slice. The times are simulated.
32 devices in a mesh: groups: 2 (over x), tm: 16 (over z, y, core).
Axes of the slice: x: 2, y: 2, z: 4, core: 2. Of those that a mesh axis runs over, the one named last changes fastest.
Arguments:
- queries: bfloat16 [12288, 1280], P(('groups', 'tm')), parts along dimension 0, may hold values from -110 to 110
- key_rows: bfloat16 [12288, 1280], P(('groups', 'tm')), parts along dimension 0, may hold values from -6 to 6
- value_rows: bfloat16 [12288, 1280], P(('groups', 'tm')), parts along dimension 0, may hold values from -6 to 6
- out_grad: bfloat16 [12288, 1280], P(('groups', 'tm')), parts along dimension 0, may hold values from -6 to 6
- block_lists: int32 [96, 8], P(('groups', 'tm')), parts along dimension 0, may hold values from 0 to 47, as said below
- list_counts: int32 [96], P(('groups', 'tm')), parts along dimension 0, may hold values from 4 to 8, as said below
Outputs:
- attended: bfloat16 [12288, 1280], P(('groups', 'tm')), parts along dimension 0
- query_grad: bfloat16 [12288, 1280], P(('groups', 'tm')), parts along dimension 0
- key_grad: bfloat16 [12288, 1280], P(('groups', 'tm')), parts along dimension 0
- value_grad: bfloat16 [12288, 1280], P(('groups', 'tm')), parts along dimension 0
There are 2 independent parts, one for each index of `groups`. A program takes and returns all parts, laid end to end along the dimension named above; each array names one. Nothing has to cross between parts.
Inputs may be any that keep to these rules, and one draw needn't show every extreme that they name: `block_lists`: the first list_counts[g] entries of row g are distinct blocks lying in the shards at most two away from the shard of block g (a shard holds 3 blocks); the other entries equal g. `list_counts`: how many leading entries of a row of block_lists count.
All inputs are finite; a program needn't handle non-finite values.
Results may differ from a plain program's by a relative error of at most 0.023.
Values may be sent and summed in bfloat16 or wider, within the bound.
No kernel may reach another device: no remote copies, remote signals or barrier semaphores. Data moves between devices by JAX's collectives and lax.ppermute only.
A program may use at most 192 MiB of HBM per device.

v0:
```python
import math

import jax
import jax.numpy as jnp
from jax import lax
from jax.sharding import PartitionSpec as P

HEADS = 20
HEAD_DIM = 64
BLK = 128
LIST = 8


def shifted(block, axis, distance):
    devices = range(lax.axis_size(axis))
    route = [(i - distance, i) for i in devices if i - distance in devices]
    return lax.ppermute(block, axis, route)


def head_group(query_cols, key_cols, value_cols, grad_cols, live_keys, score_scale, group_heads):
    block_count = query_cols.shape[0]
    query_heads = query_cols.reshape(block_count, BLK, group_heads, HEAD_DIM)
    key_heads = key_cols.reshape(block_count, LIST * BLK, group_heads, HEAD_DIM)
    value_heads = value_cols.reshape(block_count, LIST * BLK, group_heads, HEAD_DIM)
    grad_heads = grad_cols.reshape(block_count, BLK, group_heads, HEAD_DIM)
    scores = (
        jnp.einsum("bqhe,bkhe->bhqk", query_heads, key_heads, preferred_element_type=jnp.float32)
        * score_scale
    )
    scores = jnp.where(live_keys[:, None, None, :], scores, -jnp.inf)
    row_max = jnp.max(scores, axis=-1, keepdims=True)
    raised = jnp.exp(scores - row_max)
    row_sum = jnp.sum(raised, axis=-1, keepdims=True)
    weights = raised / row_sum
    weights_low = weights.astype(jnp.bfloat16)
    attended = jnp.einsum(
        "bhqk,bkhe->bqhe", weights_low, value_heads, preferred_element_type=jnp.float32
    ).astype(jnp.bfloat16)
    row_dot = jnp.sum(grad_heads.astype(jnp.float32) * attended.astype(jnp.float32), axis=-1)
    weight_grad = jnp.einsum(
        "bqhe,bkhe->bhqk", grad_heads, value_heads, preferred_element_type=jnp.float32
    )
    dscore = (weights * (weight_grad - jnp.transpose(row_dot, (0, 2, 1))[..., None])).astype(
        jnp.bfloat16
    )
    query_grad = (
        jnp.einsum("bhqk,bkhe->bqhe", dscore, key_heads, preferred_element_type=jnp.float32)
        * score_scale
    ).astype(jnp.bfloat16)
    group_width = group_heads * HEAD_DIM
    row_stats = (
        jnp.transpose(row_max[..., 0], (0, 2, 1)),
        jnp.transpose(row_sum[..., 0], (0, 2, 1)),
        row_dot,
    )
    key_part = (
        jnp.einsum("bhqk,bqhe->bkhe", dscore, query_heads, preferred_element_type=jnp.float32)
        * score_scale
    )
    value_part = jnp.einsum(
        "bhqk,bqhe->bkhe", weights_low, grad_heads, preferred_element_type=jnp.float32
    )
    key_part = key_part.reshape(block_count * LIST, BLK, group_width)
    value_part = value_part.reshape(block_count * LIST, BLK, group_width)
    return (
        attended.reshape(block_count, BLK, group_width),
        query_grad.reshape(block_count, BLK, group_width),
        key_part,
        value_part,
        row_stats,
    )


def local(queries, key_rows, value_rows, out_grad, block_lists, list_counts):
    tok_rows, feature_width = queries.shape
    local_blocks = tok_rows // BLK
    paired = jnp.stack([key_rows, value_rows], 0)
    neighbours = {}
    for offset in (2, 1, -1, -2):
        neighbours[offset] = shifted(paired, "tm", offset)
    window = jnp.concatenate(
        [neighbours[2], neighbours[1], paired, neighbours[-1], neighbours[-2]], axis=1
    )
    shard_index = lax.axis_index("tm")
    first_block = (shard_index - 2) * local_blocks
    listed_flat = (block_lists - first_block).reshape(-1)
    window_blocks = window.reshape(2, 5 * local_blocks, BLK, feature_width)
    chosen = window_blocks[:, listed_flat]
    key_sel = chosen[0].reshape(local_blocks, LIST * BLK, feature_width)
    value_sel = chosen[1].reshape(local_blocks, LIST * BLK, feature_width)
    slot_ids = jnp.arange(LIST, dtype=jnp.int32)
    live_keys = jnp.repeat(slot_ids[None, :] < list_counts[:, None], BLK, axis=1)
    query_blocks = queries.reshape(local_blocks, BLK, feature_width)
    grad_blocks = out_grad.reshape(local_blocks, BLK, feature_width)
    group_heads = 4
    group_width = group_heads * HEAD_DIM
    group_total = HEADS // group_heads
    score_scale = 1.0 / math.sqrt(HEAD_DIM)
    output_start = jnp.zeros((local_blocks, BLK, feature_width), jnp.bfloat16)

    def per_group(group_index, running):
        attended_all, query_all, grad_keys, grad_values = running
        column = group_index * group_width

        def columns(source):
            return lax.dynamic_slice_in_dim(source, column, group_width, source.ndim - 1)

        attended, query_grad, key_part, value_part, row_stats = head_group(
            columns(query_blocks),
            columns(key_sel),
            columns(value_sel),
            columns(grad_blocks),
            live_keys,
            score_scale,
            group_heads,
        )
        attended_all = lax.dynamic_update_slice_in_dim(attended_all, attended, column, 2)
        query_all = lax.dynamic_update_slice_in_dim(query_all, query_grad, column, 2)
        key_cols = columns(grad_keys).at[listed_flat].add(key_part)
        value_cols = columns(grad_values).at[listed_flat].add(value_part)
        grad_keys = lax.dynamic_update_slice_in_dim(grad_keys, key_cols, column, 2)
        grad_values = lax.dynamic_update_slice_in_dim(grad_values, value_cols, column, 2)
        return (attended_all, query_all, grad_keys, grad_values)

    window_start = jnp.zeros((5 * local_blocks, BLK, feature_width), jnp.float32)
    attended_all, query_all, grad_keys, grad_values = lax.fori_loop(
        0, group_total, per_group, (output_start, output_start, window_start, window_start)
    )
    grad_pair = jnp.stack([grad_keys, grad_values], 0).reshape(2, 5, tok_rows, feature_width)
    summed = grad_pair[:, 2]
    for offset in (-2, -1, 1, 2):
        summed = summed + shifted(
            grad_pair[:, offset + 2].astype(jnp.bfloat16), "tm", offset
        ).astype(jnp.float32)
    key_grad = summed[0].astype(jnp.bfloat16)
    value_grad = summed[1].astype(jnp.bfloat16)
    return (
        attended_all.reshape(tok_rows, feature_width),
        query_all.reshape(tok_rows, feature_width),
        key_grad,
        value_grad,
    )


def solution(mesh):
    placed = (
        P(("groups", "tm"), None),
        P(("groups", "tm"), None),
        P(("groups", "tm"), None),
        P(("groups", "tm"), None),
        P(("groups", "tm"), None),
        P(("groups", "tm")),
    )
    return jax.shard_map(
        local,
        mesh=mesh,
        in_specs=placed,
        out_specs=(
            P(("groups", "tm"), None),
            P(("groups", "tm"), None),
            P(("groups", "tm"), None),
            P(("groups", "tm"), None),
        ),
        check_vma=False,
    )
```

profile of v0, /device:TPU:1, one launch (start us, length us, event | category | flops | bytes accessed | tf_op | source)
XLA Modules:
  0.0 724.0 jit_solution(4737088905888134957)
XLA Ops:
  2.3 5.3 collective-permute-start
  14.8 96.2 %collective-permute-done = bf16[2,384,1280]{2,1,0:T(8,128)(2,1)} collective-permute-done((bf16[2,384,1280]{2,1,0:T(8,128)(2,1)S(1)}, bf16[2,384,1280]{2,1,0:T(8,128)(2,1)}, u32[]{:S(2)}, u32[]{:S(2)}) %collective-permute-start) | collective-permute-done | bytes 1966112 | tf_op jit(solution)/shard_map/ppermute | solution.py:17
  113.9 19.3 %collective-permute-done.1 = bf16[2,384,1280]{2,1,0:T(8,128)(2,1)} collective-permute-done((bf16[2,384,1280]{2,1,0:T(8,128)(2,1)S(1)}, bf16[2,384,1280]{2,1,0:T(8,128)(2,1)}, u32[]{:S(2)}, u32[]{:S(2)}) %collective-permute-start.1) | collective-permute-done | bytes 1966112 | tf_op jit(solution)/shard_map/ppermute | solution.py:17
  143.6 11.0 %gather_fusion = bf16[24,2,128,1280]{3,2,1,0:T(8,128)(2,1)} fusion(bf16[2,15,128,1280]{3,2,1,0:T(8,128)(2,1)} %bitcast.2, s32[1024]{0:T(1024)S(1)} %pad_clamp_fusion), kind=kCustom, calls=%fused_computation | custom fusion | bytes 31457376 | tf_op jit(solution)/shard_map/gather | solution.py:88
  154.6 11.0 %fusion.24 = (bf16[1,24,128,1280]{3,2,0,1:T(8,128)(2,1)}, bf16[1,24,128,1280]{3,2,0,1:T(8,128)(2,1)}) fusion(bf16[2,24,128,1280]{3,2,0,1:T(8,128)(2,1)} %bitcast.146), kind=kLoop, calls=%fused_computation.66 | loop fusion | bytes 31457280 | tf_op jit(solution)/shard_map/slice | solution.py:89
  167.7 4.7 broadcast_in_dim.54.clone
  172.3 4.7 broadcast_in_dim.54
  177.1 404.0 %while.20 = (s32[]{:T(128)}, bf16[3,128,1280]{2,1,0:T(8,128)(2,1)}, bf16[3,128,1280]{2,1,0:T(8,128)(2,1)}, f32[15,128,1280]{2,1,0:T(8,128)}, f32[15,128,1280]{2,...) while((s32[]{:T(128)}, bf16[3,128,1280]{2,1,0:T(8,128)(2,1)}, ...), condition=%wide.region_6.7_spmd.clone, body=%wide.region_0.6_spmd.clone.sunk | while | flops 1226735104 | bytes 155561840 | solution.py:126
  191.1 5.7 fusion.67
  211.5 6.6 copy.62
  218.1 6.9 reshape.203
  225.0 9.4 %scatter_fusion.1 = f32[15,128,256]{2,1,0:T(8,128)} fusion(f32[15,128,256]{2,1,0:T(8,128)} %constant_dynamic-slice_fusion.17, s32[24]{0:T(128)S(1)} %fusion.70, f32[24,128,256]{2,1,0:T(8,128)} %reshape.203), kind=kCustom, calls=%fused_computation.1.clone.clone.1 | custom fusion | flops 786432 | bytes 9437280 | tf_op jit(solution)/shard_map/while/body/eval_jaxpr/scatter-add | solution.py:119
  234.4 6.6 copy.61
  240.9 6.9 reshape.202
  247.8 6.1 scatter_fusion
  271.9 5.7 fusion.67
  292.3 6.6 copy.62
  298.9 6.9 reshape.203
  305.8 9.4 %scatter_fusion.1 = f32[15,128,256]{2,1,0:T(8,128)} fusion(f32[15,128,256]{2,1,0:T(8,128)} %constant_dynamic-slice_fusion.17, s32[24]{0:T(128)S(1)} %fusion.70, f32[24,128,256]{2,1,0:T(8,128)} %reshape.203), kind=kCustom, calls=%fused_computation.1.clone.clone.1 | custom fusion | flops 786432 | bytes 9437280 | tf_op jit(solution)/shard_map/while/body/eval_jaxpr/scatter-add | solution.py:119
  315.2 6.6 copy.61
  321.7 6.9 reshape.202
  328.6 6.1 scatter_fusion
  352.7 5.7 fusion.67
  373.2 6.6 copy.62
  379.7 6.9 reshape.203
  386.6 9.4 %scatter_fusion.1 = f32[15,128,256]{2,1,0:T(8,128)} fusion(f32[15,128,256]{2,1,0:T(8,128)} %constant_dynamic-slice_fusion.17, s32[24]{0:T(128)S(1)} %fusion.70, f32[24,128,256]{2,1,0:T(8,128)} %reshape.203), kind=kCustom, calls=%fused_computation.1.clone.clone.1 | custom fusion | flops 786432 | bytes 9437280 | tf_op jit(solution)/shard_map/while/body/eval_jaxpr/scatter-add | solution.py:119
  396.0 6.6 copy.61
  402.5 6.9 reshape.202
  409.4 6.1 scatter_fusion
  433.5 5.7 fusion.67
  453.9 6.6 copy.62
  460.5 6.9 reshape.203
  467.4 9.4 %scatter_fusion.1 = f32[15,128,256]{2,1,0:T(8,128)} fusion(f32[15,128,256]{2,1,0:T(8,128)} %constant_dynamic-slice_fusion.17, s32[24]{0:T(128)S(1)} %fusion.70, f32[24,128,256]{2,1,0:T(8,128)} %reshape.203), kind=kCustom, calls=%fused_computation.1.clone.clone.1 | custom fusion | flops 786432 | bytes 9437280 | tf_op jit(solution)/shard_map/while/body/eval_jaxpr/scatter-add | solution.py:119
  476.8 6.6 copy.61
  483.3 6.9 reshape.202
  490.2 6.1 scatter_fusion
  514.3 5.7 fusion.67
  534.8 6.6 copy.62
  541.3 6.9 reshape.203
  548.2 9.4 %scatter_fusion.1 = f32[15,128,256]{2,1,0:T(8,128)} fusion(f32[15,128,256]{2,1,0:T(8,128)} %constant_dynamic-slice_fusion.17, s32[24]{0:T(128)S(1)} %fusion.70, f32[24,128,256]{2,1,0:T(8,128)} %reshape.203), kind=kCustom, calls=%fused_computation.1.clone.clone.1 | custom fusion | flops 786432 | bytes 9437280 | tf_op jit(solution)/shard_map/while/body/eval_jaxpr/scatter-add | solution.py:119
  557.6 6.6 copy.61
  564.2 6.9 reshape.202
  571.0 6.1 scatter_fusion
  581.1 9.5 %fusion.14 = bf16[2,5,384,1280]{3,2,0,1:T(8,128)(2,1)S(1)} fusion(f32[1,5,384,1280]{3,2,0,1:T(8,128)} %bitcast.132, f32[1,5,384,1280]{3,2,0,1:T(8,128)} %bitcast.136), kind=kLoop, calls=%fused_computation.40 | loop fusion | flops 4915200 | bytes 29491200 | tf_op jit(solution)/shard_map/convert.5
  596.9 7.0 collective-permute-start.6
  605.9 29.7 %collective-permute-done.4 = bf16[2,384,1280]{2,1,0:T(8,128)(2,1)S(1)} collective-permute-done((bf16[2,384,1280]{2,1,0:T(8,128)(2,1)S(1)}, bf16[2,384,1280]{2,1,0:T(8,128)(2,1)S(1)}, u32[]{:S(2)}, u32[]{:S(2)}) %collective-permute-start.4) | collective-permute-done | bytes 1966112 | tf_op jit(solution)/shard_map/ppermute | solution.py:17
  635.5 64.7 %collective-permute-done.7 = bf16[2,384,1280]{2,1,0:T(8,128)(2,1)S(1)} collective-permute-done((bf16[2,384,1280]{2,1,0:T(8,128)(2,1)S(1)}, bf16[2,384,1280]{2,1,0:T(8,128)(2,1)S(1)}, u32[]{:S(2)}, u32[]{:S(2)}) %collective-permute-start.7) | collective-permute-done | bytes 1966112 | tf_op jit(solution)/shard_map/ppermute | solution.py:17
  700.2 21.2 %collective-permute-done.6 = bf16[2,384,1280]{2,1,0:T(8,128)(2,1)S(1)} collective-permute-done((bf16[2,384,1280]{2,1,0:T(8,128)(2,1)S(1)}, bf16[2,384,1280]{2,1,0:T(8,128)(2,1)S(1)}, u32[]{:S(2)}, u32[]{:S(2)}) %collective-permute-start.6) | collective-permute-done | bytes 1966112 | tf_op jit(solution)/shard_map/ppermute | solution.py:17
  (278 shorter events, 197.7 us)
Async XLA Ops:
  0.6 13.9 %copy-start.9 = (s32[3,8]{1,0:T(4,128)S(1)}, s32[3,8]{1,0:T(4,128)}, u32[]{:S(2)}) copy-start(s32[3,8]{1,0:T(4,128)} %param.12) | copy-start | bytes 292
  0.6 14.1 %copy-start.12 = (s32[3]{0:T(128)S(1)}, s32[3]{0:T(128)}, u32[]{:S(2)}) copy-start(s32[3]{0:T(128)} %param.13) | copy-start | bytes 40
  2.3 108.7 %collective-permute-start = (bf16[2,384,1280]{2,1,0:T(8,128)(2,1)S(1)}, bf16[2,384,1280]{2,1,0:T(8,128)(2,1)}, u32[]{:S(2)}, u32[]{:S(2)}) collective-permute-start(bf16[2,384,1280]{2,1,0:T(8,128)(2,1)S(1)} %pad_maximum_fusion.1), channel_id=1, source_target_pairs={{0,2},{1,3},{2,4},{3,5},{4,6},{5,7},{6,8},{7,9},{8,10},{9,11},{10,... | collective-permute-start | bytes 5898248 | tf_op jit(solution)/shard_map/ppermute | solution.py:17
  7.6 125.6 %collective-permute-start.1 = (bf16[2,384,1280]{2,1,0:T(8,128)(2,1)S(1)}, bf16[2,384,1280]{2,1,0:T(8,128)(2,1)}, u32[]{:S(2)}, u32[]{:S(2)}) collective-permute-start(bf16[2,384,1280]{2,1,0:T(8,128)(2,1)S(1)} %pad_maximum_fusion.1), channel_id=1, source_target_pairs={{0,1},{1,2},{2,3},{3,4},{4,5},{5,6},{6,7},{7,8},{8,9},{9,10},{10,1... | collective-permute-start | bytes 5898248 | tf_op jit(solution)/shard_map/ppermute | solution.py:17
  10.3 127.3 %collective-permute-start.2 = (bf16[2,384,1280]{2,1,0:T(8,128)(2,1)S(1)}, bf16[2,384,1280]{2,1,0:T(8,128)(2,1)}, u32[]{:S(2)}, u32[]{:S(2)}) collective-permute-start(bf16[2,384,1280]{2,1,0:T(8,128)(2,1)S(1)} %pad_maximum_fusion.1), channel_id=1, source_target_pairs={{1,0},{2,1},{3,2},{4,3},{5,4},{6,5},{7,6},{8,7},{9,8},{10,9},{11,1... | collective-permute-start | bytes 5898248 | tf_op jit(solution)/shard_map/ppermute | solution.py:17
  13.2 127.3 %collective-permute-start.3 = (bf16[2,384,1280]{2,1,0:T(8,128)(2,1)S(1)}, bf16[2,384,1280]{2,1,0:T(8,128)(2,1)}, u32[]{:S(2)}, u32[]{:S(2)}) collective-permute-start(bf16[2,384,1280]{2,1,0:T(8,128)(2,1)S(1)} %pad_maximum_fusion.1), channel_id=1, source_target_pairs={{2,0},{3,1},{4,2},{5,3},{6,4},{7,5},{8,6},{9,7},{10,8},{11,9},{12,... | collective-permute-start | bytes 5898248 | tf_op jit(solution)/shard_map/ppermute | solution.py:17
  14.8 121.4 %copy-start.5 = (bf16[384,1280]{1,0:T(8,128)(2,1)S(1)}, bf16[384,1280]{1,0:T(8,128)(2,1)}, u32[]{:S(2)}) copy-start(bf16[384,1280]{1,0:T(8,128)(2,1)} %param.10) | copy-start | bytes 2949124
  14.8 121.4 %copy-start.6 = (bf16[384,1280]{1,0:T(8,128)(2,1)S(1)}, bf16[384,1280]{1,0:T(8,128)(2,1)}, u32[]{:S(2)}) copy-start(bf16[384,1280]{1,0:T(8,128)(2,1)} %param.9) | copy-start | bytes 2949124
  196.8 3.7 copy-start
  196.8 3.7 copy-start.1
  196.8 7.8 %slice-start.6 = ((s8[6291456]{0:T(1024)(128)(4,1)}), s8[4194304]{0:T(1024)(128)(4,1)S(1)}, s32[]{:S(2)}) async-start(s8[6291456]{0:T(1024)(128)(4,1)} %bitcast.140), calls=%async_computation.6 | async-start | bytes 8388608 | tf_op jit(solution)/shard_map/while
  200.6 4.1 slice-start.7
  253.9 3.9 copy-start.8
  253.9 3.9 copy-start.11
  277.6 3.7 copy-start
  277.6 3.7 copy-start.1
  277.6 7.8 %slice-start.6 = ((s8[6291456]{0:T(1024)(128)(4,1)}), s8[4194304]{0:T(1024)(128)(4,1)S(1)}, s32[]{:S(2)}) async-start(s8[6291456]{0:T(1024)(128)(4,1)} %bitcast.140), calls=%async_computation.6 | async-start | bytes 8388608 | tf_op jit(solution)/shard_map/while
  281.3 4.1 slice-start.7
  334.7 4.0 copy-start.8
  334.7 4.0 copy-start.11
  358.5 3.7 copy-start
  358.5 3.7 copy-start.1
  358.5 7.8 %slice-start.6 = ((s8[6291456]{0:T(1024)(128)(4,1)}), s8[4194304]{0:T(1024)(128)(4,1)S(1)}, s32[]{:S(2)}) async-start(s8[6291456]{0:T(1024)(128)(4,1)} %bitcast.140), calls=%async_computation.6 | async-start | bytes 8388608 | tf_op jit(solution)/shard_map/while
  362.2 4.1 slice-start.7
  415.5 3.9 copy-start.8
  415.5 3.9 copy-start.11
  439.2 3.7 copy-start
  439.2 3.7 copy-start.1
  439.2 7.8 %slice-start.6 = ((s8[6291456]{0:T(1024)(128)(4,1)}), s8[4194304]{0:T(1024)(128)(4,1)S(1)}, s32[]{:S(2)}) async-start(s8[6291456]{0:T(1024)(128)(4,1)} %bitcast.140), calls=%async_computation.6 | async-start | bytes 8388608 | tf_op jit(solution)/shard_map/while
  442.9 4.1 slice-start.7
  496.3 4.0 copy-start.8
  496.3 4.0 copy-start.11
  520.1 3.7 copy-start
  520.1 3.7 copy-start.1
  520.1 7.8 %slice-start.6 = ((s8[6291456]{0:T(1024)(128)(4,1)}), s8[4194304]{0:T(1024)(128)(4,1)S(1)}, s32[]{:S(2)}) async-start(s8[6291456]{0:T(1024)(128)(4,1)} %bitcast.140), calls=%async_computation.6 | async-start | bytes 8388608 | tf_op jit(solution)/shard_map/while
  523.8 4.1 slice-start.7
  577.1 3.9 copy-start.8
  577.1 3.9 copy-start.11
  581.1 140.3 %slice-start = ((s8[9830400]{0:T(1024)(128)(4,1)}), s8[4194304]{0:T(1024)(128)(4,1)S(1)}, s32[]{:S(2)}) async-start(s8[9830400]{0:T(1024)(128)(4,1)} %bitcast.133), calls=%async_computation | async-start | bytes 8388608
  581.1 140.3 %slice-start.1 = ((s8[9830400]{0:T(1024)(128)(4,1)}), s8[4194304]{0:T(1024)(128)(4,1)S(1)}, s32[]{:S(2)}) async-start(s8[9830400]{0:T(1024)(128)(4,1)} %bitcast.133), calls=%async_computation.1 | async-start | bytes 8388608
  581.1 140.3 %slice-start.3 = ((s8[9830400]{0:T(1024)(128)(4,1)}), s8[4194304]{0:T(1024)(128)(4,1)S(1)}, s32[]{:S(2)}) async-start(s8[9830400]{0:T(1024)(128)(4,1)} %bitcast.137), calls=%async_computation.3 | async-start | bytes 8388608
  581.1 140.3 %slice-start.4 = ((s8[9830400]{0:T(1024)(128)(4,1)}), s8[4194304]{0:T(1024)(128)(4,1)S(1)}, s32[]{:S(2)}) async-start(s8[9830400]{0:T(1024)(128)(4,1)} %bitcast.137), calls=%async_computation.4 | async-start | bytes 8388608
  590.6 130.7 %slice-start.2 = ((s8[9830400]{0:T(1024)(128)(4,1)}), s8[1441792]{0:T(1024)(128)(4,1)S(1)}, s32[]{:S(2)}) async-start(s8[9830400]{0:T(1024)(128)(4,1)} %bitcast.133), calls=%async_computation.2 | async-start | bytes 2883584
  590.7 130.7 %slice-start.5 = ((s8[9830400]{0:T(1024)(128)(4,1)}), s8[1441792]{0:T(1024)(128)(4,1)S(1)}, s32[]{:S(2)}) async-start(s8[9830400]{0:T(1024)(128)(4,1)} %bitcast.137), calls=%async_computation.5 | async-start | bytes 2883584
  591.2 44.3 %collective-permute-start.4 = (bf16[2,384,1280]{2,1,0:T(8,128)(2,1)S(1)}, bf16[2,384,1280]{2,1,0:T(8,128)(2,1)S(1)}, u32[]{:S(2)}, u32[]{:S(2)}) collective-permute-start(bf16[2,384,1280]{2,1,0:T(8,128)(2,1)S(1)} %get-tuple-element.274), channel_id=1, source_target_pairs={{2,0},{3,1},{4,2},{5,3},{6,4},{7,5},{8,6},{9,7},{10,8},{11,9},{12,... | collective-permute-start | bytes 5898248 | tf_op jit(solution)/shard_map/ppermute | solution.py:17
  592.8 107.4 %collective-permute-start.7 = (bf16[2,384,1280]{2,1,0:T(8,128)(2,1)S(1)}, bf16[2,384,1280]{2,1,0:T(8,128)(2,1)S(1)}, u32[]{:S(2)}, u32[]{:S(2)}) collective-permute-start(bf16[2,384,1280]{2,1,0:T(8,128)(2,1)S(1)} %get-tuple-element.275), channel_id=1, source_target_pairs={{0,2},{1,3},{2,4},{3,5},{4,6},{5,7},{6,8},{7,9},{8,10},{9,11},{10,... | collective-permute-start | bytes 5898248 | tf_op jit(solution)/shard_map/ppermute | solution.py:17
  596.9 124.4 %collective-permute-start.6 = (bf16[2,384,1280]{2,1,0:T(8,128)(2,1)S(1)}, bf16[2,384,1280]{2,1,0:T(8,128)(2,1)S(1)}, u32[]{:S(2)}, u32[]{:S(2)}) collective-permute-start(bf16[2,384,1280]{2,1,0:T(8,128)(2,1)S(1)} %get-tuple-element.276), channel_id=1, source_target_pairs={{0,1},{1,2},{2,3},{3,4},{4,5},{5,6},{6,7},{7,8},{8,9},{9,10},{10,1... | collective-permute-start | bytes 5898248 | tf_op jit(solution)/shard_map/ppermute | solution.py:17
  604.0 117.4 %collective-permute-start.5 = (bf16[2,384,1280]{2,1,0:T(8,128)(2,1)S(1)}, bf16[2,384,1280]{2,1,0:T(8,128)(2,1)S(1)}, u32[]{:S(2)}, u32[]{:S(2)}) collective-permute-start(bf16[2,384,1280]{2,1,0:T(8,128)(2,1)S(1)} %get-tuple-element.277), channel_id=1, source_target_pairs={{1,0},{2,1},{3,2},{4,3},{5,4},{6,5},{7,6},{8,7},{9,8},{10,9},{11,1... | collective-permute-start | bytes 5898248 | tf_op jit(solution)/shard_map/ppermute | solution.py:17
  (25 other events, 70.4 us)
where the time goes:
time: 730 us; the launch traced here: 724 us
  local copies, waits for them, and re-layouts  277 us (38%)
  waiting for transfers between devices  231 us (32%)
  other arithmetic  110 us (15%)
  matrix products  78 us (11%)
  starting transfers between devices  26.8 us (4%)
    ppermute x8, waiting for transfers between devices, shifted(): return lax.ppermute(block, axis, route)  231 us
    dynamic_slice x50, local copies, waits for them, and re-layouts, columns(): lax.dynamic_slice_in_dim(source, column, group_width, source.ndim - 1)  69.5 us
    reshape x10, local copies, waits for them, and re-layouts, head_group(): value_part = value_part.reshape(block_count * LIST, BLK, group_width)  67.3 us
    reshape x10, local copies, waits for them, and re-layouts, head_group(): key_part = key_part.reshape(block_count * LIST, BLK, group_width)  67.2 us
    scatter-add x5, other arithmetic, per_group(): key_cols = columns(grad_keys).at[listed_flat].add(key_part)  46.8 us
    scatter-add x5, other arithmetic, per_group(): value_cols = columns(grad_values).at[listed_flat].add(value_part)  30.4 us
    sub x5, matrix products, head_group(): raised = jnp.exp(scores - row_max)  28.6 us
    ppermute x8, starting transfers between devices, shifted(): return lax.ppermute(block, axis, route)  26.8 us
  transfers between devices with their start and end apart: 8, of which 5 were waited for; matrix products, arithmetic and copies ran while one was open for 1% of the time, Pallas kernels for 0%

commit v1 on v0

v1 whole, which is shorter than its diff:
```python
import functools
import math

import jax
import jax.numpy as jnp
from jax import lax
from jax.experimental import pallas as pl
from jax.experimental.pallas import tpu as pltpu
from jax.sharding import PartitionSpec as P

HEADS = 20
HEAD_DIM = 64
WIDE = 2 * HEAD_DIM
BLK = 128
LIST = 8
MIN_LIVE = 4
QUAD = 4
PIECES = 2 * QUAD
CHUNKS = (1, 2, 2)
LOG2E = math.log2(math.e)
VMEM_LIMIT = 48 * 1024 * 1024


def swapped(x):
    return jnp.concatenate([x[:, HEAD_DIM:], x[:, :HEAD_DIM]], axis=1)


def pack_body(place, query_ref, grad_ref, key_ref, value_ref, *outs):
    side, core = place[0] // 2, place[0] % 2
    rows = query_ref.shape[0]
    left = lax.broadcasted_iota(jnp.int32, (rows, WIDE), 1) < HEAD_DIM
    for (first_ref, second_ref), pieces in (
        ((query_ref, grad_ref), outs[:QUAD]),
        ((key_ref, value_ref), outs[QUAD:]),
    ):
        for other in range(2):
            column = pl.ds(pl.multiple_of((side ^ other) * WIDE, WIDE), WIDE)
            first, second = first_ref[:, column], second_ref[:, column]
            low = jnp.where(left, first, swapped(second))
            high = jnp.where(left, swapped(first), second)
            pieces[2 * other][0] = jnp.where(core == 0, low, high)
            pieces[2 * other + 1][0] = jnp.where(core == 0, high, low)


def pack(place, queries, out_grad, key_rows, value_rows, start, heads):
    rows = queries.shape[0]
    source = pl.BlockSpec((rows, 2 * WIDE), lambda h, _: (0, start + h))
    piece = pl.BlockSpec((1, rows, WIDE), lambda h, _: (h, 0, 0))
    shape = jax.ShapeDtypeStruct((heads, rows, WIDE), jnp.bfloat16)
    outs = pl.pallas_call(
        pack_body,
        grid_spec=pltpu.PrefetchScalarGridSpec(
            num_scalar_prefetch=1,
            grid=(heads,),
            in_specs=[source] * 4,
            out_specs=[piece] * (2 * QUAD),
        ),
        out_shape=[shape] * (2 * QUAD),
        compiler_params=pltpu.CompilerParams(vmem_limit_bytes=VMEM_LIMIT),
        cost_estimate=pl.CostEstimate(
            flops=0, bytes_accessed=heads * rows * WIDE * 32, transcendentals=0
        ),
        name="pack",
    )(place, queries, out_grad, key_rows, value_rows)
    return outs[:QUAD], outs[QUAD:]


def unpack_body(place, *refs):
    query_parts, key_parts, outs = refs[:QUAD], refs[QUAD : 2 * QUAD], refs[-4:]
    side, core = place[0] // 2, place[0] % 2
    rows = query_parts[0].shape[1]
    left = lax.broadcasted_iota(jnp.int32, (rows, WIDE), 1) < HEAD_DIM
    for parts, (first_out, second_out) in ((query_parts, outs[:2]), (key_parts, outs[2:])):
        for other in range(2):
            column = pl.ds(pl.multiple_of((side ^ other) * WIDE, WIDE), WIDE)
            even, odd = parts[2 * other][0], parts[2 * other + 1][0]
            low = jnp.where(core == 0, even, odd)
            high = jnp.where(core == 0, odd, even)
            first_out[:, column] = jnp.where(left, low, swapped(high))
            second_out[:, column] = jnp.where(left, swapped(low), high)


def unpack(place, query_parts, key_parts, so_far, start, full_width):
    heads, rows, _ = query_parts[0].shape
    piece = pl.BlockSpec((1, rows, WIDE), lambda h, _: (h, 0, 0))
    target = pl.BlockSpec((rows, 2 * WIDE), lambda h, _: (0, start + h))
    kept = [] if so_far is None else list(so_far)
    return pl.pallas_call(
        unpack_body,
        grid_spec=pltpu.PrefetchScalarGridSpec(
            num_scalar_prefetch=1,
            grid=(heads,),
            in_specs=[piece] * (2 * QUAD) + [pl.BlockSpec(memory_space=pl.ANY)] * len(kept),
            out_specs=[target] * 4,
        ),
        out_shape=[jax.ShapeDtypeStruct((rows, full_width), jnp.bfloat16)] * 4,
        input_output_aliases={1 + 2 * QUAD + n: n for n in range(len(kept))},
        compiler_params=pltpu.CompilerParams(vmem_limit_bytes=VMEM_LIMIT),
        cost_estimate=pl.CostEstimate(
            flops=0, bytes_accessed=heads * rows * WIDE * 32, transcendentals=0
        ),
        name="unpack",
    )(place, *query_parts, *key_parts, *kept)


def attend_body(lists, counts, *refs, blocks):
    query_parts, key_parts = refs[:QUAD], refs[QUAD : QUAD + PIECES]
    results = refs[QUAD + PIECES : 2 * QUAD + PIECES]
    own = refs[2 * QUAD + PIECES : 3 * QUAD + PIECES]
    near, far, window, window_t, total, pair = refs[3 * QUAD + PIECES :]
    score_scale = 1.0 / math.sqrt(HEAD_DIM)
    exponent_scale = LOG2E * score_scale
    for piece in range(PIECES):
        for block in range(blocks):
            rows = key_parts[piece][0, block * BLK : (block + 1) * BLK, :]
            window[piece * blocks + block] = rows
            window_t[piece * blocks + block] = rows.T
    total[...] = jnp.zeros_like(total)
    left = lax.broadcasted_iota(jnp.int32, (BLK, WIDE), 1) < HEAD_DIM

    for piece in range(QUAD):

        def query_block(block, carry, piece=piece):
            rows = pl.ds(pl.multiple_of(block * BLK, BLK), BLK)
            query_grad = query_parts[piece][0, rows, :]
            nothing = jnp.zeros_like(query_grad)
            operand = jnp.concatenate(
                [jnp.where(left, query_grad, nothing), jnp.where(left, nothing, query_grad)], 0
            )
            index = piece * blocks + block
            count = counts[index]
            listed = [lists[index * LIST + slot] for slot in range(LIST)]
            scores, weight_grads = [], []
            for slot in range(LIST):
                both = lax.dot_general(
                    window[listed[slot]],
                    operand,
                    (((1,), (1,)), ((), ())),
                    preferred_element_type=jnp.float32,
                )
                score = both[:, :BLK]
                if slot >= MIN_LIVE:
                    score = jnp.where(slot < count, score, -jnp.inf)
                scores.append(score)
                weight_grads.append(both[:, BLK:])
            top = jnp.max(functools.reduce(jnp.maximum, scores), axis=0, keepdims=True)
            raised = [jnp.exp2((score - top) * exponent_scale) for score in scores]
            row_sum = jnp.sum(functools.reduce(jnp.add, raised), axis=0, keepdims=True)
            products = [e * g for e, g in zip(raised, weight_grads)]
            row_dot = jnp.sum(functools.reduce(jnp.add, products), axis=0, keepdims=True)
            inverse = 1.0 / row_sum
            row_dot = row_dot * inverse
            for slot in range(LIST):
                span = slice(slot * BLK, (slot + 1) * BLK)
                pair[span, :BLK] = raised[slot].astype(jnp.bfloat16)
                pair[span, BLK:] = (raised[slot] * (weight_grads[slot] - row_dot)).astype(
                    jnp.bfloat16
                )
            listed_t = jnp.concatenate([window_t[listed[slot]] for slot in range(LIST)], axis=1)
            product = jnp.dot(listed_t, pair[...], preferred_element_type=jnp.float32)
            query_part = product[:HEAD_DIM, BLK:] * (inverse * score_scale)
            attended_part = product[HEAD_DIM:, :BLK] * inverse
            results[piece][0, rows, :] = (
                jnp.concatenate([query_part, attended_part], 0).T.astype(jnp.bfloat16)
            )
            scaled = query_grad.astype(jnp.float32) * jnp.broadcast_to(inverse, (BLK, BLK)).T
            blank = jnp.zeros_like(scaled)
            operand_back = jnp.concatenate(
                [jnp.where(left, blank, scaled), jnp.where(left, scaled * score_scale, blank)], 0
            ).astype(jnp.bfloat16)
            for slot in range(LIST):
                total[listed[slot]] += jnp.dot(
                    pair[slot * BLK : (slot + 1) * BLK, :],
                    operand_back,
                    preferred_element_type=jnp.float32,
                )
            return carry

        lax.fori_loop(0, blocks, query_block, 0)

    for piece in range(PIECES):
        for block in range(blocks):
            span = slice(block * BLK, (block + 1) * BLK)
            part = total[piece * blocks + block]
            if piece < QUAD:
                own[piece][0, span, :] = part
            elif piece < QUAD + 2:
                near[piece - QUAD, 0, span, :] = part.astype(jnp.bfloat16)
            else:
                far[piece - QUAD - 2, 0, span, :] = part.astype(jnp.bfloat16)


def attend(lists, counts, query_parts, key_parts):
    heads, rows, _ = query_parts[0].shape
    blocks = rows // BLK
    piece = pl.BlockSpec((1, rows, WIDE), lambda h, *_: (h, 0, 0))
    couple = pl.BlockSpec((2, 1, rows, WIDE), lambda h, *_: (0, h, 0, 0))
    shape = (heads, rows, WIDE)
    outs = pl.pallas_call(
        functools.partial(attend_body, blocks=blocks),
        grid_spec=pltpu.PrefetchScalarGridSpec(
            num_scalar_prefetch=2,
            grid=(heads,),
            in_specs=[piece] * (QUAD + PIECES),
            out_specs=[piece] * (2 * QUAD) + [couple] * 2,
            scratch_shapes=[
                pltpu.VMEM((PIECES * blocks, BLK, WIDE), jnp.bfloat16),
                pltpu.VMEM((PIECES * blocks, WIDE, BLK), jnp.bfloat16),
                pltpu.VMEM((PIECES * blocks, BLK, WIDE), jnp.float32),
                pltpu.VMEM((LIST * BLK, 2 * BLK), jnp.bfloat16),
            ],
        ),
        out_shape=[jax.ShapeDtypeStruct(shape, jnp.bfloat16)] * QUAD
        + [jax.ShapeDtypeStruct(shape, jnp.float32)] * QUAD
        + [jax.ShapeDtypeStruct((2,) + shape, jnp.bfloat16)] * 2,
        compiler_params=pltpu.CompilerParams(vmem_limit_bytes=VMEM_LIMIT),
        cost_estimate=pl.CostEstimate(
            flops=heads * QUAD * blocks * LIST * BLK * BLK * WIDE * 16,
            bytes_accessed=heads * rows * WIDE * 56,
            transcendentals=heads * QUAD * blocks * LIST * BLK * BLK,
        ),
        name="attend",
    )(lists, counts, *query_parts, *key_parts)
    return outs[:QUAD], outs[QUAD : 2 * QUAD], outs[2 * QUAD], outs[2 * QUAD + 1]


def combine_body(*refs):
    own, near, far, outs = refs[:QUAD], refs[QUAD], refs[QUAD + 1], refs[QUAD + 2 :]
    for piece in range(QUAD):
        other = near if piece < 2 else far
        outs[piece][0] = (own[piece][0] + other[piece % 2, 0].astype(jnp.float32)).astype(
            jnp.bfloat16
        )


def combine(own, near, far):
    heads, rows, _ = own[0].shape
    piece = pl.BlockSpec((1, rows, WIDE), lambda h: (h, 0, 0))
    couple = pl.BlockSpec((2, 1, rows, WIDE), lambda h: (0, h, 0, 0))
    return pl.pallas_call(
        combine_body,
        grid=(heads,),
        in_specs=[piece] * QUAD + [couple] * 2,
        out_specs=[piece] * QUAD,
        out_shape=[jax.ShapeDtypeStruct(own[0].shape, jnp.bfloat16)] * QUAD,
        compiler_params=pltpu.CompilerParams(vmem_limit_bytes=VMEM_LIMIT),
        cost_estimate=pl.CostEstimate(
            flops=0, bytes_accessed=heads * rows * WIDE * 32, transcendentals=0
        ),
        name="combine",
    )(*own, near, far)


def local(queries, key_rows, value_rows, out_grad, block_lists, list_counts):
    rows, width = queries.shape
    blocks = rows // BLK
    shards = lax.axis_size("tm")
    shard = lax.axis_index("tm")
    quad, place = shard // QUAD, shard % QUAD

    def across(x, flip):
        return lax.ppermute(x, "tm", [(i, i ^ flip) for i in range(shards)])

    def along(x, sign, flip=0):
        route = []
        for i in range(shards):
            j = i + (-QUAD if i % QUAD < 2 else QUAD) * sign
            if 0 <= j < shards:
                route.append((i, j ^ flip))
        return lax.ppermute(x, "tm", route)

    place_array = place.astype(jnp.int32).reshape(1)
    plan = jnp.concatenate([block_lists.reshape(-1), list_counts]).astype(jnp.int32)
    plans = jnp.stack([plan] + [across(plan, flip) for flip in range(1, QUAD)])
    listed = plans[:, : blocks * LIST].reshape(-1)
    counts = plans[:, blocks * LIST :].reshape(-1)
    owner = listed // blocks
    slots = ((owner % QUAD) ^ place) + jnp.where(owner // QUAD == quad, 0, QUAD)
    slots = slots * blocks + listed % blocks

    starts = [sum(CHUNKS[:n]) for n in range(len(CHUNKS))]
    packed = [
        pack(place_array, queries, out_grad, key_rows, value_rows, start, heads)
        for start, heads in zip(starts, CHUNKS)
    ]
    outs = None
    for start, (query_sent, key_sent) in zip(starts, packed):
        key_own = [key_sent[0]] + [across(key_sent[flip], flip) for flip in (1, 2, 3)]
        query_own = [query_sent[0]] + [across(query_sent[flip], flip) for flip in (1, 2, 3)]
        key_halo = [
            along(key_sent[0], 1),
            along(key_sent[1], 1, 1),
            along(key_own[2], -1),
            along(key_own[3], -1),
        ]
        results, own, near, far = attend(slots, counts, query_own, key_own + key_halo)
        near = along(near, -1)
        far = along(far, 1)
        sums = combine(own, near, far)
        query_back = [results[0]] + [across(results[flip], flip) for flip in (1, 2, 3)]
        key_back = [sums[0]] + [across(sums[flip], flip) for flip in (1, 2, 3)]
        outs = unpack(place_array, query_back, key_back, outs, start, width)
    query_grad, attended, key_grad, value_grad = outs
    return attended, query_grad, key_grad, value_grad


def solution(mesh):
    rows = P(("groups", "tm"), None)
    return jax.shard_map(
        local,
        mesh=mesh,
        in_specs=(rows, rows, rows, rows, rows, P(("groups", "tm"))),
        out_specs=(rows, rows, rows, rows),
        check_vma=False,
    )
```

time: 730 us -> 218 us (0.30)
  local copies, waits for them, and re-layouts: 277 us -> 22.2 us
  waiting for transfers between devices: 231 us -> 38.7 us
  other arithmetic: 110 us -> 0.12 us
  matrix products: 78 us -> 0 us
  Pallas kernels: 0 us -> 68.7 us
  starting transfers between devices: 26.8 us -> 85.9 us
    ppermute x8 -> x57, waiting for transfers between devices: 231 us -> 38.7 us  [the longest x39 33.2 us: across(): return lax.ppermute(x, 'tm', [(i, i ^ flip) for i in range(shards)])]
    reshape x22 -> x2, local copies, waits for them, and re-layouts: 135 us -> 0.85 us  [the longest x1 0.77 us: local(): block_lists.reshape(-1)]
    scatter-add x10 -> x0, other arithmetic: 77.3 us -> none  [the longest x5 46.8 us: per_group(): key_cols = columns(grad_keys).at[listed_flat].add(key_part)]
    dynamic_slice x50 -> x0, local copies, waits for them, and re-layouts: 69.5 us -> none  [columns(): lax.dynamic_slice_in_dim(source, column, group_width, source.ndim - 1)]
    pallas_call x0 -> x12, Pallas kernels: none -> 68.7 us  [the longest x3 61.5 us: attend(): pl.pallas_call(functools.partial(attend_body, blocks=blocks), grid_spec=p...]
    ppermute x8 -> x57, starting transfers between devices: 26.8 us -> 85.9 us  [the longest x39 43 us: across(): return lax.ppermute(x, 'tm', [(i, i ^ flip) for i in range(shards)])]
    dot_general x25 -> x0, matrix products: 49.3 us -> none  [the longest x5 11.6 us: head_group(): jnp.einsum('bhqk,bqhe->bkhe', dscore, query_heads, preferred_element_type...]
    sub x5 -> x0, matrix products: 28.6 us -> none  [head_group(): raised = jnp.exp(scores - row_max)]
  transfers between devices with their start and end apart: 8 -> 57, of which waited for: 5 -> 12; matrix products, arithmetic and copies ran while one was open for 1% -> 0% of each run, Pallas kernels for 0% -> 31%
where the time goes in v1:
time: 218 us; the launch traced here: 217 us
  starting transfers between devices  85.9 us (39%)
  Pallas kernels  68.7 us (32%)
  waiting for transfers between devices  38.7 us (18%)
  local copies, waits for them, and re-layouts  22.2 us (10%)
    pallas_call x3, Pallas kernels, attend(): pl.pallas_call(functools.partial(attend_body, blocks=blocks), grid_spec=p...  61.5 us
    ppermute x39, starting transfers between devices, across(): return lax.ppermute(x, 'tm', [(i, i ^ flip) for i in range(shards)])  43 us
    ppermute x18, starting transfers between devices, along(): return lax.ppermute(x, 'tm', route)  42.9 us
    ppermute x39, waiting for transfers between devices, across(): return lax.ppermute(x, 'tm', [(i, i ^ flip) for i in range(shards)])  33.2 us
    unnamed x70, local copies, waits for them, and re-layouts  21.1 us
    ppermute x18, waiting for transfers between devices, along(): return lax.ppermute(x, 'tm', route)  5.44 us
  transfers between devices with their start and end apart: 57, of which 12 were waited for; matrix products, arithmetic and copies ran while one was open for 0% of the time, Pallas kernels for 31%

profile of v1, /device:TPU:1, one launch (start us, length us, event | category | flops | bytes accessed | tf_op | source)
XLA Modules:
  0.0 216.8 jit_solution(3779843820856462668)
XLA Ops:
  1.5 2.7 %collective-permute-start.1 = (s32[27]{0:T(128)S(1)}, s32[27]{0:T(128)S(1)}, u32[]{:S(2)}, u32[]{:S(2)}) collective-permute-start(s32[27]{0:T(128)S(1)} %pad_add_fusion.1), channel_id=1, source_target_pairs={{0,2},{1,3},{2,0},{3,1},{4,6},{5,7},{6,4},{7,5},{8,10},{9,11},{10,... | collective-permute-start | bytes 332 | tf_op jit(solution)/shard_map/ppermute | solution.py:262
  14.8 1.3 collective-permute-start.46
  27.8 4.2 %collective-permute-start.43 = (bf16[1,384,128]{2,1,0:T(8,128)(2,1)}, bf16[1,384,128]{2,1,0:T(8,128)(2,1)S(1)}, u32[]{:S(2)}, u32[]{:S(2)}) collective-permute-start(bf16[1,384,128]{2,1,0:T(8,128)(2,1)} %copy-done.33), channel_id=1, source_target_pairs={{0,2},{1,3},{2,0},{3,1},{4,6},{5,7},{6,4},{7,5},{8,10},{9,11},{10,... | collective-permute-start | bytes 294920 | tf_op jit(solution)/shard_map/ppermute | solution.py:262
  32.1 1.3 collective-permute-start.45
  33.4 1.8 collective-permute-done.43.refs_6_
  37.4 1.4 collective-permute-start.40
  41.6 3.1 %collective-permute-start.47 = (bf16[1,384,128]{2,1,0:T(8,128)(2,1)S(1)}, bf16[1,384,128]{2,1,0:T(8,128)(2,1)S(1)}, u32[]{:S(2)}, u32[]{:S(2)}) collective-permute-start(bf16[1,384,128]{2,1,0:T(8,128)(2,1)S(1)} %collective-permute-done.43.refs_6_), channel_id=1, source_target_pairs={{0,4},{1,5},{4,8},{5,9},{6,2},{7,3},{8,12},{9,13},{10,6},{11,7},{1... | collective-permute-start | bytes 294920 | tf_op jit(solution)/shard_map/ppermute | solution.py:270
  44.8 3.2 %collective-permute-start.48 = (bf16[1,384,128]{2,1,0:T(8,128)(2,1)S(1)}, bf16[1,384,128]{2,1,0:T(8,128)(2,1)S(1)}, u32[]{:S(2)}, u32[]{:S(2)}) collective-permute-start(bf16[1,384,128]{2,1,0:T(8,128)(2,1)S(1)} %collective-permute-done.44.refs_7_), channel_id=1, source_target_pairs={{0,4},{1,5},{4,8},{5,9},{6,2},{7,3},{8,12},{9,13},{10,6},{11,7},{1... | collective-permute-start | bytes 294920 | tf_op jit(solution)/shard_map/ppermute | solution.py:270
  48.4 1.3 collective-permute-start.28
  49.7 1.3 collective-permute-start.27
  51.0 2.5 %collective-permute-start.21 = (bf16[2,384,128]{2,1,0:T(8,128)(2,1)}, bf16[2,384,128]{2,1,0:T(8,128)(2,1)S(1)}, u32[]{:S(2)}, u32[]{:S(2)}) collective-permute-start(bf16[2,384,128]{2,1,0:T(8,128)(2,1)} %copy-done.21), channel_id=1, source_target_pairs={{0,1},{1,0},{2,3},{3,2},{4,5},{5,4},{6,7},{7,6},{8,9},{9,8},{10,11... | collective-permute-start | bytes 589832 | tf_op jit(solution)/shard_map/ppermute | solution.py:262
  53.6 3.7 %collective-permute-start.22 = (bf16[2,384,128]{2,1,0:T(8,128)(2,1)}, bf16[2,384,128]{2,1,0:T(8,128)(2,1)S(1)}, u32[]{:S(2)}, u32[]{:S(2)}) collective-permute-start(bf16[2,384,128]{2,1,0:T(8,128)(2,1)} %copy-done.20), channel_id=1, source_target_pairs={{0,2},{1,3},{2,0},{3,1},{4,6},{5,7},{6,4},{7,5},{8,10},{9,11},{10,... | collective-permute-start | bytes 589832 | tf_op jit(solution)/shard_map/ppermute | solution.py:262
  57.7 5.4 %collective-permute-done.27.refs_8_ = bf16[2,384,128]{2,1,0:T(8,128)(2,1)S(1)} collective-permute-done((bf16[2,384,128]{2,1,0:T(8,128)(2,1)}, bf16[2,384,128]{2,1,0:T(8,128)(2,1)S(1)}, u32[]{:S(2)}, u32[]{:S(2)}) %collective-permute-start.27) | collective-permute-done | bytes 196640 | tf_op jit(solution)/shard_map/ppermute | solution.py:270
  63.1 1.3 collective-permute-start.10
  64.5 2.1 collective-permute-start.7
  67.0 1.3 collective-permute-start.9
  70.1 13.2 %attend.5 = (bf16[1,384,128]{2,1,0:T(8,128)(2,1)S(1)}, bf16[1,384,128]{2,1,0:T(8,128)(2,1)S(1)}, bf16[1,384,128]{2,1,0:T(8,128)(2,1)S(1)}, bf16[1,384,128]{2,1,0...) custom-call(s32[96]{0:T(128)S(1)} %fusion.lists, ...), custom_call_target="tpu_custom_call" | custom-call | flops 3221225472 | bytes 2752512 | tf_op jit(solution)/shard_map/attend/pallas_call | solution.py:199
  83.7 4.3 %collective-permute-start.52 = (bf16[2,1,384,128]{3,2,1,0:T(8,128)(2,1)S(1)}, bf16[2,1,384,128]{3,2,1,0:T(8,128)(2,1)S(1)}, u32[]{:S(2)}, u32[]{:S(2)}) collective-permute-start(bf16[2,1,384,128]{3,2,1,0:T(8,128)(2,1)S(1)} %get-tuple-element.142), channel_id=1, source_target_pairs={{0,4},{1,5},{4,8},{5,9},{6,2},{7,3},{8,12},{9,13},{10,6},{11,7},{1... | collective-permute-start | bytes 589832 | tf_op jit(solution)/shard_map/ppermute | solution.py:270
  88.0 1.3 collective-permute-start.53
  89.3 4.1 %collective-permute-start.29 = (bf16[2,384,128]{2,1,0:T(8,128)(2,1)S(1)}, bf16[2,384,128]{2,1,0:T(8,128)(2,1)S(1)}, u32[]{:S(2)}, u32[]{:S(2)}) collective-permute-start(bf16[2,384,128]{2,1,0:T(8,128)(2,1)S(1)} %collective-permute-done.25.refs_6_), channel_id=1, source_target_pairs={{0,4},{1,5},{4,8},{5,9},{6,2},{7,3},{8,12},{9,13},{10,6},{11,7},{1... | collective-permute-start | bytes 589832 | tf_op jit(solution)/shard_map/ppermute | solution.py:270
  93.4 3.4 %collective-permute-start.30 = (bf16[2,384,128]{2,1,0:T(8,128)(2,1)S(1)}, bf16[2,384,128]{2,1,0:T(8,128)(2,1)S(1)}, u32[]{:S(2)}, u32[]{:S(2)}) collective-permute-start(bf16[2,384,128]{2,1,0:T(8,128)(2,1)S(1)} %collective-permute-done.26.refs_7_), channel_id=1, source_target_pairs={{0,4},{1,5},{4,8},{5,9},{6,2},{7,3},{8,12},{9,13},{10,6},{11,7},{1... | collective-permute-start | bytes 589832 | tf_op jit(solution)/shard_map/ppermute | solution.py:270
  96.9 2.8 %collective-permute-start.5 = (bf16[2,384,128]{2,1,0:T(8,128)(2,1)S(1)}, bf16[2,384,128]{2,1,0:T(8,128)(2,1)S(1)}, u32[]{:S(2)}, u32[]{:S(2)}) collective-permute-start(bf16[2,384,128]{2,1,0:T(8,128)(2,1)S(1)} %get-tuple-element.85), channel_id=1, source_target_pairs={{0,3},{1,2},{2,1},{3,0},{4,7},{5,6},{6,5},{7,4},{8,11},{9,10},{10,... | collective-permute-start | bytes 589832 | tf_op jit(solution)/shard_map/ppermute | solution.py:262
  99.7 3.2 %collective-permute-start.11 = (bf16[2,384,128]{2,1,0:T(8,128)(2,1)S(1)}, bf16[2,384,128]{2,1,0:T(8,128)(2,1)S(1)}, u32[]{:S(2)}, u32[]{:S(2)}) collective-permute-start(bf16[2,384,128]{2,1,0:T(8,128)(2,1)S(1)} %collective-permute-done.7.refs_6_), channel_id=1, source_target_pairs={{0,4},{1,5},{4,8},{5,9},{6,2},{7,3},{8,12},{9,13},{10,6},{11,7},{1... | collective-permute-start | bytes 589832 | tf_op jit(solution)/shard_map/ppermute | solution.py:270
  102.9 2.9 %collective-permute-start.12 = (bf16[2,384,128]{2,1,0:T(8,128)(2,1)S(1)}, bf16[2,384,128]{2,1,0:T(8,128)(2,1)S(1)}, u32[]{:S(2)}, u32[]{:S(2)}) collective-permute-start(bf16[2,384,128]{2,1,0:T(8,128)(2,1)S(1)} %collective-permute-done.8.refs_7_), channel_id=1, source_target_pairs={{0,4},{1,5},{4,8},{5,9},{6,2},{7,3},{8,12},{9,13},{10,6},{11,7},{1... | collective-permute-start | bytes 589832 | tf_op jit(solution)/shard_map/ppermute | solution.py:270
  105.9 24.1 %attend.4 = (bf16[2,384,128]{2,1,0:T(8,128)(2,1)S(1)}, bf16[2,384,128]{2,1,0:T(8,128)(2,1)S(1)}, bf16[2,384,128]{2,1,0:T(8,128)(2,1)S(1)}, bf16[2,384,128]{2,1,0...) custom-call(s32[96]{0:T(128)S(1)} %fusion.lists, ...), custom_call_target="tpu_custom_call" | custom-call | flops 6442450944 | bytes 5505024 | tf_op jit(solution)/shard_map/attend/pallas_call | solution.py:199
  130.2 3.6 %collective-permute-start.51 = (bf16[1,384,128]{2,1,0:T(8,128)(2,1)S(1)}, bf16[1,384,128]{2,1,0:T(8,128)(2,1)S(1)}, u32[]{:S(2)}, u32[]{:S(2)}) collective-permute-start(bf16[1,384,128]{2,1,0:T(8,128)(2,1)S(1)} %get-tuple-element.137), channel_id=1, source_target_pairs={{0,3},{1,2},{2,1},{3,0},{4,7},{5,6},{6,5},{7,4},{8,11},{9,10},{10,... | collective-permute-start | bytes 294920 | tf_op jit(solution)/shard_map/ppermute | solution.py:262
  133.8 3.2 %collective-permute-start.34 = (bf16[2,2,384,128]{3,2,1,0:T(8,128)(2,1)S(1)}, bf16[2,2,384,128]{3,2,1,0:T(8,128)(2,1)S(1)}, u32[]{:S(2)}, u32[]{:S(2)}) collective-permute-start(bf16[2,2,384,128]{3,2,1,0:T(8,128)(2,1)S(1)} %get-tuple-element.120), channel_id=1, source_target_pairs={{0,4},{1,5},{4,8},{5,9},{6,2},{7,3},{8,12},{9,13},{10,6},{11,7},{1... | collective-permute-start | bytes 1179656 | tf_op jit(solution)/shard_map/ppermute | solution.py:270
  137.1 1.3 collective-permute-start.35
  138.4 24.1 %attend.3 = (bf16[2,384,128]{2,1,0:T(8,128)(2,1)S(1)}, bf16[2,384,128]{2,1,0:T(8,128)(2,1)S(1)}, bf16[2,384,128]{2,1,0:T(8,128)(2,1)S(1)}, bf16[2,384,128]{2,1,0...) custom-call(s32[96]{0:T(128)S(1)} %fusion.lists, ...), custom_call_target="tpu_custom_call" | custom-call | flops 6442450944 | bytes 5505024 | tf_op jit(solution)/shard_map/attend/pallas_call | solution.py:199
  162.5 4.0 %collective-permute-start.16 = (bf16[2,2,384,128]{3,2,1,0:T(8,128)(2,1)S(1)}, bf16[2,2,384,128]{3,2,1,0:T(8,128)(2,1)S(1)}, u32[]{:S(2)}, u32[]{:S(2)}) collective-permute-start(bf16[2,2,384,128]{3,2,1,0:T(8,128)(2,1)S(1)} %get-tuple-element.98), channel_id=1, source_target_pairs={{0,4},{1,5},{4,8},{5,9},{6,2},{7,3},{8,12},{9,13},{10,6},{11,7},{1... | collective-permute-start | bytes 1179656 | tf_op jit(solution)/shard_map/ppermute | solution.py:270
  166.5 1.3 collective-permute-start.17
  167.8 2.0 collective-permute-start.55
  169.8 2.0 collective-permute-done.55.refs_6_
  171.8 2.2 %collective-permute-start.31 = (bf16[2,384,128]{2,1,0:T(8,128)(2,1)S(1)}, bf16[2,384,128]{2,1,0:T(8,128)(2,1)S(1)}, u32[]{:S(2)}, u32[]{:S(2)}) collective-permute-start(bf16[2,384,128]{2,1,0:T(8,128)(2,1)S(1)} %get-tuple-element.113), channel_id=1, source_target_pairs={{0,1},{1,0},{2,3},{3,2},{4,5},{5,4},{6,7},{7,6},{8,9},{9,8},{10,11... | collective-permute-start | bytes 589832 | tf_op jit(solution)/shard_map/ppermute | solution.py:262
  174.0 1.8 collective-permute-start.32
  176.1 7.1 %collective-permute-done.56.refs_7_ = bf16[1,384,128]{2,1,0:T(8,128)(2,1)S(1)} collective-permute-done((bf16[1,384,128]{2,1,0:T(8,128)(2,1)S(1)}, bf16[1,384,128]{2,1,0:T(8,128)(2,1)S(1)}, u32[]{:S(2)}, u32[]{:S(2)}) %collective-permute-start.56) | collective-permute-done | bytes 98336 | tf_op jit(solution)/shard_map/ppermute | solution.py:262
  183.1 1.6 collective-permute-start.33
  185.5 1.6 collective-permute-start.38
  187.4 3.0 %collective-permute-done.33.refs_3_ = bf16[2,384,128]{2,1,0:T(8,128)(2,1)S(1)} collective-permute-done((bf16[2,384,128]{2,1,0:T(8,128)(2,1)S(1)}, bf16[2,384,128]{2,1,0:T(8,128)(2,1)S(1)}, u32[]{:S(2)}, u32[]{:S(2)}) %collective-permute-start.33) | collective-permute-done | bytes 196640 | tf_op jit(solution)/shard_map/ppermute | solution.py:262
  192.2 2.0 collective-permute-done.37.refs_6_
  194.3 1.3 collective-permute-start.19
  195.6 3.2 %collective-permute-done.38.refs_7_ = bf16[2,384,128]{2,1,0:T(8,128)(2,1)S(1)} collective-permute-done((bf16[2,384,128]{2,1,0:T(8,128)(2,1)S(1)}, bf16[2,384,128]{2,1,0:T(8,128)(2,1)S(1)}, u32[]{:S(2)}, u32[]{:S(2)}) %collective-permute-start.38) | collective-permute-done | bytes 196640 | tf_op jit(solution)/shard_map/ppermute | solution.py:262
  198.8 1.3 collective-permute-start.20
  201.2 1.4 unpack.4
  202.7 4.5 %collective-permute-done.15.refs_3_ = bf16[2,384,128]{2,1,0:T(8,128)(2,1)S(1)} collective-permute-done((bf16[2,384,128]{2,1,0:T(8,128)(2,1)S(1)}, bf16[2,384,128]{2,1,0:T(8,128)(2,1)S(1)}, u32[]{:S(2)}, u32[]{:S(2)}) %collective-permute-start.15) | collective-permute-done | bytes 196640 | tf_op jit(solution)/shard_map/ppermute | solution.py:262
  207.2 3.9 %collective-permute-done.19.refs_6_ = bf16[2,384,128]{2,1,0:T(8,128)(2,1)S(1)} collective-permute-done((bf16[2,384,128]{2,1,0:T(8,128)(2,1)S(1)}, bf16[2,384,128]{2,1,0:T(8,128)(2,1)S(1)}, u32[]{:S(2)}, u32[]{:S(2)}) %collective-permute-start.19) | collective-permute-done | bytes 196640 | tf_op jit(solution)/shard_map/ppermute | solution.py:262
  211.1 4.2 %collective-permute-done.20.refs_7_ = bf16[2,384,128]{2,1,0:T(8,128)(2,1)S(1)} collective-permute-done((bf16[2,384,128]{2,1,0:T(8,128)(2,1)S(1)}, bf16[2,384,128]{2,1,0:T(8,128)(2,1)S(1)}, u32[]{:S(2)}, u32[]{:S(2)}) %collective-permute-start.20) | collective-permute-done | bytes 196640 | tf_op jit(solution)/shard_map/ppermute | solution.py:262
  215.3 1.4 unpack.5
  (159 shorter events, 36.4 us)
Async XLA Ops:
  1.5 26.3 %collective-permute-start = (s32[27]{0:T(128)S(1)}, s32[27]{0:T(128)S(1)}, u32[]{:S(2)}, u32[]{:S(2)}) collective-permute-start(s32[27]{0:T(128)S(1)} %pad_add_fusion.1), channel_id=1, source_target_pairs={{0,1},{1,0},{2,3},{3,2},{4,5},{5,4},{6,7},{7,6},{8,9},{9,8},{10,11... | collective-permute-start | bytes 332 | tf_op jit(solution)/shard_map/ppermute | solution.py:262
  1.5 30.5 %collective-permute-start.1 = (s32[27]{0:T(128)S(1)}, s32[27]{0:T(128)S(1)}, u32[]{:S(2)}, u32[]{:S(2)}) collective-permute-start(s32[27]{0:T(128)S(1)} %pad_add_fusion.1), channel_id=1, source_target_pairs={{0,2},{1,3},{2,0},{3,1},{4,6},{5,7},{6,4},{7,5},{8,10},{9,11},{10,... | collective-permute-start | bytes 332 | tf_op jit(solution)/shard_map/ppermute | solution.py:262
  4.2 27.9 %collective-permute-start.2 = (s32[27]{0:T(128)S(1)}, s32[27]{0:T(128)S(1)}, u32[]{:S(2)}, u32[]{:S(2)}) collective-permute-start(s32[27]{0:T(128)S(1)} %pad_add_fusion.1), channel_id=1, source_target_pairs={{0,3},{1,2},{2,1},{3,0},{4,7},{5,6},{6,5},{7,4},{8,11},{9,10},{10,... | collective-permute-start | bytes 332 | tf_op jit(solution)/shard_map/ppermute | solution.py:262
  14.5 24.4 %collective-permute-start.42 = (bf16[1,384,128]{2,1,0:T(8,128)(2,1)}, bf16[1,384,128]{2,1,0:T(8,128)(2,1)}, u32[]{:S(2)}, u32[]{:S(2)}) collective-permute-start(bf16[1,384,128]{2,1,0:T(8,128)(2,1)} %get-tuple-element.131), channel_id=1, source_target_pairs={{0,1},{1,0},{2,3},{3,2},{4,5},{5,4},{6,7},{7,6},{8,9},{9,8},{10,11... | collective-permute-start | bytes 294920 | tf_op jit(solution)/shard_map/ppermute | solution.py:262
  14.8 25.9 %collective-permute-start.46 = (bf16[1,384,128]{2,1,0:T(8,128)(2,1)}, bf16[1,384,128]{2,1,0:T(8,128)(2,1)}, u32[]{:S(2)}, u32[]{:S(2)}) collective-permute-start(bf16[1,384,128]{2,1,0:T(8,128)(2,1)} %get-tuple-element.131), channel_id=1, source_target_pairs={{2,7},{3,6},{4,1},{5,0},{6,11},{7,10},{8,5},{9,4},{10,15},{11,14},... | collective-permute-start | bytes 294920 | tf_op jit(solution)/shard_map/ppermute | solution.py:270
  27.8 7.4 %collective-permute-start.43 = (bf16[1,384,128]{2,1,0:T(8,128)(2,1)}, bf16[1,384,128]{2,1,0:T(8,128)(2,1)S(1)}, u32[]{:S(2)}, u32[]{:S(2)}) collective-permute-start(bf16[1,384,128]{2,1,0:T(8,128)(2,1)} %copy-done.33), channel_id=1, source_target_pairs={{0,2},{1,3},{2,0},{3,1},{4,6},{5,7},{6,4},{7,5},{8,10},{9,11},{10,... | collective-permute-start | bytes 294920 | tf_op jit(solution)/shard_map/ppermute | solution.py:262
  32.1 7.3 %collective-permute-start.45 = (bf16[1,384,128]{2,1,0:T(8,128)(2,1)}, bf16[1,384,128]{2,1,0:T(8,128)(2,1)S(1)}, u32[]{:S(2)}, u32[]{:S(2)}) collective-permute-start(bf16[1,384,128]{2,1,0:T(8,128)(2,1)} %copy-done.27), channel_id=1, source_target_pairs={{2,6},{3,7},{4,0},{5,1},{6,10},{7,11},{8,4},{9,5},{10,14},{11,15},... | collective-permute-start | bytes 294920 | tf_op jit(solution)/shard_map/ppermute | solution.py:270
  39.5 11.5 %collective-permute-start.25 = (bf16[2,384,128]{2,1,0:T(8,128)(2,1)}, bf16[2,384,128]{2,1,0:T(8,128)(2,1)S(1)}, u32[]{:S(2)}, u32[]{:S(2)}) collective-permute-start(bf16[2,384,128]{2,1,0:T(8,128)(2,1)} %copy-done.24), channel_id=1, source_target_pairs={{0,2},{1,3},{2,0},{3,1},{4,6},{5,7},{6,4},{7,5},{8,10},{9,11},{10,... | collective-permute-start | bytes 589832 | tf_op jit(solution)/shard_map/ppermute | solution.py:262
  40.7 12.8 %collective-permute-start.26 = (bf16[2,384,128]{2,1,0:T(8,128)(2,1)}, bf16[2,384,128]{2,1,0:T(8,128)(2,1)S(1)}, u32[]{:S(2)}, u32[]{:S(2)}) collective-permute-start(bf16[2,384,128]{2,1,0:T(8,128)(2,1)} %copy-done.23), channel_id=1, source_target_pairs={{0,3},{1,2},{2,1},{3,0},{4,7},{5,6},{6,5},{7,4},{8,11},{9,10},{10,... | collective-permute-start | bytes 589832 | tf_op jit(solution)/shard_map/ppermute | solution.py:262
  41.1 16.2 %collective-permute-start.24 = (bf16[2,384,128]{2,1,0:T(8,128)(2,1)}, bf16[2,384,128]{2,1,0:T(8,128)(2,1)S(1)}, u32[]{:S(2)}, u32[]{:S(2)}) collective-permute-start(bf16[2,384,128]{2,1,0:T(8,128)(2,1)} %copy-done.22), channel_id=1, source_target_pairs={{0,1},{1,0},{2,3},{3,2},{4,5},{5,4},{6,7},{7,6},{8,9},{9,8},{10,11... | collective-permute-start | bytes 589832 | tf_op jit(solution)/shard_map/ppermute | solution.py:262
  48.4 16.0 %collective-permute-start.28 = (bf16[2,384,128]{2,1,0:T(8,128)(2,1)}, bf16[2,384,128]{2,1,0:T(8,128)(2,1)S(1)}, u32[]{:S(2)}, u32[]{:S(2)}) collective-permute-start(bf16[2,384,128]{2,1,0:T(8,128)(2,1)} %copy-done.22), channel_id=1, source_target_pairs={{2,7},{3,6},{4,1},{5,0},{6,11},{7,10},{8,5},{9,4},{10,15},{11,14},... | collective-permute-start | bytes 589832 | tf_op jit(solution)/shard_map/ppermute | solution.py:270
  49.7 13.4 %collective-permute-start.27 = (bf16[2,384,128]{2,1,0:T(8,128)(2,1)}, bf16[2,384,128]{2,1,0:T(8,128)(2,1)S(1)}, u32[]{:S(2)}, u32[]{:S(2)}) collective-permute-start(bf16[2,384,128]{2,1,0:T(8,128)(2,1)} %copy-done.12), channel_id=1, source_target_pairs={{2,6},{3,7},{4,0},{5,1},{6,10},{7,11},{8,4},{9,5},{10,14},{11,15},... | collective-permute-start | bytes 589832 | tf_op jit(solution)/shard_map/ppermute | solution.py:270
  51.0 13.5 %collective-permute-start.21 = (bf16[2,384,128]{2,1,0:T(8,128)(2,1)}, bf16[2,384,128]{2,1,0:T(8,128)(2,1)S(1)}, u32[]{:S(2)}, u32[]{:S(2)}) collective-permute-start(bf16[2,384,128]{2,1,0:T(8,128)(2,1)} %copy-done.21), channel_id=1, source_target_pairs={{0,1},{1,0},{2,3},{3,2},{4,5},{5,4},{6,7},{7,6},{8,9},{9,8},{10,11... | collective-permute-start | bytes 589832 | tf_op jit(solution)/shard_map/ppermute | solution.py:262
  53.6 13.0 %collective-permute-start.22 = (bf16[2,384,128]{2,1,0:T(8,128)(2,1)}, bf16[2,384,128]{2,1,0:T(8,128)(2,1)S(1)}, u32[]{:S(2)}, u32[]{:S(2)}) collective-permute-start(bf16[2,384,128]{2,1,0:T(8,128)(2,1)} %copy-done.20), channel_id=1, source_target_pairs={{0,2},{1,3},{2,0},{3,1},{4,6},{5,7},{6,4},{7,5},{8,10},{9,11},{10,... | collective-permute-start | bytes 589832 | tf_op jit(solution)/shard_map/ppermute | solution.py:262
  57.3 9.7 %collective-permute-start.23 = (bf16[2,384,128]{2,1,0:T(8,128)(2,1)}, bf16[2,384,128]{2,1,0:T(8,128)(2,1)S(1)}, u32[]{:S(2)}, u32[]{:S(2)}) collective-permute-start(bf16[2,384,128]{2,1,0:T(8,128)(2,1)} %copy-done.19), channel_id=1, source_target_pairs={{0,3},{1,2},{2,1},{3,0},{4,7},{5,6},{6,5},{7,4},{8,11},{9,10},{10,... | collective-permute-start | bytes 589832 | tf_op jit(solution)/shard_map/ppermute | solution.py:262
  63.1 24.9 %collective-permute-start.10 = (bf16[2,384,128]{2,1,0:T(8,128)(2,1)}, bf16[2,384,128]{2,1,0:T(8,128)(2,1)S(1)}, u32[]{:S(2)}, u32[]{:S(2)}) collective-permute-start(bf16[2,384,128]{2,1,0:T(8,128)(2,1)} %copy-done.16), channel_id=1, source_target_pairs={{2,7},{3,6},{4,1},{5,0},{6,11},{7,10},{8,5},{9,4},{10,15},{11,14},... | collective-permute-start | bytes 589832 | tf_op jit(solution)/shard_map/ppermute | solution.py:270
  64.4 24.9 %collective-permute-start.6 = (bf16[2,384,128]{2,1,0:T(8,128)(2,1)}, bf16[2,384,128]{2,1,0:T(8,128)(2,1)S(1)}, u32[]{:S(2)}, u32[]{:S(2)}) collective-permute-start(bf16[2,384,128]{2,1,0:T(8,128)(2,1)} %copy-done.16), channel_id=1, source_target_pairs={{0,1},{1,0},{2,3},{3,2},{4,5},{5,4},{6,7},{7,6},{8,9},{9,8},{10,11... | collective-permute-start | bytes 589832 | tf_op jit(solution)/shard_map/ppermute | solution.py:262
  64.5 18.8 %collective-permute-start.7 = (bf16[2,384,128]{2,1,0:T(8,128)(2,1)}, bf16[2,384,128]{2,1,0:T(8,128)(2,1)S(1)}, u32[]{:S(2)}, u32[]{:S(2)}) collective-permute-start(bf16[2,384,128]{2,1,0:T(8,128)(2,1)} %copy-done.18), channel_id=1, source_target_pairs={{0,2},{1,3},{2,0},{3,1},{4,6},{5,7},{6,4},{7,5},{8,10},{9,11},{10,... | collective-permute-start | bytes 589832 | tf_op jit(solution)/shard_map/ppermute | solution.py:262
  66.6 17.1 %collective-permute-start.8 = (bf16[2,384,128]{2,1,0:T(8,128)(2,1)}, bf16[2,384,128]{2,1,0:T(8,128)(2,1)S(1)}, u32[]{:S(2)}, u32[]{:S(2)}) collective-permute-start(bf16[2,384,128]{2,1,0:T(8,128)(2,1)} %copy-done.17), channel_id=1, source_target_pairs={{0,3},{1,2},{2,1},{3,0},{4,7},{5,6},{6,5},{7,4},{8,11},{9,10},{10,... | collective-permute-start | bytes 589832 | tf_op jit(solution)/shard_map/ppermute | solution.py:262
  67.0 26.4 %collective-permute-start.9 = (bf16[2,384,128]{2,1,0:T(8,128)(2,1)S(1)}, bf16[2,384,128]{2,1,0:T(8,128)(2,1)S(1)}, u32[]{:S(2)}, u32[]{:S(2)}) collective-permute-start(bf16[2,384,128]{2,1,0:T(8,128)(2,1)S(1)} %get-tuple-element.86.refs_4_), channel_id=1, source_target_pairs={{2,6},{3,7},{4,0},{5,1},{6,10},{7,11},{8,4},{9,5},{10,14},{11,15},... | collective-permute-start | bytes 589832 | tf_op jit(solution)/shard_map/ppermute | solution.py:270
  83.3 13.5 %collective-permute-start.3 = (bf16[2,384,128]{2,1,0:T(8,128)(2,1)S(1)}, bf16[2,384,128]{2,1,0:T(8,128)(2,1)S(1)}, u32[]{:S(2)}, u32[]{:S(2)}) collective-permute-start(bf16[2,384,128]{2,1,0:T(8,128)(2,1)S(1)} %copy-done.15), channel_id=1, source_target_pairs={{0,1},{1,0},{2,3},{3,2},{4,5},{5,4},{6,7},{7,6},{8,9},{9,8},{10,11... | collective-permute-start | bytes 589832 | tf_op jit(solution)/shard_map/ppermute | solution.py:262
  83.7 13.1 %collective-permute-start.52 = (bf16[2,1,384,128]{3,2,1,0:T(8,128)(2,1)S(1)}, bf16[2,1,384,128]{3,2,1,0:T(8,128)(2,1)S(1)}, u32[]{:S(2)}, u32[]{:S(2)}) collective-permute-start(bf16[2,1,384,128]{3,2,1,0:T(8,128)(2,1)S(1)} %get-tuple-element.142), channel_id=1, source_target_pairs={{0,4},{1,5},{4,8},{5,9},{6,2},{7,3},{8,12},{9,13},{10,6},{11,7},{1... | collective-permute-start | bytes 589832 | tf_op jit(solution)/shard_map/ppermute | solution.py:270
  88.0 11.7 %collective-permute-start.53 = (bf16[2,1,384,128]{3,2,1,0:T(8,128)(2,1)S(1)}, bf16[2,1,384,128]{3,2,1,0:T(8,128)(2,1)S(1)}, u32[]{:S(2)}, u32[]{:S(2)}) collective-permute-start(bf16[2,1,384,128]{3,2,1,0:T(8,128)(2,1)S(1)} %get-tuple-element.143), channel_id=1, source_target_pairs={{2,6},{3,7},{4,0},{5,1},{6,10},{7,11},{8,4},{9,5},{10,14},{11,15},... | collective-permute-start | bytes 589832 | tf_op jit(solution)/shard_map/ppermute | solution.py:270
  89.3 10.4 %collective-permute-start.29 = (bf16[2,384,128]{2,1,0:T(8,128)(2,1)S(1)}, bf16[2,384,128]{2,1,0:T(8,128)(2,1)S(1)}, u32[]{:S(2)}, u32[]{:S(2)}) collective-permute-start(bf16[2,384,128]{2,1,0:T(8,128)(2,1)S(1)} %collective-permute-done.25.refs_6_), channel_id=1, source_target_pairs={{0,4},{1,5},{4,8},{5,9},{6,2},{7,3},{8,12},{9,13},{10,6},{11,7},{1... | collective-permute-start | bytes 589832 | tf_op jit(solution)/shard_map/ppermute | solution.py:270
  93.4 9.5 %collective-permute-start.30 = (bf16[2,384,128]{2,1,0:T(8,128)(2,1)S(1)}, bf16[2,384,128]{2,1,0:T(8,128)(2,1)S(1)}, u32[]{:S(2)}, u32[]{:S(2)}) collective-permute-start(bf16[2,384,128]{2,1,0:T(8,128)(2,1)S(1)} %collective-permute-done.26.refs_7_), channel_id=1, source_target_pairs={{0,4},{1,5},{4,8},{5,9},{6,2},{7,3},{8,12},{9,13},{10,6},{11,7},{1... | collective-permute-start | bytes 589832 | tf_op jit(solution)/shard_map/ppermute | solution.py:270
  96.8 33.3 %collective-permute-start.4 = (bf16[2,384,128]{2,1,0:T(8,128)(2,1)S(1)}, bf16[2,384,128]{2,1,0:T(8,128)(2,1)S(1)}, u32[]{:S(2)}, u32[]{:S(2)}) collective-permute-start(bf16[2,384,128]{2,1,0:T(8,128)(2,1)S(1)} %copy-done.9), channel_id=1, source_target_pairs={{0,2},{1,3},{2,0},{3,1},{4,6},{5,7},{6,4},{7,5},{8,10},{9,11},{10,... | collective-permute-start | bytes 589832 | tf_op jit(solution)/shard_map/ppermute | solution.py:262
  96.9 33.3 %collective-permute-start.5 = (bf16[2,384,128]{2,1,0:T(8,128)(2,1)S(1)}, bf16[2,384,128]{2,1,0:T(8,128)(2,1)S(1)}, u32[]{:S(2)}, u32[]{:S(2)}) collective-permute-start(bf16[2,384,128]{2,1,0:T(8,128)(2,1)S(1)} %get-tuple-element.85), channel_id=1, source_target_pairs={{0,3},{1,2},{2,1},{3,0},{4,7},{5,6},{6,5},{7,4},{8,11},{9,10},{10,... | collective-permute-start | bytes 589832 | tf_op jit(solution)/shard_map/ppermute | solution.py:262
  99.7 34.1 %collective-permute-start.49 = (bf16[1,384,128]{2,1,0:T(8,128)(2,1)S(1)}, bf16[1,384,128]{2,1,0:T(8,128)(2,1)S(1)}, u32[]{:S(2)}, u32[]{:S(2)}) collective-permute-start(bf16[1,384,128]{2,1,0:T(8,128)(2,1)S(1)} %get-tuple-element.135), channel_id=1, source_target_pairs={{0,1},{1,0},{2,3},{3,2},{4,5},{5,4},{6,7},{7,6},{8,9},{9,8},{10,11... | collective-permute-start | bytes 294920 | tf_op jit(solution)/shard_map/ppermute | solution.py:262
  99.7 34.1 %collective-permute-start.11 = (bf16[2,384,128]{2,1,0:T(8,128)(2,1)S(1)}, bf16[2,384,128]{2,1,0:T(8,128)(2,1)S(1)}, u32[]{:S(2)}, u32[]{:S(2)}) collective-permute-start(bf16[2,384,128]{2,1,0:T(8,128)(2,1)S(1)} %collective-permute-done.7.refs_6_), channel_id=1, source_target_pairs={{0,4},{1,5},{4,8},{5,9},{6,2},{7,3},{8,12},{9,13},{10,6},{11,7},{1... | collective-permute-start | bytes 589832 | tf_op jit(solution)/shard_map/ppermute | solution.py:270
  102.9 34.1 %collective-permute-start.12 = (bf16[2,384,128]{2,1,0:T(8,128)(2,1)S(1)}, bf16[2,384,128]{2,1,0:T(8,128)(2,1)S(1)}, u32[]{:S(2)}, u32[]{:S(2)}) collective-permute-start(bf16[2,384,128]{2,1,0:T(8,128)(2,1)S(1)} %collective-permute-done.8.refs_7_), channel_id=1, source_target_pairs={{0,4},{1,5},{4,8},{5,9},{6,2},{7,3},{8,12},{9,13},{10,6},{11,7},{1... | collective-permute-start | bytes 589832 | tf_op jit(solution)/shard_map/ppermute | solution.py:270
  130.1 32.4 %collective-permute-start.50 = (bf16[1,384,128]{2,1,0:T(8,128)(2,1)S(1)}, bf16[1,384,128]{2,1,0:T(8,128)(2,1)S(1)}, u32[]{:S(2)}, u32[]{:S(2)}) collective-permute-start(bf16[1,384,128]{2,1,0:T(8,128)(2,1)S(1)} %get-tuple-element.136), channel_id=1, source_target_pairs={{0,2},{1,3},{2,0},{3,1},{4,6},{5,7},{6,4},{7,5},{8,10},{9,11},{10,... | collective-permute-start | bytes 294920 | tf_op jit(solution)/shard_map/ppermute | solution.py:262
  130.2 36.3 %collective-permute-start.51 = (bf16[1,384,128]{2,1,0:T(8,128)(2,1)S(1)}, bf16[1,384,128]{2,1,0:T(8,128)(2,1)S(1)}, u32[]{:S(2)}, u32[]{:S(2)}) collective-permute-start(bf16[1,384,128]{2,1,0:T(8,128)(2,1)S(1)} %get-tuple-element.137), channel_id=1, source_target_pairs={{0,3},{1,2},{2,1},{3,0},{4,7},{5,6},{6,5},{7,4},{8,11},{9,10},{10,... | collective-permute-start | bytes 294920 | tf_op jit(solution)/shard_map/ppermute | solution.py:262
  133.8 34.0 %collective-permute-start.54 = (bf16[1,384,128]{2,1,0:T(8,128)(2,1)S(1)}, bf16[1,384,128]{2,1,0:T(8,128)(2,1)S(1)}, u32[]{:S(2)}, u32[]{:S(2)}) collective-permute-start(bf16[1,384,128]{2,1,0:T(8,128)(2,1)S(1)} %get-tuple-element.145), channel_id=1, source_target_pairs={{0,1},{1,0},{2,3},{3,2},{4,5},{5,4},{6,7},{7,6},{8,9},{9,8},{10,11... | collective-permute-start | bytes 294920 | tf_op jit(solution)/shard_map/ppermute | solution.py:262
  133.8 40.2 %collective-permute-start.34 = (bf16[2,2,384,128]{3,2,1,0:T(8,128)(2,1)S(1)}, bf16[2,2,384,128]{3,2,1,0:T(8,128)(2,1)S(1)}, u32[]{:S(2)}, u32[]{:S(2)}) collective-permute-start(bf16[2,2,384,128]{3,2,1,0:T(8,128)(2,1)S(1)} %get-tuple-element.120), channel_id=1, source_target_pairs={{0,4},{1,5},{4,8},{5,9},{6,2},{7,3},{8,12},{9,13},{10,6},{11,7},{1... | collective-permute-start | bytes 1179656 | tf_op jit(solution)/shard_map/ppermute | solution.py:270
  137.1 38.7 %collective-permute-start.35 = (bf16[2,2,384,128]{3,2,1,0:T(8,128)(2,1)S(1)}, bf16[2,2,384,128]{3,2,1,0:T(8,128)(2,1)S(1)}, u32[]{:S(2)}, u32[]{:S(2)}) collective-permute-start(bf16[2,2,384,128]{3,2,1,0:T(8,128)(2,1)S(1)} %get-tuple-element.121), channel_id=1, source_target_pairs={{2,6},{3,7},{4,0},{5,1},{6,10},{7,11},{8,4},{9,5},{10,14},{11,15},... | collective-permute-start | bytes 1179656 | tf_op jit(solution)/shard_map/ppermute | solution.py:270
  162.5 22.7 %collective-permute-start.16 = (bf16[2,2,384,128]{3,2,1,0:T(8,128)(2,1)S(1)}, bf16[2,2,384,128]{3,2,1,0:T(8,128)(2,1)S(1)}, u32[]{:S(2)}, u32[]{:S(2)}) collective-permute-start(bf16[2,2,384,128]{3,2,1,0:T(8,128)(2,1)S(1)} %get-tuple-element.98), channel_id=1, source_target_pairs={{0,4},{1,5},{4,8},{5,9},{6,2},{7,3},{8,12},{9,13},{10,6},{11,7},{1... | collective-permute-start | bytes 1179656 | tf_op jit(solution)/shard_map/ppermute | solution.py:270
  166.5 18.9 %collective-permute-start.17 = (bf16[2,2,384,128]{3,2,1,0:T(8,128)(2,1)S(1)}, bf16[2,2,384,128]{3,2,1,0:T(8,128)(2,1)S(1)}, u32[]{:S(2)}, u32[]{:S(2)}) collective-permute-start(bf16[2,2,384,128]{3,2,1,0:T(8,128)(2,1)S(1)} %get-tuple-element.99), channel_id=1, source_target_pairs={{2,6},{3,7},{4,0},{5,1},{6,10},{7,11},{8,4},{9,5},{10,14},{11,15},... | collective-permute-start | bytes 1179656 | tf_op jit(solution)/shard_map/ppermute | solution.py:270
  171.8 12.9 %collective-permute-start.31 = (bf16[2,384,128]{2,1,0:T(8,128)(2,1)S(1)}, bf16[2,384,128]{2,1,0:T(8,128)(2,1)S(1)}, u32[]{:S(2)}, u32[]{:S(2)}) collective-permute-start(bf16[2,384,128]{2,1,0:T(8,128)(2,1)S(1)} %get-tuple-element.113), channel_id=1, source_target_pairs={{0,1},{1,0},{2,3},{3,2},{4,5},{5,4},{6,7},{7,6},{8,9},{9,8},{10,11... | collective-permute-start | bytes 589832 | tf_op jit(solution)/shard_map/ppermute | solution.py:262
  174.0 10.9 %collective-permute-start.32 = (bf16[2,384,128]{2,1,0:T(8,128)(2,1)S(1)}, bf16[2,384,128]{2,1,0:T(8,128)(2,1)S(1)}, u32[]{:S(2)}, u32[]{:S(2)}) collective-permute-start(bf16[2,384,128]{2,1,0:T(8,128)(2,1)S(1)} %get-tuple-element.114), channel_id=1, source_target_pairs={{0,2},{1,3},{2,0},{3,1},{4,6},{5,7},{6,4},{7,5},{8,10},{9,11},{10,... | collective-permute-start | bytes 589832 | tf_op jit(solution)/shard_map/ppermute | solution.py:262
  175.8 7.4 %collective-permute-start.56 = (bf16[1,384,128]{2,1,0:T(8,128)(2,1)S(1)}, bf16[1,384,128]{2,1,0:T(8,128)(2,1)S(1)}, u32[]{:S(2)}, u32[]{:S(2)}) collective-permute-start(bf16[1,384,128]{2,1,0:T(8,128)(2,1)S(1)} %get-tuple-element.147), channel_id=1, source_target_pairs={{0,3},{1,2},{2,1},{3,0},{4,7},{5,6},{6,5},{7,4},{8,11},{9,10},{10,... | collective-permute-start | bytes 294920 | tf_op jit(solution)/shard_map/ppermute | solution.py:262
  183.1 7.2 %collective-permute-start.33 = (bf16[2,384,128]{2,1,0:T(8,128)(2,1)S(1)}, bf16[2,384,128]{2,1,0:T(8,128)(2,1)S(1)}, u32[]{:S(2)}, u32[]{:S(2)}) collective-permute-start(bf16[2,384,128]{2,1,0:T(8,128)(2,1)S(1)} %get-tuple-element.115), channel_id=1, source_target_pairs={{0,3},{1,2},{2,1},{3,0},{4,7},{5,6},{6,5},{7,4},{8,11},{9,10},{10,... | collective-permute-start | bytes 589832 | tf_op jit(solution)/shard_map/ppermute | solution.py:262
  185.2 9.0 %collective-permute-start.37 = (bf16[2,384,128]{2,1,0:T(8,128)(2,1)S(1)}, bf16[2,384,128]{2,1,0:T(8,128)(2,1)S(1)}, u32[]{:S(2)}, u32[]{:S(2)}) collective-permute-start(bf16[2,384,128]{2,1,0:T(8,128)(2,1)S(1)} %get-tuple-element.124), channel_id=1, source_target_pairs={{0,2},{1,3},{2,0},{3,1},{4,6},{5,7},{6,4},{7,5},{8,10},{9,11},{10,... | collective-permute-start | bytes 589832 | tf_op jit(solution)/shard_map/ppermute | solution.py:262
  185.5 13.3 %collective-permute-start.38 = (bf16[2,384,128]{2,1,0:T(8,128)(2,1)S(1)}, bf16[2,384,128]{2,1,0:T(8,128)(2,1)S(1)}, u32[]{:S(2)}, u32[]{:S(2)}) collective-permute-start(bf16[2,384,128]{2,1,0:T(8,128)(2,1)S(1)} %get-tuple-element.125), channel_id=1, source_target_pairs={{0,3},{1,2},{2,1},{3,0},{4,7},{5,6},{6,5},{7,4},{8,11},{9,10},{10,... | collective-permute-start | bytes 589832 | tf_op jit(solution)/shard_map/ppermute | solution.py:262
  190.3 12.3 %collective-permute-start.14 = (bf16[2,384,128]{2,1,0:T(8,128)(2,1)S(1)}, bf16[2,384,128]{2,1,0:T(8,128)(2,1)S(1)}, u32[]{:S(2)}, u32[]{:S(2)}) collective-permute-start(bf16[2,384,128]{2,1,0:T(8,128)(2,1)S(1)} %get-tuple-element.92), channel_id=1, source_target_pairs={{0,2},{1,3},{2,0},{3,1},{4,6},{5,7},{6,4},{7,5},{8,10},{9,11},{10,... | collective-permute-start | bytes 589832 | tf_op jit(solution)/shard_map/ppermute | solution.py:262
  191.6 15.6 %collective-permute-start.15 = (bf16[2,384,128]{2,1,0:T(8,128)(2,1)S(1)}, bf16[2,384,128]{2,1,0:T(8,128)(2,1)S(1)}, u32[]{:S(2)}, u32[]{:S(2)}) collective-permute-start(bf16[2,384,128]{2,1,0:T(8,128)(2,1)S(1)} %get-tuple-element.93), channel_id=1, source_target_pairs={{0,3},{1,2},{2,1},{3,0},{4,7},{5,6},{6,5},{7,4},{8,11},{9,10},{10,... | collective-permute-start | bytes 589832 | tf_op jit(solution)/shard_map/ppermute | solution.py:262
  192.1 15.1 %collective-permute-start.18 = (bf16[2,384,128]{2,1,0:T(8,128)(2,1)S(1)}, bf16[2,384,128]{2,1,0:T(8,128)(2,1)S(1)}, u32[]{:S(2)}, u32[]{:S(2)}) collective-permute-start(bf16[2,384,128]{2,1,0:T(8,128)(2,1)S(1)} %get-tuple-element.101), channel_id=1, source_target_pairs={{0,1},{1,0},{2,3},{3,2},{4,5},{5,4},{6,7},{7,6},{8,9},{9,8},{10,11... | collective-permute-start | bytes 589832 | tf_op jit(solution)/shard_map/ppermute | solution.py:262
  194.3 16.9 %collective-permute-start.19 = (bf16[2,384,128]{2,1,0:T(8,128)(2,1)S(1)}, bf16[2,384,128]{2,1,0:T(8,128)(2,1)S(1)}, u32[]{:S(2)}, u32[]{:S(2)}) collective-permute-start(bf16[2,384,128]{2,1,0:T(8,128)(2,1)S(1)} %get-tuple-element.102), channel_id=1, source_target_pairs={{0,2},{1,3},{2,0},{3,1},{4,6},{5,7},{6,4},{7,5},{8,10},{9,11},{10,... | collective-permute-start | bytes 589832 | tf_op jit(solution)/shard_map/ppermute | solution.py:262
  198.8 16.6 %collective-permute-start.20 = (bf16[2,384,128]{2,1,0:T(8,128)(2,1)S(1)}, bf16[2,384,128]{2,1,0:T(8,128)(2,1)S(1)}, u32[]{:S(2)}, u32[]{:S(2)}) collective-permute-start(bf16[2,384,128]{2,1,0:T(8,128)(2,1)S(1)} %get-tuple-element.103), channel_id=1, source_target_pairs={{0,3},{1,2},{2,1},{3,0},{4,7},{5,6},{6,5},{7,4},{8,11},{9,10},{10,... | collective-permute-start | bytes 589832 | tf_op jit(solution)/shard_map/ppermute | solution.py:262
  (44 other events, 205.6 us)

commit v2 on v1

v2 whole, which is shorter than its diff:
```python
import functools
import math

import jax
import jax.numpy as jnp
from jax import lax
from jax.experimental import pallas as pl
from jax.experimental.pallas import tpu as pltpu
from jax.sharding import PartitionSpec as P

HEADS = 20
HEAD_DIM = 64
WIDE = 2 * HEAD_DIM
BLK = 128
LIST = 8
MIN_LIVE = 4
QUAD = 4
PIECES = 2 * QUAD
INS = (2, 2, 1)
OWNS = (2, 3)
OUTS = ((2, False), (2, False), (1, False))
COSTS = {"pack": 1.0, "gather": 0.5, "attend": 8.0, "combine": 0.3, "unpack": 0.8}
LOG2E = math.log2(math.e)
PACK_VMEM = 60 * 1024 * 1024
ATTEND_VMEM = 24 * 1024 * 1024
SMALL_VMEM = 12 * 1024 * 1024
PLAN_ROWS = 16
SPLIT = 128
ANYWHERE = pl.BlockSpec(memory_space=pl.ANY)


def cost(name, heads):
    return pl.CostEstimate(
        flops=int(COSTS[name] * heads * 1153e6), bytes_accessed=0, transcendentals=0
    )


def swapped(x):
    return jnp.concatenate([x[:, HEAD_DIM:], x[:, :HEAD_DIM]], axis=1)


def halves(first, second, core, left):
    low = jnp.where(left, first, swapped(second))
    high = jnp.where(left, swapped(first), second)
    return jnp.where(core == 0, low, high), jnp.where(core == 0, high, low)


def pair_columns(place, other):
    return pl.ds(pl.multiple_of((((place[0] // 2) % 2) ^ other) * WIDE, WIDE), WIDE)


def plan_rows(lists, counts):
    blocks = counts.shape[0]
    lane = lax.broadcasted_iota(jnp.int32, (PLAN_ROWS, WIDE), 1)
    row = lax.broadcasted_iota(jnp.int32, (PLAN_ROWS, WIDE), 0)
    values = jnp.zeros((PLAN_ROWS, WIDE), jnp.int32)
    for block in range(blocks):
        for slot in range(LIST):
            values = jnp.where(lane == block * LIST + slot, lists[block, slot], values)
        values = jnp.where(lane == blocks * LIST + block, counts[block], values)
    high = values // SPLIT
    return jnp.where(row == 0, values - high * SPLIT, jnp.where(row == 1, high, 0)).astype(jnp.float32)


def pack_body(place, lists, counts, *refs, heads, own, planned, after):
    sources, outs = refs[: 4 * heads], refs[4 * heads + after :]
    rows = sources[0].shape[0]
    left = lax.broadcasted_iota(jnp.int32, (rows, WIDE), 1) < HEAD_DIM
    plan = plan_rows(lists, counts).astype(jnp.bfloat16) if planned else None
    for h in range(heads):
        for kind in range(2):
            first, second = sources[4 * h + 2 * kind], sources[4 * h + 2 * kind + 1]
            pair = halves(first[...], second[...], place[0] % 2, left)
            if not own:
                outs[0][kind, h, :rows, :], outs[1][kind, h, :rows, :] = pair
            else:
                keys_ref, partner_ref, own_ref = outs
                partner_ref[kind, h, :rows, :] = pair[1]
                if kind == 0:
                    keys_ref[0, h], keys_ref[1, h] = pair
                else:
                    own_ref[0, h] = pair[0]
            if planned:
                for out in outs[1:2] if own else outs:
                    out[kind, h, rows:, :] = plan


def pack(scalars, arrays, start, heads, own, planned, after):
    rows = arrays[0].shape[0]

    def source(h):
        return pl.BlockSpec(
            (rows, WIDE),
            lambda _, place, *__: (0, 2 * (start + h) + (((place[0] // 2) % 2) ^ (0 if own else 1))),
        )

    shapes = [(2, heads, rows + PLAN_ROWS * planned, WIDE)] * 2
    if own:
        shapes = [(2, heads, rows, WIDE), shapes[0], (1, heads, rows, WIDE)]
    return pl.pallas_call(
        functools.partial(pack_body, heads=heads, own=own, planned=planned, after=len(after)),
        grid_spec=pltpu.PrefetchScalarGridSpec(
            num_scalar_prefetch=3,
            grid=(1,),
            in_specs=[source(h) for h in range(heads) for _ in range(4)] + [ANYWHERE] * len(after),
            out_specs=[pl.BlockSpec(shape, lambda *_: (0, 0, 0, 0)) for shape in shapes],
        ),
        out_shape=[jax.ShapeDtypeStruct(shape, jnp.bfloat16) for shape in shapes],
        compiler_params=pltpu.CompilerParams(vmem_limit_bytes=PACK_VMEM),
        cost_estimate=cost("pack", heads),
        name="pack",
    )(*scalars, *(arrays * heads), *after)


def follow_body(*refs):
    pass


def follow(x, after):
    return pl.pallas_call(
        follow_body,
        in_specs=[ANYWHERE] * 2,
        out_specs=ANYWHERE,
        out_shape=jax.ShapeDtypeStruct(x.shape, x.dtype),
        input_output_aliases={0: 0},
        compiler_params=pltpu.CompilerParams(vmem_limit_bytes=PACK_VMEM),
        name="follow",
    )(x, after)


def route_body(place, lists, counts, facing_ref, crossing_ref, partner_ref, out_ref):
    blocks = counts.shape[0]
    lane = lax.broadcasted_iota(jnp.int32, (1, WIDE), 1)
    own = plan_rows(lists, counts)
    for piece in range(QUAD):
        if piece == 0:
            rows = own
        else:
            source = (partner_ref, facing_ref, crossing_ref)[piece - 1]
            rows = source[0, 0].astype(jnp.float32)
        values = rows[0:1] + SPLIT * rows[1:2]
        owner = jnp.floor((values + 0.5) * (1.0 / blocks))
        quad = jnp.floor((owner + 0.5) * (1.0 / QUAD))
        inside = (owner - QUAD * quad).astype(jnp.int32) ^ (place[0] % QUAD)
        away = jnp.where(quad.astype(jnp.int32) == place[0] // QUAD, 0, QUAD)
        slots = (inside + away) * blocks + (values - blocks * owner).astype(jnp.int32)
        out_ref[piece : piece + 1, :] = jnp.where(
            lane < blocks * LIST, slots, values.astype(jnp.int32)
        )
    out_ref[QUAD:, :] = jnp.zeros((QUAD, WIDE), jnp.int32)


def route(scalars, facing, crossing, partner):
    rows = facing.shape[2] - PLAN_ROWS
    tail = pl.BlockSpec((1, 1, PLAN_ROWS, WIDE), lambda *_: (0, 0, rows // PLAN_ROWS, 0))
    return pl.pallas_call(
        route_body,
        grid_spec=pltpu.PrefetchScalarGridSpec(
            num_scalar_prefetch=3,
            grid=(1,),
            in_specs=[tail] * 3,
            out_specs=pl.BlockSpec((2 * QUAD, WIDE), lambda *_: (0, 0)),
        ),
        out_shape=jax.ShapeDtypeStruct((2 * QUAD, WIDE), jnp.int32),
        compiler_params=pltpu.CompilerParams(vmem_limit_bytes=SMALL_VMEM),
        cost_estimate=cost("gather", 1),
        name="route",
    )(*scalars, facing, crossing, partner)


def part(source, rows):
    _, index, first = source
    return pl.BlockSpec((1, 1, rows, WIDE), lambda h, *_: (index, first + h, 0, 0))


def unpack_body(place, *refs):
    parts, outs = refs[: 2 * QUAD], refs[-4:]
    core = place[0] % 2
    left = lax.broadcasted_iota(jnp.int32, (outs[0].shape[0], WIDE), 1) < HEAD_DIM
    for kind, (first_out, second_out) in enumerate((outs[:2], outs[2:])):
        for other in range(2):
            column = pair_columns(place, other)
            even = parts[kind * QUAD + 2 * other][0, 0]
            odd = parts[kind * QUAD + 2 * other + 1][0, 0]
            low = jnp.where(core == 0, even, odd)
            high = jnp.where(core == 0, odd, even)
            first_out[:, column] = jnp.where(left, low, swapped(high))
            second_out[:, column] = jnp.where(left, swapped(low), high)


def unpack(place, sources, so_far, start, heads, shape):
    rows, width = shape
    target = pl.BlockSpec((rows, 2 * WIDE), lambda h, _: (0, start + h))
    kept = [] if so_far is None else list(so_far)
    return pl.pallas_call(
        unpack_body,
        grid_spec=pltpu.PrefetchScalarGridSpec(
            num_scalar_prefetch=1,
            grid=(heads,),
            in_specs=[part(source, rows) for source in sources] + [ANYWHERE] * len(kept),
            out_specs=[target] * 4,
        ),
        out_shape=[jax.ShapeDtypeStruct(shape, jnp.bfloat16)] * 4,
        input_output_aliases={1 + 2 * QUAD + n: n for n in range(len(kept))},
        compiler_params=pltpu.CompilerParams(vmem_limit_bytes=SMALL_VMEM),
        cost_estimate=cost("unpack", heads),
        name="unpack",
    )(place, *[source[0] for source in sources], *kept)


def gather_body(facing_ref, crossing_ref, *refs):
    out_ref = refs[-1]
    out_ref[0, 0] = facing_ref[0, 0]
    out_ref[1, 0] = crossing_ref[0, 0]


def gather(facing, crossing, rows, after):
    heads = facing.shape[1]
    return pl.pallas_call(
        gather_body,
        grid=(heads,),
        in_specs=[part((facing, 0, 0), rows), part((crossing, 0, 0), rows)]
        + [ANYWHERE] * len(after),
        out_specs=pl.BlockSpec((2, 1, rows, WIDE), lambda h: (0, h, 0, 0)),
        out_shape=jax.ShapeDtypeStruct((2, heads, rows, WIDE), jnp.bfloat16),
        compiler_params=pltpu.CompilerParams(vmem_limit_bytes=SMALL_VMEM),
        cost_estimate=cost("gather", heads),
        name="gather",
    )(facing, crossing, *after)


def attend_body(plan, *refs, blocks, after):
    query_parts, key_parts = refs[:QUAD], refs[QUAD : QUAD + PIECES]
    refs = refs[QUAD + PIECES + after :]
    results, own, (near, far, window, window_t, total) = refs[:QUAD], refs[QUAD : 2 * QUAD], refs[2 * QUAD : 2 * QUAD + 5]
    products, pairs = refs[-4:-2], refs[-2:]
    score_scale = 1.0 / math.sqrt(HEAD_DIM)
    for piece in range(PIECES):
        for block in range(blocks):
            rows = key_parts[piece][0, 0, block * BLK : (block + 1) * BLK, :]
            window[piece * blocks + block] = rows
            window_t[piece * blocks + block] = rows.T
    total[...] = jnp.zeros_like(total)
    left = lax.broadcasted_iota(jnp.int32, (BLK, WIDE), 1) < HEAD_DIM
    upper = lax.broadcasted_iota(jnp.int32, (WIDE, BLK), 0) < HEAD_DIM
    spans = [slice(slot * BLK, (slot + 1) * BLK) for slot in range(LIST)]

    def listed(index):
        piece, block = divmod(index, blocks)
        return [plan[piece, block * LIST + slot] for slot in range(LIST)]

    def packed_rows(index):
        block = index % blocks
        return query_parts[index // blocks][0, 0, block * BLK : (block + 1) * BLK, :]

    def folded(combine_rows, x):
        return combine_rows(x.reshape(BLK // 8, 8, BLK), axis=0)

    tops, inverses = {}, {}

    def score(index):
        turned = packed_rows(index).T
        nothing = jnp.zeros_like(turned)
        operand = jnp.concatenate(
            [jnp.where(upper, turned, nothing), jnp.where(upper, nothing, turned)], axis=1
        )
        count = plan[index // blocks, blocks * LIST + index % blocks]
        product = products[index % 2]
        top = None
        for slot, block in enumerate(listed(index)):
            both = jnp.dot(window[block], operand, preferred_element_type=jnp.float32)
            scores = both[:, :BLK]
            if slot >= MIN_LIVE:
                scores = jnp.where(slot < count, scores, -jnp.inf)
            product[spans[slot], :BLK] = scores
            product[spans[slot], BLK:] = both[:, BLK:]
            here = folded(jnp.max, scores)
            top = here if top is None else jnp.maximum(top, here)
        tops[index] = top

    def soften(index):
        product, pair = products[index % 2], pairs[index % 2]
        top = jnp.max(tops.pop(index), axis=0, keepdims=True)
        row_sum = row_dot = jnp.zeros((8, BLK), jnp.float32)
        for span in spans:
            raised = jnp.exp2((product[span, :BLK] - top) * (LOG2E * score_scale))
            product[span, :BLK] = raised
            pair[span, :BLK] = raised.astype(jnp.bfloat16)
            row_sum += folded(jnp.sum, raised)
            row_dot += folded(jnp.sum, raised * product[span, BLK:])
        inverse = 1.0 / jnp.sum(row_sum, axis=0, keepdims=True)
        row_dot = jnp.sum(row_dot, axis=0, keepdims=True) * inverse
        for span in spans:
            pair[span, BLK:] = (product[span, :BLK] * (product[span, BLK:] - row_dot)).astype(
                jnp.bfloat16
            )
        inverses[index] = inverse

    def spread(index):
        pair, inverse = pairs[index % 2], inverses.pop(index)
        blocks_listed = listed(index)
        scaled = packed_rows(index).astype(jnp.float32) * jnp.broadcast_to(inverse, (BLK, BLK)).T
        blank = jnp.zeros_like(scaled)
        operand = jnp.concatenate(
            [jnp.where(left, blank, scaled), jnp.where(left, scaled * score_scale, blank)], 0
        ).astype(jnp.bfloat16)
        keys_t = jnp.concatenate([window_t[block] for block in blocks_listed], axis=1)
        product = jnp.dot(keys_t, pair[...], preferred_element_type=jnp.float32)
        query_part = product[:HEAD_DIM, BLK:] * (inverse * score_scale)
        attended_part = product[HEAD_DIM:, :BLK] * inverse
        block = index % blocks
        results[index // blocks][0, 0, block * BLK : (block + 1) * BLK, :] = (
            jnp.concatenate([query_part, attended_part], 0).astype(jnp.bfloat16).T
        )
        for span, block in zip(spans, blocks_listed):
            total[block] += jnp.dot(pair[span, :], operand, preferred_element_type=jnp.float32)

    count_all = QUAD * blocks
    for step in range(count_all + 2):
        if step >= 2:
            spread(step - 2)
        if 1 <= step <= count_all:
            soften(step - 1)
        if step < count_all:
            score(step)

    for piece in range(PIECES):
        for block in range(blocks):
            span = slice(block * BLK, (block + 1) * BLK)
            share = total[piece * blocks + block]
            if piece < QUAD:
                own[piece][0, span, :] = share
            elif piece < QUAD + 2:
                near[piece - QUAD, 0, span, :] = share.astype(jnp.bfloat16)
            else:
                far[piece - QUAD - 2, 0, span, :] = share.astype(jnp.bfloat16)


def attend(plan, sources, heads, split, after):
    rows = sources[0][0].shape[2]
    blocks = rows // BLK
    piece = pl.BlockSpec((1, rows, WIDE), lambda h, *_: (h, 0, 0))
    couple = pl.BlockSpec((2, 1, rows, WIDE), lambda h, *_: (0, h, 0, 0))
    shape = (heads, rows, WIDE)
    depth = 1 if split else 2
    result = part((None, depth - 1, 0), rows)
    outs = pl.pallas_call(
        functools.partial(attend_body, blocks=blocks, after=len(after)),
        grid_spec=pltpu.PrefetchScalarGridSpec(
            num_scalar_prefetch=1,
            grid=(heads,),
            in_specs=[part(source, rows) for source in sources] + [ANYWHERE] * len(after),
            out_specs=[result] * QUAD + [piece] * QUAD + [couple] * 2,
            scratch_shapes=[
                pltpu.VMEM((PIECES * blocks, BLK, WIDE), jnp.bfloat16),
                pltpu.VMEM((PIECES * blocks, WIDE, BLK), jnp.bfloat16),
                pltpu.VMEM((PIECES * blocks, BLK, WIDE), jnp.float32),
            ]
            + [pltpu.VMEM((LIST * BLK, 2 * BLK), jnp.float32)] * 2
            + [pltpu.VMEM((LIST * BLK, 2 * BLK), jnp.bfloat16)] * 2,
        ),
        out_shape=[jax.ShapeDtypeStruct((depth,) + shape, jnp.bfloat16)] * QUAD
        + [jax.ShapeDtypeStruct(shape, jnp.float32)] * QUAD
        + [jax.ShapeDtypeStruct((2,) + shape, jnp.bfloat16)] * 2,
        compiler_params=pltpu.CompilerParams(vmem_limit_bytes=ATTEND_VMEM),
        cost_estimate=cost("attend", heads),
        name="attend",
    )(plan, *[source[0] for source in sources], *after)
    return outs[:QUAD], outs[QUAD : 2 * QUAD], outs[2 * QUAD], outs[2 * QUAD + 1]


def combine_body(*refs):
    own, near, far, outs = refs[:QUAD], refs[QUAD], refs[QUAD + 1], refs[-QUAD:]
    for piece in range(QUAD):
        other = near if piece < 2 else far
        outs[piece][0, 0] = (own[piece][0] + other[piece % 2, 0].astype(jnp.float32)).astype(
            jnp.bfloat16
        )


def combine(own, near, far, results, after):
    heads, rows, _ = own[0].shape
    piece = pl.BlockSpec((1, rows, WIDE), lambda h: (h, 0, 0))
    couple = pl.BlockSpec((2, 1, rows, WIDE), lambda h: (0, h, 0, 0))
    shape = results[0].shape if results else (1, heads, rows, WIDE)
    return pl.pallas_call(
        combine_body,
        grid=(heads,),
        in_specs=[piece] * QUAD + [couple] * 2 + [ANYWHERE] * (len(results) + len(after)),
        out_specs=[part((None, 0, 0), rows)] * QUAD,
        out_shape=[jax.ShapeDtypeStruct(shape, jnp.bfloat16)] * QUAD,
        input_output_aliases={QUAD + 2 + n: n for n in range(len(results))},
        compiler_params=pltpu.CompilerParams(vmem_limit_bytes=SMALL_VMEM),
        cost_estimate=cost("combine", heads),
        name="combine",
    )(*own, near, far, *results, *after)


def started(sizes):
    return [sum(sizes[:n]) for n in range(len(sizes))]


def local(queries, key_rows, value_rows, out_grad, block_lists, list_counts):
    rows, width = queries.shape
    shards = lax.axis_size("tm")
    shard = lax.axis_index("tm")
    arrays = (key_rows, value_rows, queries, out_grad)

    def across(x, flip, name="lists"):
        with jax.named_scope(name):
            return lax.ppermute(x, "tm", [(i, i ^ flip) for i in range(shards)])

    def along(x, sign, name):
        route = []
        for i in range(shards):
            j = i + (-QUAD if i % QUAD < 2 else QUAD) * sign
            if 0 <= j < shards:
                route.append((i, j))
        with jax.named_scope(name):
            return lax.ppermute(x, "tm", route)

    def all_ways(parts, name):
        return [parts[0]] + [across(parts[flip], flip, name) for flip in (2, 3, 1)]

    scalars = (shard.astype(jnp.int32).reshape(1), block_lists, list_counts)
    ins, owns = [], []
    after = []
    for n, (start, heads) in enumerate(zip(started(INS), INS)):
        planned = n == 0
        facing, crossing = pack(scalars, arrays, start, heads, False, planned, after)
        after = [crossing]
        if n:
            facing, crossing = follow(facing, ins[-1][1]), follow(crossing, ins[-1][2])
        ins.append((start, across(facing, 2, f"facing{n}"), across(crossing, 3, f"crossing{n}")))
        if n < len(OWNS):
            start, heads = started(OWNS)[n], OWNS[n]
            keys, partner, query_own = pack(scalars, arrays, start, heads, True, planned, after)
            after = [partner]
            near = along(keys, 1, f"near{n}")
            partner = across(partner, 1, f"partner{n}")
            near_partner = across(near, 1, f"near_partner{n}")
            owns.append((start, keys, partner, query_own, near, near_partner))
    plan = route(scalars, ins[0][1], ins[0][2], owns[0][2])

    outs, fars, pending, previous, behind, ahead, earlier = None, {}, None, [], [], [], []
    calls = list(enumerate(zip(started([heads for heads, _ in OUTS]), OUTS)))
    for n, call in calls + [(len(calls), None)]:
        waiting, pending = pending, None
        if call is not None:
            start, (heads, split) = call
            first, keys, partner, query_own, near, near_partner = [
                o for o in owns if o[0] <= start
            ][-1]
            first = start - first
            later, facing, crossing = [i for i in ins if i[0] <= start][-1]
            if later not in fars:
                gathered = gather(facing, crossing, rows, earlier)
                fars[later] = along(gathered, -1, f"far{len(fars)}")
            far = fars[later]
            later = start - later
            sources = [
                (query_own, 0, first), (partner, 1, first), (facing, 1, later), (crossing, 1, later),
                (keys, 0, first), (partner, 0, first), (facing, 0, later), (crossing, 0, later),
                (near, 0, first), (near_partner, 1, first), (far, 0, later), (far, 1, later),
            ]
            results, own, near_back, far_back = attend(plan, sources, heads, split, previous + behind)
            earlier, previous = previous, [own[0]]
            if split:
                results = all_ways(results, f"results{n}")
            near_back = along(near_back, -1, f"near_back{n}")
            far_back = along(far_back, 1, f"far_back{n}")
            pending = (n, start, heads, split, results, own, near_back, far_back)
        if waiting is None:
            continue
        m, start, heads, split, results, own, near_back, far_back = waiting
        sums = combine(own, near_back, far_back, [] if split else results, (previous if call else []) + ahead)
        behind = [sums[0]]
        sums = all_ways(sums, f"sums{m}")
        ahead = sums[1:3] if m < len(OUTS) - 2 else []
        order = (0, 3, 1, 2)
        pieces = [(sums[k], 0, 0) for k in order]
        pieces += [(results[k], 0, 0) if split else (sums[k], 1, 0) for k in order]
        outs = unpack(scalars[0], pieces, outs, start, heads, (rows, width))
    key_grad, value_grad, query_grad, attended = outs
    return attended, query_grad, key_grad, value_grad


def solution(mesh):
    rows = P(("groups", "tm"), None)
    return jax.shard_map(
        local,
        mesh=mesh,
        in_specs=(rows, rows, rows, rows, rows, P(("groups", "tm"))),
        out_specs=(rows, rows, rows, rows),
        check_vma=False,
    )
```

time: 218 us -> 148 us (0.68)
  starting transfers between devices: 85.9 us -> 49.7 us
  local copies, waits for them, and re-layouts: 22.2 us -> 5.94 us
  waiting for transfers between devices: 38.7 us -> 28.6 us
  Pallas kernels: 68.7 us -> 61.7 us
    ppermute x39 -> x19, starting transfers between devices: 43 us -> 22.8 us  [across(): return lax.ppermute(x, 'tm', [(i, i ^ flip) for i in range(shards)])]
    ppermute x18 -> x11, starting transfers between devices: 42.9 us -> 26.9 us  [along(): return lax.ppermute(x, 'tm', route)]
    unnamed x70 -> x34, local copies, waits for them, and re-layouts: 21.1 us -> 5.94 us
    ppermute x39 -> x19, waiting for transfers between devices: 33.2 us -> 25.2 us  [across(): return lax.ppermute(x, 'tm', [(i, i ^ flip) for i in range(shards)])]
    pallas_call x6 -> x16, Pallas kernels: 64 us -> 57.2 us  [the longest x3 39.9 us: attend(): pl.pallas_call(functools.partial(attend_body, blocks=blocks, after=len(af...]
    ppermute x18 -> x11, waiting for transfers between devices: 5.44 us -> 3.38 us  [along(): return lax.ppermute(x, 'tm', route)]
  transfers between devices with their start and end apart: 57 -> 30, of which waited for: 12 -> 7; matrix products, arithmetic and copies ran while one was open for 0% -> 0% of each run, Pallas kernels for 31% -> 39%
where the time goes in v2:
time: 148 us; the launch traced here: 147 us
  Pallas kernels  61.7 us (42%)
  starting transfers between devices  49.7 us (34%)
  waiting for transfers between devices  28.6 us (19%)
  local copies, waits for them, and re-layouts  5.94 us (4%)
    pallas_call x3, Pallas kernels, attend(): pl.pallas_call(functools.partial(attend_body, blocks=blocks, after=len(af...  39.9 us
    ppermute x11, starting transfers between devices, along(): return lax.ppermute(x, 'tm', route)  26.9 us
    ppermute x19, waiting for transfers between devices, across(): return lax.ppermute(x, 'tm', [(i, i ^ flip) for i in range(shards)])  25.2 us
    ppermute x19, starting transfers between devices, across(): return lax.ppermute(x, 'tm', [(i, i ^ flip) for i in range(shards)])  22.8 us
    pallas_call x5, Pallas kernels, pack(): pl.pallas_call(functools.partial(pack_body, heads=heads, own=own, planned...  15.8 us
    unnamed x34, local copies, waits for them, and re-layouts  5.94 us
    pallas_call x3, Pallas kernels, unpack(): pl.pallas_call(unpack_body, grid_spec=pltpu.PrefetchScalarGridSpec(num_sc...  3.94 us
    ppermute x11, waiting for transfers between devices, along(): return lax.ppermute(x, 'tm', route)  3.38 us
  transfers between devices with their start and end apart: 30, of which 7 were waited for; matrix products, arithmetic and copies ran while one was open for 0% of the time, Pallas kernels for 39%

profile of v2, /device:TPU:1, one launch (start us, length us, event | category | flops | bytes accessed | tf_op | source)
XLA Modules:
  0.0 146.9 jit_solution(6686007196535025834)
XLA Ops:
  0.6 3.1 %pack.5 = (bf16[2,2,400,128]{3,2,1,0:T(8,128)(2,1)}, bf16[2,2,400,128]{3,2,1,0:T(8,128)(2,1)}) custom-call(s32[1]{0:T(128)} %bitcast.place, s32[3,8]{1,0:T(4,128)} %lists.11, s32[3]{0:T(128)} %counts.11, bf16[384,1280]{1,0:T(8,128)(2,1)} %refs_0_.9, bf16[384,1280]{1,0:T(8,128)(2,1)} %refs_1_.9, bf16[384,1280]{1,0:T(8,128)(2,1)} %refs_2_.9, ...), custom_call_target="tpu_custom_call" | custom-call | flops 2305999872 | tf_op jit(solution)/shard_map/pack/pallas_call | solution.py:100
  3.8 2.1 %collective-permute-start = (bf16[2,2,400,128]{3,2,1,0:T(8,128)(2,1)}, bf16[2,2,400,128]{3,2,1,0:T(8,128)(2,1)S(1)}, u32[]{:S(2)}, u32[]{:S(2)}) collective-permute-start(bf16[2,2,400,128]{3,2,1,0:T(8,128)(2,1)} %get-tuple-element.70), channel_id=1, source_target_pairs={{0,2},{1,3},{2,0},{3,1},{4,6},{5,7},{6,4},{7,5},{8,10},{9,11},{10,... | collective-permute-start | bytes 1228808 | tf_op jit(solution)/shard_map/facing0/ppermute | solution.py:411
  5.8 0.6 collective-permute-start.1
  6.4 3.2 %pack.6 = (bf16[2,2,384,128]{3,2,1,0:T(8,128)(2,1)}, bf16[2,2,400,128]{3,2,1,0:T(8,128)(2,1)}, bf16[1,2,384,128]{3,2,1,0:T(8,128)(2,1)}) custom-call(s32[1]{0:T(128)} %bitcast.place, s32[3,8]{1,0:T(4,128)} %lists.11, s32[3]{0:T(128)} %counts.11, bf16[384,1280]{1,0:T(8,128)(2,1)} %refs_0_.9, bf16[384,1280]{1,0:T(8,128)(2,1)} %refs_1_.9, ...), custom_call_target="tpu_custom_call" | custom-call | flops 2305999872 | tf_op jit(solution)/shard_map/pack/pallas_call | solution.py:100
  9.6 1.3 collective-permute-start.10
  11.3 3.1 %pack.7 = (bf16[2,2,384,128]{3,2,1,0:T(8,128)(2,1)}, bf16[2,2,384,128]{3,2,1,0:T(8,128)(2,1)}) custom-call(s32[1]{0:T(128)} %bitcast.place, s32[3,8]{1,0:T(4,128)} %lists.11, s32[3]{0:T(128)} %counts.11, bf16[384,1280]{1,0:T(8,128)(2,1)} %refs_0_.9, bf16[384,1280]{1,0:T(8,128)(2,1)} %refs_1_.9, bf16[384,1280]{1,0:T(8,128)(2,1)} %refs_2_.9, ...), custom_call_target="tpu_custom_call" | custom-call | flops 2305999872 | tf_op jit(solution)/shard_map/pack/pallas_call | solution.py:100
  14.5 3.6 %pack.8 = (bf16[2,3,384,128]{3,2,1,0:T(8,128)(2,1)}, bf16[2,3,384,128]{3,2,1,0:T(8,128)(2,1)}, bf16[1,3,384,128]{3,2,1,0:T(8,128)(2,1)}) custom-call(s32[1]{0:T(128)} %bitcast.place, s32[3,8]{1,0:T(4,128)} %lists.11, s32[3]{0:T(128)} %counts.11, bf16[384,1280]{1,0:T(8,128)(2,1)} %refs_0_.9, bf16[384,1280]{1,0:T(8,128)(2,1)} %refs_1_.9, ...), custom_call_target="tpu_custom_call" | custom-call | flops 3459000064 | tf_op jit(solution)/shard_map/pack/pallas_call | solution.py:100
  18.0 1.3 collective-permute-start.8
  19.3 0.7 copy-done
  20.1 5.2 %collective-permute-start.4 = (bf16[2,2,384,128]{3,2,1,0:T(8,128)(2,1)}, bf16[2,2,384,128]{3,2,1,0:T(8,128)(2,1)S(1)}, u32[]{:S(2)}, u32[]{:S(2)}) collective-permute-start(bf16[2,2,384,128]{3,2,1,0:T(8,128)(2,1)} %follow.4), channel_id=1, source_target_pairs={{0,2},{1,3},{2,0},{3,1},{4,6},{5,7},{6,4},{7,5},{8,10},{9,11},{10,... | collective-permute-start | bytes 1179656 | tf_op jit(solution)/shard_map/facing1/ppermute | solution.py:411
  25.3 0.8 copy-done.2
  26.1 0.7 collective-permute-start.6
  27.2 1.0 copy-done.3
  28.2 0.8 gather.3
  28.9 4.0 %collective-permute-start.12 = (bf16[2,2,384,128]{3,2,1,0:T(8,128)(2,1)}, bf16[2,2,384,128]{3,2,1,0:T(8,128)(2,1)}, u32[]{:S(2)}, u32[]{:S(2)}) collective-permute-start(bf16[2,2,384,128]{3,2,1,0:T(8,128)(2,1)} %gather.3), channel_id=1, source_target_pairs={{0,4},{1,5},{4,8},{5,9},{6,2},{7,3},{8,12},{9,13},{10,6},{11,7},{1... | collective-permute-start | bytes 1179656 | tf_op jit(solution)/shard_map/far0/ppermute | solution.py:420
  32.9 2.8 %pack.9 = (bf16[2,1,384,128]{3,2,1,0:T(8,128)(2,1)}, bf16[2,1,384,128]{3,2,1,0:T(8,128)(2,1)}) custom-call(s32[1]{0:T(128)} %bitcast.place, s32[3,8]{1,0:T(4,128)} %lists.11, s32[3]{0:T(128)} %counts.11, bf16[384,1280]{1,0:T(8,128)(2,1)} %refs_0_.9, bf16[384,1280]{1,0:T(8,128)(2,1)} %refs_1_.9, bf16[384,1280]{1,0:T(8,128)(2,1)} %refs_2_.9, ...), custom_call_target="tpu_custom_call" | custom-call | flops 1152999936 | tf_op jit(solution)/shard_map/pack/pallas_call | solution.py:100
  35.7 0.6 route.1.plan
  36.9 0.6 copy-done.5
  37.5 5.8 %collective-permute-done.6.refs_1_.crossing_ref.refs_3_.refs_7_ = bf16[2,2,384,128]{3,2,1,0:T(8,128)(2,1)S(1)} collective-permute-done((bf16[2,2,384,128]{3,2,1,0:T(8,128)(2,1)}, bf16[2,2,384,128]{3,2,1,0:T(8,128)(2,1)S(1)}, u32[]{:S(2)}, u32[]{:S(2)}) %collective-permute-start.6) | collective-permute-done | bytes 393248 | tf_op jit(solution)/shard_map/crossing1/ppermute | solution.py:411
  43.3 1.5 collective-permute-start.5
  44.8 1.0 copy-done.6
  45.8 1.0 copy-done.8
  46.9 0.8 copy-done.16
  48.0 3.2 %collective-permute-start.14 = (bf16[2,2,384,128]{3,2,1,0:T(8,128)(2,1)S(1)}, bf16[2,2,384,128]{3,2,1,0:T(8,128)(2,1)S(1)}, u32[]{:S(2)}, u32[]{:S(2)}) collective-permute-start(bf16[2,2,384,128]{3,2,1,0:T(8,128)(2,1)S(1)} %gather.5), channel_id=1, source_target_pairs={{0,4},{1,5},{4,8},{5,9},{6,2},{7,3},{8,12},{9,13},{10,6},{11,7},{1... | collective-permute-start | bytes 1179656 | tf_op jit(solution)/shard_map/far1/ppermute | solution.py:420
  51.2 16.5 %attend.3 = (bf16[2,2,384,128]{3,2,1,0:T(8,128)(2,1)S(1)}, bf16[2,2,384,128]{3,2,1,0:T(8,128)(2,1)S(1)}, bf16[2,2,384,128]{3,2,1,0:T(8,128)(2,1)S(1)}, bf16[2,2,...) custom-call(s32[8,128]{1,0:T(8,128)S(1)} %route.1.plan, ...), custom_call_target="tpu_custom_call" | custom-call | flops 18447998976 | tf_op jit(solution)/shard_map/attend/pallas_call | solution.py:347
  67.7 2.1 %collective-permute-start.15 = (bf16[2,2,384,128]{3,2,1,0:T(8,128)(2,1)S(1)}, bf16[2,2,384,128]{3,2,1,0:T(8,128)(2,1)S(1)}, u32[]{:S(2)}, u32[]{:S(2)}) collective-permute-start(bf16[2,2,384,128]{3,2,1,0:T(8,128)(2,1)S(1)} %get-tuple-element.87), channel_id=1, source_target_pairs={{0,4},{1,5},{4,8},{5,9},{6,2},{7,3},{8,12},{9,13},{10,6},{11,7},{1... | collective-permute-start | bytes 1179656 | tf_op jit(solution)/shard_map/near_back0/ppermute | solution.py:420
  69.8 1.3 collective-permute-start.16
  71.2 4.3 %collective-permute-start.13 = (bf16[2,1,384,128]{3,2,1,0:T(8,128)(2,1)S(1)}, bf16[2,1,384,128]{3,2,1,0:T(8,128)(2,1)S(1)}, u32[]{:S(2)}, u32[]{:S(2)}) collective-permute-start(bf16[2,1,384,128]{3,2,1,0:T(8,128)(2,1)S(1)} %gather.4), channel_id=1, source_target_pairs={{0,4},{1,5},{4,8},{5,9},{6,2},{7,3},{8,12},{9,13},{10,6},{11,7},{1... | collective-permute-start | bytes 589832 | tf_op jit(solution)/shard_map/far2/ppermute | solution.py:420
  75.5 15.5 %attend.4 = (bf16[2,2,384,128]{3,2,1,0:T(8,128)(2,1)S(1)}, bf16[2,2,384,128]{3,2,1,0:T(8,128)(2,1)S(1)}, bf16[2,2,384,128]{3,2,1,0:T(8,128)(2,1)S(1)}, bf16[2,2,...) custom-call(s32[8,128]{1,0:T(8,128)S(1)} %route.1.plan, ...), custom_call_target="tpu_custom_call" | custom-call | flops 18447998976 | tf_op jit(solution)/shard_map/attend/pallas_call | solution.py:347
  91.0 2.4 %collective-permute-start.22 = (bf16[2,2,384,128]{3,2,1,0:T(8,128)(2,1)S(1)}, bf16[2,2,384,128]{3,2,1,0:T(8,128)(2,1)S(1)}, u32[]{:S(2)}, u32[]{:S(2)}) collective-permute-start(bf16[2,2,384,128]{3,2,1,0:T(8,128)(2,1)S(1)} %get-tuple-element.111), channel_id=1, source_target_pairs={{0,4},{1,5},{4,8},{5,9},{6,2},{7,3},{8,12},{9,13},{10,6},{11,7},{1... | collective-permute-start | bytes 1179656 | tf_op jit(solution)/shard_map/near_back1/ppermute | solution.py:420
  93.4 1.5 %collective-permute-start.23 = (bf16[2,2,384,128]{3,2,1,0:T(8,128)(2,1)S(1)}, bf16[2,2,384,128]{3,2,1,0:T(8,128)(2,1)S(1)}, u32[]{:S(2)}, u32[]{:S(2)}) collective-permute-start(bf16[2,2,384,128]{3,2,1,0:T(8,128)(2,1)S(1)} %get-tuple-element.112), channel_id=1, source_target_pairs={{2,6},{3,7},{4,0},{5,1},{6,10},{7,11},{8,4},{9,5},{10,14},{11,15},... | collective-permute-start | bytes 1179656 | tf_op jit(solution)/shard_map/far_back1/ppermute | solution.py:420
  95.2 1.1 collective-permute-start.24
  96.3 2.9 %collective-permute-start.25 = (bf16[2,2,384,128]{3,2,1,0:T(8,128)(2,1)S(1)}, bf16[2,2,384,128]{3,2,1,0:T(8,128)(2,1)S(1)}, u32[]{:S(2)}, u32[]{:S(2)}) collective-permute-start(bf16[2,2,384,128]{3,2,1,0:T(8,128)(2,1)S(1)} %get-tuple-element.118), channel_id=1, source_target_pairs={{0,3},{1,2},{2,1},{3,0},{4,7},{5,6},{6,5},{7,4},{8,11},{9,10},{10,... | collective-permute-start | bytes 1179656 | tf_op jit(solution)/shard_map/sums0/ppermute | solution.py:411
  99.3 8.0 %attend.5 = (bf16[2,1,384,128]{3,2,1,0:T(8,128)(2,1)S(1)}, bf16[2,1,384,128]{3,2,1,0:T(8,128)(2,1)S(1)}, bf16[2,1,384,128]{3,2,1,0:T(8,128)(2,1)S(1)}, bf16[2,1,...) custom-call(s32[8,128]{1,0:T(8,128)S(1)} %route.1.plan, ...), custom_call_target="tpu_custom_call" | custom-call | flops 9223999488 | tf_op jit(solution)/shard_map/attend/pallas_call | solution.py:347
  107.2 4.3 %collective-permute-start.17 = (bf16[2,1,384,128]{3,2,1,0:T(8,128)(2,1)S(1)}, bf16[2,1,384,128]{3,2,1,0:T(8,128)(2,1)S(1)}, u32[]{:S(2)}, u32[]{:S(2)}) collective-permute-start(bf16[2,1,384,128]{3,2,1,0:T(8,128)(2,1)S(1)} %get-tuple-element.98), channel_id=1, source_target_pairs={{0,4},{1,5},{4,8},{5,9},{6,2},{7,3},{8,12},{9,13},{10,6},{11,7},{1... | collective-permute-start | bytes 589832 | tf_op jit(solution)/shard_map/near_back2/ppermute | solution.py:420
  111.6 3.0 %collective-permute-done.25.refs_12_.refs_3_.refs_7_ = bf16[2,2,384,128]{3,2,1,0:T(8,128)(2,1)S(1)} collective-permute-done((bf16[2,2,384,128]{3,2,1,0:T(8,128)(2,1)S(1)}, bf16[2,2,384,128]{3,2,1,0:T(8,128)(2,1)S(1)}, u32[]{:S(2)}, u32[]{:S(2)}) %collective-permute-start.25) | collective-permute-done | bytes 393248 | tf_op jit(solution)/shard_map/sums0/ppermute | solution.py:411
  114.9 1.3 collective-permute-start.18
  116.2 3.4 %collective-permute-start.27 = (bf16[2,2,384,128]{3,2,1,0:T(8,128)(2,1)S(1)}, bf16[2,2,384,128]{3,2,1,0:T(8,128)(2,1)S(1)}, u32[]{:S(2)}, u32[]{:S(2)}) collective-permute-start(bf16[2,2,384,128]{3,2,1,0:T(8,128)(2,1)S(1)} %get-tuple-element.121), channel_id=1, source_target_pairs={{0,2},{1,3},{2,0},{3,1},{4,6},{5,7},{6,4},{7,5},{8,10},{9,11},{10,... | collective-permute-start | bytes 1179656 | tf_op jit(solution)/shard_map/sums1/ppermute | solution.py:411
  119.6 0.7 collective-permute-start.28
  120.4 3.4 %collective-permute-done.18.refs_5_ = bf16[2,1,384,128]{3,2,1,0:T(8,128)(2,1)S(1)} collective-permute-done((bf16[2,1,384,128]{3,2,1,0:T(8,128)(2,1)S(1)}, bf16[2,1,384,128]{3,2,1,0:T(8,128)(2,1)S(1)}, u32[]{:S(2)}, u32[]{:S(2)}) %collective-permute-start.18) | collective-permute-done | bytes 196640 | tf_op jit(solution)/shard_map/far_back2/ppermute | solution.py:420
  123.8 1.1 collective-permute-start.19
  124.9 1.7 %collective-permute-start.21 = (bf16[2,1,384,128]{3,2,1,0:T(8,128)(2,1)S(1)}, bf16[2,1,384,128]{3,2,1,0:T(8,128)(2,1)S(1)}, u32[]{:S(2)}, u32[]{:S(2)}) collective-permute-start(bf16[2,1,384,128]{3,2,1,0:T(8,128)(2,1)S(1)} %get-tuple-element.107), channel_id=1, source_target_pairs={{0,3},{1,2},{2,1},{3,0},{4,7},{5,6},{6,5},{7,4},{8,11},{9,10},{10,... | collective-permute-start | bytes 589832 | tf_op jit(solution)/shard_map/sums2/ppermute | solution.py:411
  126.6 1.4 unpack.3
  128.4 10.0 %collective-permute-done.28.refs_3_.refs_7_ = bf16[2,2,384,128]{3,2,1,0:T(8,128)(2,1)S(1)} collective-permute-done((bf16[2,2,384,128]{3,2,1,0:T(8,128)(2,1)S(1)}, bf16[2,2,384,128]{3,2,1,0:T(8,128)(2,1)S(1)}, u32[]{:S(2)}, u32[]{:S(2)}) %collective-permute-start.28) | collective-permute-done | bytes 393248 | tf_op jit(solution)/shard_map/sums1/ppermute | solution.py:411
  138.4 1.4 unpack.4
  139.8 1.2 collective-permute-done.20.refs_2_.refs_6_
  141.0 4.9 %collective-permute-done.21.refs_3_.refs_7_ = bf16[2,1,384,128]{3,2,1,0:T(8,128)(2,1)S(1)} collective-permute-done((bf16[2,1,384,128]{3,2,1,0:T(8,128)(2,1)S(1)}, bf16[2,1,384,128]{3,2,1,0:T(8,128)(2,1)S(1)}, u32[]{:S(2)}, u32[]{:S(2)}) %collective-permute-start.21) | collective-permute-done | bytes 196640 | tf_op jit(solution)/shard_map/sums2/ppermute | solution.py:411
  145.9 1.1 unpack.5
  (68 shorter events, 3.0 us)
Async XLA Ops:
  3.8 15.5 %collective-permute-start = (bf16[2,2,400,128]{3,2,1,0:T(8,128)(2,1)}, bf16[2,2,400,128]{3,2,1,0:T(8,128)(2,1)S(1)}, u32[]{:S(2)}, u32[]{:S(2)}) collective-permute-start(bf16[2,2,400,128]{3,2,1,0:T(8,128)(2,1)} %get-tuple-element.70), channel_id=1, source_target_pairs={{0,2},{1,3},{2,0},{3,1},{4,6},{5,7},{6,4},{7,5},{8,10},{9,11},{10,... | collective-permute-start | bytes 1228808 | tf_op jit(solution)/shard_map/facing0/ppermute | solution.py:411
  5.8 19.5 %collective-permute-start.1 = (bf16[2,2,400,128]{3,2,1,0:T(8,128)(2,1)}, bf16[2,2,400,128]{3,2,1,0:T(8,128)(2,1)S(1)}, u32[]{:S(2)}, u32[]{:S(2)}) collective-permute-start(bf16[2,2,400,128]{3,2,1,0:T(8,128)(2,1)} %get-tuple-element.71.refs_8_), channel_id=1, source_target_pairs={{0,3},{1,2},{2,1},{3,0},{4,7},{5,6},{6,5},{7,4},{8,11},{9,10},{10,... | collective-permute-start | bytes 1228808 | tf_op jit(solution)/shard_map/crossing0/ppermute | solution.py:411
  9.6 17.1 %collective-permute-start.10 = (bf16[2,2,384,128]{3,2,1,0:T(8,128)(2,1)}, bf16[2,2,384,128]{3,2,1,0:T(8,128)(2,1)}, u32[]{:S(2)}, u32[]{:S(2)}) collective-permute-start(bf16[2,2,384,128]{3,2,1,0:T(8,128)(2,1)} %get-tuple-element.81.refs_4_), channel_id=1, source_target_pairs={{2,6},{3,7},{4,0},{5,1},{6,10},{7,11},{8,4},{9,5},{10,14},{11,15},... | collective-permute-start | bytes 1179656 | tf_op jit(solution)/shard_map/near0/ppermute | solution.py:420
  10.9 18.0 %collective-permute-start.2 = (bf16[2,2,400,128]{3,2,1,0:T(8,128)(2,1)}, bf16[2,2,400,128]{3,2,1,0:T(8,128)(2,1)S(1)}, u32[]{:S(2)}, u32[]{:S(2)}) collective-permute-start(bf16[2,2,400,128]{3,2,1,0:T(8,128)(2,1)} %get-tuple-element.72.refs_8_), channel_id=1, source_target_pairs={{0,1},{1,0},{2,3},{3,2},{4,5},{5,4},{6,7},{7,6},{8,9},{9,8},{10,11... | collective-permute-start | bytes 1228808 | tf_op jit(solution)/shard_map/partner0/ppermute | solution.py:411
  18.0 18.3 %collective-permute-start.8 = (bf16[2,3,384,128]{3,2,1,0:T(8,128)(2,1)}, bf16[2,3,384,128]{3,2,1,0:T(8,128)(2,1)S(1)}, u32[]{:S(2)}, u32[]{:S(2)}) collective-permute-start(bf16[2,3,384,128]{3,2,1,0:T(8,128)(2,1)} %get-tuple-element.79.refs_4_), channel_id=1, source_target_pairs={{2,6},{3,7},{4,0},{5,1},{6,10},{7,11},{8,4},{9,5},{10,14},{11,15},... | collective-permute-start | bytes 1769480 | tf_op jit(solution)/shard_map/near1/ppermute | solution.py:420
  19.3 0.8 copy-start
  20.1 7.1 %copy-start.1 = (bf16[2,2,400,128]{3,2,1,0:T(8,128)(2,1)S(1)}, bf16[2,2,400,128]{3,2,1,0:T(8,128)(2,1)}, u32[]{:S(2)}) copy-start(bf16[2,2,400,128]{3,2,1,0:T(8,128)(2,1)} %copy-done) | copy-start | bytes 1228804
  20.1 16.7 %collective-permute-start.4 = (bf16[2,2,384,128]{3,2,1,0:T(8,128)(2,1)}, bf16[2,2,384,128]{3,2,1,0:T(8,128)(2,1)S(1)}, u32[]{:S(2)}, u32[]{:S(2)}) collective-permute-start(bf16[2,2,384,128]{3,2,1,0:T(8,128)(2,1)} %follow.4), channel_id=1, source_target_pairs={{0,2},{1,3},{2,0},{3,1},{4,6},{5,7},{6,4},{7,5},{8,10},{9,11},{10,... | collective-permute-start | bytes 1179656 | tf_op jit(solution)/shard_map/facing1/ppermute | solution.py:411
  25.3 0.8 copy-start.2
  26.1 17.3 %collective-permute-start.6 = (bf16[2,2,384,128]{3,2,1,0:T(8,128)(2,1)}, bf16[2,2,384,128]{3,2,1,0:T(8,128)(2,1)S(1)}, u32[]{:S(2)}, u32[]{:S(2)}) collective-permute-start(bf16[2,2,384,128]{3,2,1,0:T(8,128)(2,1)} %follow.6), channel_id=1, source_target_pairs={{0,3},{1,2},{2,1},{3,0},{4,7},{5,6},{6,5},{7,4},{8,11},{9,10},{10,... | collective-permute-start | bytes 1179656 | tf_op jit(solution)/shard_map/crossing1/ppermute | solution.py:411
  26.7 20.2 %collective-permute-start.11 = (bf16[2,2,384,128]{3,2,1,0:T(8,128)(2,1)}, bf16[2,2,384,128]{3,2,1,0:T(8,128)(2,1)}, u32[]{:S(2)}, u32[]{:S(2)}) collective-permute-start(bf16[2,2,384,128]{3,2,1,0:T(8,128)(2,1)} %collective-permute-done.10.refs_8_), channel_id=1, source_target_pairs={{0,1},{1,0},{2,3},{3,2},{4,5},{5,4},{6,7},{7,6},{8,9},{9,8},{10,11... | collective-permute-start | bytes 1179656 | tf_op jit(solution)/shard_map/near_partner0/ppermute | solution.py:411
  27.2 1.0 copy-start.3
  28.9 19.0 %collective-permute-start.12 = (bf16[2,2,384,128]{3,2,1,0:T(8,128)(2,1)}, bf16[2,2,384,128]{3,2,1,0:T(8,128)(2,1)}, u32[]{:S(2)}, u32[]{:S(2)}) collective-permute-start(bf16[2,2,384,128]{3,2,1,0:T(8,128)(2,1)} %gather.3), channel_id=1, source_target_pairs={{0,4},{1,5},{4,8},{5,9},{6,2},{7,3},{8,12},{9,13},{10,6},{11,7},{1... | collective-permute-start | bytes 1179656 | tf_op jit(solution)/shard_map/far0/ppermute | solution.py:420
  32.9 2.8 %copy-start.4 = (bf16[2,2,400,128]{3,2,1,0:T(8,128)(2,1)S(1)}, bf16[2,2,400,128]{3,2,1,0:T(8,128)(2,1)}, u32[]{:S(2)}) copy-start(bf16[2,2,400,128]{3,2,1,0:T(8,128)(2,1)} %copy-done.2) | copy-start | bytes 1228804
  32.9 2.8 %copy-start.10 = (s32[3,8]{1,0:T(4,128)S(1)}, s32[3,8]{1,0:T(4,128)}, u32[]{:S(2)}) copy-start(s32[3,8]{1,0:T(4,128)} %lists.11) | copy-start | bytes 292
  32.9 2.8 %copy-start.11 = (s32[3]{0:T(128)S(1)}, s32[3]{0:T(128)}, u32[]{:S(2)}) copy-start(s32[3]{0:T(128)} %counts.11) | copy-start | bytes 40
  36.4 34.8 %collective-permute-start.3 = (bf16[2,3,384,128]{3,2,1,0:T(8,128)(2,1)}, bf16[2,3,384,128]{3,2,1,0:T(8,128)(2,1)S(1)}, u32[]{:S(2)}, u32[]{:S(2)}) collective-permute-start(bf16[2,3,384,128]{3,2,1,0:T(8,128)(2,1)} %get-tuple-element.75.refs_4_), channel_id=1, source_target_pairs={{0,1},{1,0},{2,3},{3,2},{4,5},{5,4},{6,7},{7,6},{8,9},{9,8},{10,11... | collective-permute-start | bytes 1769480 | tf_op jit(solution)/shard_map/partner1/ppermute | solution.py:411
  36.8 0.7 copy-start.5
  36.8 38.7 %collective-permute-start.9 = (bf16[2,3,384,128]{3,2,1,0:T(8,128)(2,1)S(1)}, bf16[2,3,384,128]{3,2,1,0:T(8,128)(2,1)S(1)}, u32[]{:S(2)}, u32[]{:S(2)}) collective-permute-start(bf16[2,3,384,128]{3,2,1,0:T(8,128)(2,1)S(1)} %collective-permute-done.8.refs_8_), channel_id=1, source_target_pairs={{0,1},{1,0},{2,3},{3,2},{4,5},{5,4},{6,7},{7,6},{8,9},{9,8},{10,11... | collective-permute-start | bytes 1769480 | tf_op jit(solution)/shard_map/near_partner1/ppermute | solution.py:411
  43.3 1.5 copy-start.7
  43.3 24.3 %collective-permute-start.5 = (bf16[2,1,384,128]{3,2,1,0:T(8,128)(2,1)}, bf16[2,1,384,128]{3,2,1,0:T(8,128)(2,1)S(1)}, u32[]{:S(2)}, u32[]{:S(2)}) collective-permute-start(bf16[2,1,384,128]{3,2,1,0:T(8,128)(2,1)} %follow.5), channel_id=1, source_target_pairs={{0,2},{1,3},{2,0},{3,1},{4,6},{5,7},{6,4},{7,5},{8,10},{9,11},{10,... | collective-permute-start | bytes 589832 | tf_op jit(solution)/shard_map/facing2/ppermute | solution.py:411
  44.8 1.0 copy-start.6
  45.8 1.0 copy-start.8
  46.8 0.9 copy-start.16
  46.8 4.3 %copy-start.13 = (bf16[2,2,384,128]{3,2,1,0:T(8,128)(2,1)S(1)}, bf16[2,2,384,128]{3,2,1,0:T(8,128)(2,1)}, u32[]{:S(2)}) copy-start(bf16[2,2,384,128]{3,2,1,0:T(8,128)(2,1)} %get-tuple-element.81.refs_4_) | copy-start | bytes 1179652
  46.8 4.4 %copy-start.14 = (bf16[1,2,384,128]{3,2,1,0:T(8,128)(2,1)S(1)}, bf16[1,2,384,128]{3,2,1,0:T(8,128)(2,1)}, u32[]{:S(2)}) copy-start(bf16[1,2,384,128]{3,2,1,0:T(8,128)(2,1)} %get-tuple-element.80.refs_0_) | copy-start | bytes 589828
  47.7 22.1 %collective-permute-start.7 = (bf16[2,1,384,128]{3,2,1,0:T(8,128)(2,1)S(1)}, bf16[2,1,384,128]{3,2,1,0:T(8,128)(2,1)S(1)}, u32[]{:S(2)}, u32[]{:S(2)}) collective-permute-start(bf16[2,1,384,128]{3,2,1,0:T(8,128)(2,1)S(1)} %copy-done.16), channel_id=1, source_target_pairs={{0,3},{1,2},{2,1},{3,0},{4,7},{5,6},{6,5},{7,4},{8,11},{9,10},{10,... | collective-permute-start | bytes 589832 | tf_op jit(solution)/shard_map/crossing2/ppermute | solution.py:411
  48.0 27.5 %collective-permute-start.14 = (bf16[2,2,384,128]{3,2,1,0:T(8,128)(2,1)S(1)}, bf16[2,2,384,128]{3,2,1,0:T(8,128)(2,1)S(1)}, u32[]{:S(2)}, u32[]{:S(2)}) collective-permute-start(bf16[2,2,384,128]{3,2,1,0:T(8,128)(2,1)S(1)} %gather.5), channel_id=1, source_target_pairs={{0,4},{1,5},{4,8},{5,9},{6,2},{7,3},{8,12},{9,13},{10,6},{11,7},{1... | collective-permute-start | bytes 1179656 | tf_op jit(solution)/shard_map/far1/ppermute | solution.py:420
  67.7 27.2 %collective-permute-start.15 = (bf16[2,2,384,128]{3,2,1,0:T(8,128)(2,1)S(1)}, bf16[2,2,384,128]{3,2,1,0:T(8,128)(2,1)S(1)}, u32[]{:S(2)}, u32[]{:S(2)}) collective-permute-start(bf16[2,2,384,128]{3,2,1,0:T(8,128)(2,1)S(1)} %get-tuple-element.87), channel_id=1, source_target_pairs={{0,4},{1,5},{4,8},{5,9},{6,2},{7,3},{8,12},{9,13},{10,6},{11,7},{1... | collective-permute-start | bytes 1179656 | tf_op jit(solution)/shard_map/near_back0/ppermute | solution.py:420
  69.8 25.1 %collective-permute-start.16 = (bf16[2,2,384,128]{3,2,1,0:T(8,128)(2,1)S(1)}, bf16[2,2,384,128]{3,2,1,0:T(8,128)(2,1)S(1)}, u32[]{:S(2)}, u32[]{:S(2)}) collective-permute-start(bf16[2,2,384,128]{3,2,1,0:T(8,128)(2,1)S(1)} %get-tuple-element.88), channel_id=1, source_target_pairs={{2,6},{3,7},{4,0},{5,1},{6,10},{7,11},{8,4},{9,5},{10,14},{11,15},... | collective-permute-start | bytes 1179656 | tf_op jit(solution)/shard_map/far_back0/ppermute | solution.py:420
  71.1 4.4 %copy-start.9 = (bf16[2,2,384,128]{3,2,1,0:T(8,128)(2,1)S(1)}, bf16[2,2,384,128]{3,2,1,0:T(8,128)(2,1)}, u32[]{:S(2)}) copy-start(bf16[2,2,384,128]{3,2,1,0:T(8,128)(2,1)} %copy-done.7) | copy-start | bytes 1179652
  71.1 4.4 %copy-start.12 = (bf16[2,3,384,128]{3,2,1,0:T(8,128)(2,1)S(1)}, bf16[2,3,384,128]{3,2,1,0:T(8,128)(2,1)}, u32[]{:S(2)}) copy-start(bf16[2,3,384,128]{3,2,1,0:T(8,128)(2,1)} %get-tuple-element.79.refs_4_) | copy-start | bytes 1769476
  71.1 4.4 %copy-start.15 = (bf16[1,3,384,128]{3,2,1,0:T(8,128)(2,1)S(1)}, bf16[1,3,384,128]{3,2,1,0:T(8,128)(2,1)}, u32[]{:S(2)}) copy-start(bf16[1,3,384,128]{3,2,1,0:T(8,128)(2,1)} %get-tuple-element.74.refs_0_) | copy-start | bytes 884740
  71.2 28.1 %collective-permute-start.13 = (bf16[2,1,384,128]{3,2,1,0:T(8,128)(2,1)S(1)}, bf16[2,1,384,128]{3,2,1,0:T(8,128)(2,1)S(1)}, u32[]{:S(2)}, u32[]{:S(2)}) collective-permute-start(bf16[2,1,384,128]{3,2,1,0:T(8,128)(2,1)S(1)} %gather.4), channel_id=1, source_target_pairs={{0,4},{1,5},{4,8},{5,9},{6,2},{7,3},{8,12},{9,13},{10,6},{11,7},{1... | collective-permute-start | bytes 589832 | tf_op jit(solution)/shard_map/far2/ppermute | solution.py:420
  91.0 20.5 %collective-permute-start.22 = (bf16[2,2,384,128]{3,2,1,0:T(8,128)(2,1)S(1)}, bf16[2,2,384,128]{3,2,1,0:T(8,128)(2,1)S(1)}, u32[]{:S(2)}, u32[]{:S(2)}) collective-permute-start(bf16[2,2,384,128]{3,2,1,0:T(8,128)(2,1)S(1)} %get-tuple-element.111), channel_id=1, source_target_pairs={{0,4},{1,5},{4,8},{5,9},{6,2},{7,3},{8,12},{9,13},{10,6},{11,7},{1... | collective-permute-start | bytes 1179656 | tf_op jit(solution)/shard_map/near_back1/ppermute | solution.py:420
  93.4 18.2 %collective-permute-start.23 = (bf16[2,2,384,128]{3,2,1,0:T(8,128)(2,1)S(1)}, bf16[2,2,384,128]{3,2,1,0:T(8,128)(2,1)S(1)}, u32[]{:S(2)}, u32[]{:S(2)}) collective-permute-start(bf16[2,2,384,128]{3,2,1,0:T(8,128)(2,1)S(1)} %get-tuple-element.112), channel_id=1, source_target_pairs={{2,6},{3,7},{4,0},{5,1},{6,10},{7,11},{8,4},{9,5},{10,14},{11,15},... | collective-permute-start | bytes 1179656 | tf_op jit(solution)/shard_map/far_back1/ppermute | solution.py:420
  95.2 16.4 %collective-permute-start.24 = (bf16[2,2,384,128]{3,2,1,0:T(8,128)(2,1)S(1)}, bf16[2,2,384,128]{3,2,1,0:T(8,128)(2,1)S(1)}, u32[]{:S(2)}, u32[]{:S(2)}) collective-permute-start(bf16[2,2,384,128]{3,2,1,0:T(8,128)(2,1)S(1)} %get-tuple-element.117), channel_id=1, source_target_pairs={{0,2},{1,3},{2,0},{3,1},{4,6},{5,7},{6,4},{7,5},{8,10},{9,11},{10,... | collective-permute-start | bytes 1179656 | tf_op jit(solution)/shard_map/sums0/ppermute | solution.py:411
  96.3 18.2 %collective-permute-start.25 = (bf16[2,2,384,128]{3,2,1,0:T(8,128)(2,1)S(1)}, bf16[2,2,384,128]{3,2,1,0:T(8,128)(2,1)S(1)}, u32[]{:S(2)}, u32[]{:S(2)}) collective-permute-start(bf16[2,2,384,128]{3,2,1,0:T(8,128)(2,1)S(1)} %get-tuple-element.118), channel_id=1, source_target_pairs={{0,3},{1,2},{2,1},{3,0},{4,7},{5,6},{6,5},{7,4},{8,11},{9,10},{10,... | collective-permute-start | bytes 1179656 | tf_op jit(solution)/shard_map/sums0/ppermute | solution.py:411
  107.2 12.4 %collective-permute-start.17 = (bf16[2,1,384,128]{3,2,1,0:T(8,128)(2,1)S(1)}, bf16[2,1,384,128]{3,2,1,0:T(8,128)(2,1)S(1)}, u32[]{:S(2)}, u32[]{:S(2)}) collective-permute-start(bf16[2,1,384,128]{3,2,1,0:T(8,128)(2,1)S(1)} %get-tuple-element.98), channel_id=1, source_target_pairs={{0,4},{1,5},{4,8},{5,9},{6,2},{7,3},{8,12},{9,13},{10,6},{11,7},{1... | collective-permute-start | bytes 589832 | tf_op jit(solution)/shard_map/near_back2/ppermute | solution.py:420
  111.5 13.4 %collective-permute-start.29 = (bf16[2,2,384,128]{3,2,1,0:T(8,128)(2,1)S(1)}, bf16[2,2,384,128]{3,2,1,0:T(8,128)(2,1)S(1)}, u32[]{:S(2)}, u32[]{:S(2)}) collective-permute-start(bf16[2,2,384,128]{3,2,1,0:T(8,128)(2,1)S(1)} %get-tuple-element.123), channel_id=1, source_target_pairs={{0,1},{1,0},{2,3},{3,2},{4,5},{5,4},{6,7},{7,6},{8,9},{9,8},{10,11... | collective-permute-start | bytes 1179656 | tf_op jit(solution)/shard_map/sums0/ppermute | solution.py:411
  114.8 10.1 %collective-permute-start.26 = (bf16[2,2,384,128]{3,2,1,0:T(8,128)(2,1)S(1)}, bf16[2,2,384,128]{3,2,1,0:T(8,128)(2,1)S(1)}, u32[]{:S(2)}, u32[]{:S(2)}) collective-permute-start(bf16[2,2,384,128]{3,2,1,0:T(8,128)(2,1)S(1)} %get-tuple-element.120), channel_id=1, source_target_pairs={{0,1},{1,0},{2,3},{3,2},{4,5},{5,4},{6,7},{7,6},{8,9},{9,8},{10,11... | collective-permute-start | bytes 1179656 | tf_op jit(solution)/shard_map/sums1/ppermute | solution.py:411
  114.9 8.8 %collective-permute-start.18 = (bf16[2,1,384,128]{3,2,1,0:T(8,128)(2,1)S(1)}, bf16[2,1,384,128]{3,2,1,0:T(8,128)(2,1)S(1)}, u32[]{:S(2)}, u32[]{:S(2)}) collective-permute-start(bf16[2,1,384,128]{3,2,1,0:T(8,128)(2,1)S(1)} %get-tuple-element.99), channel_id=1, source_target_pairs={{2,6},{3,7},{4,0},{5,1},{6,10},{7,11},{8,4},{9,5},{10,14},{11,15},... | collective-permute-start | bytes 589832 | tf_op jit(solution)/shard_map/far_back2/ppermute | solution.py:420
  116.2 12.2 %collective-permute-start.27 = (bf16[2,2,384,128]{3,2,1,0:T(8,128)(2,1)S(1)}, bf16[2,2,384,128]{3,2,1,0:T(8,128)(2,1)S(1)}, u32[]{:S(2)}, u32[]{:S(2)}) collective-permute-start(bf16[2,2,384,128]{3,2,1,0:T(8,128)(2,1)S(1)} %get-tuple-element.121), channel_id=1, source_target_pairs={{0,2},{1,3},{2,0},{3,1},{4,6},{5,7},{6,4},{7,5},{8,10},{9,11},{10,... | collective-permute-start | bytes 1179656 | tf_op jit(solution)/shard_map/sums1/ppermute | solution.py:411
  119.6 18.7 %collective-permute-start.28 = (bf16[2,2,384,128]{3,2,1,0:T(8,128)(2,1)S(1)}, bf16[2,2,384,128]{3,2,1,0:T(8,128)(2,1)S(1)}, u32[]{:S(2)}, u32[]{:S(2)}) collective-permute-start(bf16[2,2,384,128]{3,2,1,0:T(8,128)(2,1)S(1)} %get-tuple-element.122), channel_id=1, source_target_pairs={{0,3},{1,2},{2,1},{3,0},{4,7},{5,6},{6,5},{7,4},{8,11},{9,10},{10,... | collective-permute-start | bytes 1179656 | tf_op jit(solution)/shard_map/sums1/ppermute | solution.py:411
  123.8 16.0 %collective-permute-start.19 = (bf16[2,1,384,128]{3,2,1,0:T(8,128)(2,1)S(1)}, bf16[2,1,384,128]{3,2,1,0:T(8,128)(2,1)S(1)}, u32[]{:S(2)}, u32[]{:S(2)}) collective-permute-start(bf16[2,1,384,128]{3,2,1,0:T(8,128)(2,1)S(1)} %get-tuple-element.105), channel_id=1, source_target_pairs={{0,1},{1,0},{2,3},{3,2},{4,5},{5,4},{6,7},{7,6},{8,9},{9,8},{10,11... | collective-permute-start | bytes 589832 | tf_op jit(solution)/shard_map/sums2/ppermute | solution.py:411
  124.9 16.1 %collective-permute-start.20 = (bf16[2,1,384,128]{3,2,1,0:T(8,128)(2,1)S(1)}, bf16[2,1,384,128]{3,2,1,0:T(8,128)(2,1)S(1)}, u32[]{:S(2)}, u32[]{:S(2)}) collective-permute-start(bf16[2,1,384,128]{3,2,1,0:T(8,128)(2,1)S(1)} %get-tuple-element.106), channel_id=1, source_target_pairs={{0,2},{1,3},{2,0},{3,1},{4,6},{5,7},{6,4},{7,5},{8,10},{9,11},{10,... | collective-permute-start | bytes 589832 | tf_op jit(solution)/shard_map/sums2/ppermute | solution.py:411
  124.9 21.0 %collective-permute-start.21 = (bf16[2,1,384,128]{3,2,1,0:T(8,128)(2,1)S(1)}, bf16[2,1,384,128]{3,2,1,0:T(8,128)(2,1)S(1)}, u32[]{:S(2)}, u32[]{:S(2)}) collective-permute-start(bf16[2,1,384,128]{3,2,1,0:T(8,128)(2,1)S(1)} %get-tuple-element.107), channel_id=1, source_target_pairs={{0,3},{1,2},{2,1},{3,0},{4,7},{5,6},{6,5},{7,4},{8,11},{9,10},{10,... | collective-permute-start | bytes 589832 | tf_op jit(solution)/shard_map/sums2/ppermute | solution.py:411

commit v3 on v2

--- a/solution.py
+++ b/solution.py
@@ -16,9 +16,9 @@
 MIN_LIVE = 4
 QUAD = 4
 PIECES = 2 * QUAD
-INS = (2, 2, 1)
+INS = (2, 1, 2)
 OWNS = (2, 3)
-OUTS = ((2, False), (2, False), (1, False))
+OUTS = ((2, False), (1, False), (2, True))
 COSTS = {"pack": 1.0, "gather": 0.5, "attend": 8.0, "combine": 0.3, "unpack": 0.8}
 LOG2E = math.log2(math.e)
 PACK_VMEM = 60 * 1024 * 1024
@@ -116,14 +116,14 @@
     pass
 
 
-def follow(x, after):
+def follow(x, after, vmem=PACK_VMEM):
     return pl.pallas_call(
         follow_body,
         in_specs=[ANYWHERE] * 2,
         out_specs=ANYWHERE,
         out_shape=jax.ShapeDtypeStruct(x.shape, x.dtype),
         input_output_aliases={0: 0},
-        compiler_params=pltpu.CompilerParams(vmem_limit_bytes=PACK_VMEM),
+        compiler_params=pltpu.CompilerParams(vmem_limit_bytes=vmem),
         name="follow",
     )(x, after)
 
@@ -419,8 +419,12 @@
         with jax.named_scope(name):
             return lax.ppermute(x, "tm", route)
 
-    def all_ways(parts, name):
-        return [parts[0]] + [across(parts[flip], flip, name) for flip in (2, 3, 1)]
+    def both_ways(parts, name):
+        return [across(parts[flip], flip, name) for flip in (2, 3)]
+
+    def all_ways(parts, after, name):
+        far_parts = both_ways(parts, name)
+        return [parts[0]] + far_parts + [across(follow(parts[1], after, SMALL_VMEM), 1, name)]
 
     scalars = (shard.astype(jnp.int32).reshape(1), block_lists, list_counts)
     ins, owns = [], []
@@ -443,6 +447,7 @@
     plan = route(scalars, ins[0][1], ins[0][2], owns[0][2])
 
     outs, fars, pending, previous, behind, ahead, earlier = None, {}, None, [], [], [], []
+    arrived = []
     calls = list(enumerate(zip(started([heads for heads, _ in OUTS]), OUTS)))
     for n, call in calls + [(len(calls), None)]:
         waiting, pending = pending, None
@@ -454,7 +459,7 @@
             first = start - first
             later, facing, crossing = [i for i in ins if i[0] <= start][-1]
             if later not in fars:
-                gathered = gather(facing, crossing, rows, earlier)
+                gathered = gather(facing, crossing, rows, previous if n == 1 else earlier)
                 fars[later] = along(gathered, -1, f"far{len(fars)}")
             far = fars[later]
             later = start - later
@@ -465,9 +470,9 @@
             ]
             results, own, near_back, far_back = attend(plan, sources, heads, split, previous + behind)
             earlier, previous = previous, [own[0]]
+            near_back = along(near_back, -1, f"near_back{n}")
             if split:
-                results = all_ways(results, f"results{n}")
-            near_back = along(near_back, -1, f"near_back{n}")
+                results = all_ways(results, near_back, f"results{n}")
             far_back = along(far_back, 1, f"far_back{n}")
             pending = (n, start, heads, split, results, own, near_back, far_back)
         if waiting is None:
@@ -475,8 +480,13 @@
         m, start, heads, split, results, own, near_back, far_back = waiting
         sums = combine(own, near_back, far_back, [] if split else results, (previous if call else []) + ahead)
         behind = [sums[0]]
-        sums = all_ways(sums, f"sums{m}")
-        ahead = sums[1:3] if m < len(OUTS) - 2 else []
+        sent = both_ways(sums, f"sums{m}")
+        ahead = sent if m < len(OUTS) - 2 else []
+        arrived.append((start, heads, split, results, [sums[0]] + sent, sums[1]))
+    for m, (start, heads, split, results, sums, partner) in enumerate(arrived):
+        if m < len(arrived) - 1:
+            partner = follow(partner, previous[0], SMALL_VMEM)
+        sums = sums + [across(partner, 1, f"sums_partner{m}")]
         order = (0, 3, 1, 2)
         pieces = [(sums[k], 0, 0) for k in order]
         pieces += [(results[k], 0, 0) if split else (sums[k], 1, 0) for k in order]

time: 148 us -> 142 us (0.959)
  starting transfers between devices: 49.7 us -> 44.7 us
  local copies, waits for them, and re-layouts: 5.94 us -> 1.51 us
  waiting for transfers between devices: 28.6 us -> 32.3 us
    ppermute x11, waiting for transfers between devices: 3.38 us -> 12.5 us  [along(): return lax.ppermute(x, 'tm', route)]
    ppermute x19 -> x22, starting transfers between devices: 22.8 us -> 16.4 us  [across(): return lax.ppermute(x, 'tm', [(i, i ^ flip) for i in range(shards)])]
    ppermute x19 -> x22, waiting for transfers between devices: 25.2 us -> 19.9 us  [across(): return lax.ppermute(x, 'tm', [(i, i ^ flip) for i in range(shards)])]
    unnamed x34 -> x28, local copies, waits for them, and re-layouts: 5.94 us -> 1.51 us
  transfers between devices with their start and end apart: 30 -> 33, of which waited for: 7 -> 10; matrix products, arithmetic and copies ran while one was open for 0% -> 0% of each run, Pallas kernels for 39% -> 40%
where the time goes in v3:
time: 142 us; the launch traced here: 141 us
  Pallas kernels  61.8 us (44%)
  starting transfers between devices  44.7 us (31%)
  waiting for transfers between devices  32.3 us (23%)
  local copies, waits for them, and re-layouts  1.51 us (1%)
    pallas_call x3, Pallas kernels, attend(): pl.pallas_call(functools.partial(attend_body, blocks=blocks, after=len(af...  39.9 us
    ppermute x11, starting transfers between devices, along(): return lax.ppermute(x, 'tm', route)  28.2 us
    ppermute x22, waiting for transfers between devices, across(): return lax.ppermute(x, 'tm', [(i, i ^ flip) for i in range(shards)])  19.9 us
    ppermute x22, starting transfers between devices, across(): return lax.ppermute(x, 'tm', [(i, i ^ flip) for i in range(shards)])  16.4 us
    pallas_call x5, Pallas kernels, pack(): pl.pallas_call(functools.partial(pack_body, heads=heads, own=own, planned...  15.8 us
    ppermute x11, waiting for transfers between devices, along(): return lax.ppermute(x, 'tm', route)  12.5 us
    pallas_call x3, Pallas kernels, unpack(): pl.pallas_call(unpack_body, grid_spec=pltpu.PrefetchScalarGridSpec(num_sc...  3.94 us
  transfers between devices with their start and end apart: 33, of which 10 were waited for; matrix products, arithmetic and copies ran while one was open for 0% of the time, Pallas kernels for 40%

profile of v3, /device:TPU:1, one launch (start us, length us, event | category | flops | bytes accessed | tf_op | source)
XLA Modules:
  0.0 141.3 jit_solution(4776445611249872843)
XLA Ops:
  0.6 3.1 %pack.5 = (bf16[2,2,400,128]{3,2,1,0:T(8,128)(2,1)}, bf16[2,2,400,128]{3,2,1,0:T(8,128)(2,1)}) custom-call(s32[1]{0:T(128)} %bitcast.place, s32[3,8]{1,0:T(4,128)} %lists.11, s32[3]{0:T(128)} %counts.11, bf16[384,1280]{1,0:T(8,128)(2,1)} %refs_4_.7, bf16[384,1280]{1,0:T(8,128)(2,1)} %refs_5_.7, bf16[384,1280]{1,0:T(8,128)(2,1)} %refs_6_.7, ...), custom_call_target="tpu_custom_call" | custom-call | flops 2305999872 | tf_op jit(solution)/shard_map/pack/pallas_call | solution.py:100
  3.8 2.1 %collective-permute-start = (bf16[2,2,400,128]{3,2,1,0:T(8,128)(2,1)}, bf16[2,2,400,128]{3,2,1,0:T(8,128)(2,1)S(1)}, u32[]{:S(2)}, u32[]{:S(2)}) collective-permute-start(bf16[2,2,400,128]{3,2,1,0:T(8,128)(2,1)} %get-tuple-element.70), channel_id=1, source_target_pairs={{0,2},{1,3},{2,0},{3,1},{4,6},{5,7},{6,4},{7,5},{8,10},{9,11},{10,... | collective-permute-start | bytes 1228808 | tf_op jit(solution)/shard_map/facing0/ppermute | solution.py:411
  5.8 0.6 collective-permute-start.1
  6.4 3.2 %pack.6 = (bf16[2,2,384,128]{3,2,1,0:T(8,128)(2,1)}, bf16[2,2,400,128]{3,2,1,0:T(8,128)(2,1)}, bf16[1,2,384,128]{3,2,1,0:T(8,128)(2,1)}) custom-call(s32[1]{0:T(128)} %bitcast.place, s32[3,8]{1,0:T(4,128)} %lists.11, s32[3]{0:T(128)} %counts.11, bf16[384,1280]{1,0:T(8,128)(2,1)} %refs_4_.7, bf16[384,1280]{1,0:T(8,128)(2,1)} %refs_5_.7, ...), custom_call_target="tpu_custom_call" | custom-call | flops 2305999872 | tf_op jit(solution)/shard_map/pack/pallas_call | solution.py:100
  9.6 1.3 collective-permute-start.10
  10.9 0.4 collective-permute-start.2
  11.3 2.7 %pack.7 = (bf16[2,1,384,128]{3,2,1,0:T(8,128)(2,1)}, bf16[2,1,384,128]{3,2,1,0:T(8,128)(2,1)}) custom-call(s32[1]{0:T(128)} %bitcast.place, s32[3,8]{1,0:T(4,128)} %lists.11, s32[3]{0:T(128)} %counts.11, bf16[384,1280]{1,0:T(8,128)(2,1)} %refs_4_.7, bf16[384,1280]{1,0:T(8,128)(2,1)} %refs_5_.7, bf16[384,1280]{1,0:T(8,128)(2,1)} %refs_6_.7, ...), custom_call_target="tpu_custom_call" | custom-call | flops 1152999936 | tf_op jit(solution)/shard_map/pack/pallas_call | solution.py:100
  14.0 3.6 %pack.8 = (bf16[2,3,384,128]{3,2,1,0:T(8,128)(2,1)}, bf16[2,3,384,128]{3,2,1,0:T(8,128)(2,1)}, bf16[1,3,384,128]{3,2,1,0:T(8,128)(2,1)}) custom-call(s32[1]{0:T(128)} %bitcast.place, s32[3,8]{1,0:T(4,128)} %lists.11, s32[3]{0:T(128)} %counts.11, bf16[384,1280]{1,0:T(8,128)(2,1)} %refs_4_.7, bf16[384,1280]{1,0:T(8,128)(2,1)} %refs_5_.7, ...), custom_call_target="tpu_custom_call" | custom-call | flops 3459000064 | tf_op jit(solution)/shard_map/pack/pallas_call | solution.py:100
  17.6 1.3 collective-permute-start.8
  18.9 4.0 %collective-permute-done.10.refs_8_ = bf16[2,2,384,128]{3,2,1,0:T(8,128)(2,1)} collective-permute-done((bf16[2,2,384,128]{3,2,1,0:T(8,128)(2,1)}, bf16[2,2,384,128]{3,2,1,0:T(8,128)(2,1)}, u32[]{:S(2)}, u32[]{:S(2)}) %collective-permute-start.10) | collective-permute-done | bytes 393248 | tf_op jit(solution)/shard_map/near0/ppermute | solution.py:420
  22.8 0.8 collective-permute-start.11
  23.6 1.2 collective-permute-done.1.crossing_ref.refs_1_.refs_3_.refs_7_
  24.9 0.8 gather.3
  25.7 4.2 %collective-permute-start.12 = (bf16[2,2,384,128]{3,2,1,0:T(8,128)(2,1)}, bf16[2,2,384,128]{3,2,1,0:T(8,128)(2,1)}, u32[]{:S(2)}, u32[]{:S(2)}) collective-permute-start(bf16[2,2,384,128]{3,2,1,0:T(8,128)(2,1)} %gather.3), channel_id=1, source_target_pairs={{0,4},{1,5},{4,8},{5,9},{6,2},{7,3},{8,12},{9,13},{10,6},{11,7},{1... | collective-permute-start | bytes 1179656 | tf_op jit(solution)/shard_map/far0/ppermute | solution.py:420
  29.9 1.4 %collective-permute-start.6 = (bf16[2,1,384,128]{3,2,1,0:T(8,128)(2,1)}, bf16[2,1,384,128]{3,2,1,0:T(8,128)(2,1)S(1)}, u32[]{:S(2)}, u32[]{:S(2)}) collective-permute-start(bf16[2,1,384,128]{3,2,1,0:T(8,128)(2,1)} %follow.9), channel_id=1, source_target_pairs={{0,3},{1,2},{2,1},{3,0},{4,7},{5,6},{6,5},{7,4},{8,11},{9,10},{10,... | collective-permute-start | bytes 589832 | tf_op jit(solution)/shard_map/crossing1/ppermute | solution.py:411
  31.4 3.3 %pack.9 = (bf16[2,2,384,128]{3,2,1,0:T(8,128)(2,1)}, bf16[2,2,384,128]{3,2,1,0:T(8,128)(2,1)}) custom-call(s32[1]{0:T(128)} %bitcast.place, s32[3,8]{1,0:T(4,128)} %lists.11, s32[3]{0:T(128)} %counts.11, bf16[384,1280]{1,0:T(8,128)(2,1)} %refs_4_.7, bf16[384,1280]{1,0:T(8,128)(2,1)} %refs_5_.7, bf16[384,1280]{1,0:T(8,128)(2,1)} %refs_6_.7, ...), custom_call_target="tpu_custom_call" | custom-call | flops 2305999872 | tf_op jit(solution)/shard_map/pack/pallas_call | solution.py:100
  34.7 0.6 route.1.plan
  35.6 0.7 collective-permute-start.3
  36.3 4.7 %collective-permute-done.6.refs_1_.crossing_ref.refs_3_.refs_7_ = bf16[2,1,384,128]{3,2,1,0:T(8,128)(2,1)S(1)} collective-permute-done((bf16[2,1,384,128]{3,2,1,0:T(8,128)(2,1)}, bf16[2,1,384,128]{3,2,1,0:T(8,128)(2,1)S(1)}, u32[]{:S(2)}, u32[]{:S(2)}) %collective-permute-start.6) | collective-permute-done | bytes 196640 | tf_op jit(solution)/shard_map/crossing1/ppermute | solution.py:411
  41.7 0.6 collective-permute-start.7
  42.4 1.2 collective-permute-start.5
  43.5 1.0 copy-done.11
  44.5 16.5 %attend.3 = (bf16[2,2,384,128]{3,2,1,0:T(8,128)(2,1)S(1)}, bf16[2,2,384,128]{3,2,1,0:T(8,128)(2,1)S(1)}, bf16[2,2,384,128]{3,2,1,0:T(8,128)(2,1)S(1)}, bf16[2,2,...) custom-call(s32[8,128]{1,0:T(8,128)S(1)} %route.1.plan, ...), custom_call_target="tpu_custom_call" | custom-call | flops 18447998976 | tf_op jit(solution)/shard_map/attend/pallas_call | solution.py:347
  61.1 2.5 %collective-permute-start.14 = (bf16[2,1,384,128]{3,2,1,0:T(8,128)(2,1)S(1)}, bf16[2,1,384,128]{3,2,1,0:T(8,128)(2,1)S(1)}, u32[]{:S(2)}, u32[]{:S(2)}) collective-permute-start(bf16[2,1,384,128]{3,2,1,0:T(8,128)(2,1)S(1)} %gather.5), channel_id=1, source_target_pairs={{0,4},{1,5},{4,8},{5,9},{6,2},{7,3},{8,12},{9,13},{10,6},{11,7},{1... | collective-permute-start | bytes 589832 | tf_op jit(solution)/shard_map/far1/ppermute | solution.py:420
  63.7 2.7 %collective-permute-start.15 = (bf16[2,2,384,128]{3,2,1,0:T(8,128)(2,1)S(1)}, bf16[2,2,384,128]{3,2,1,0:T(8,128)(2,1)S(1)}, u32[]{:S(2)}, u32[]{:S(2)}) collective-permute-start(bf16[2,2,384,128]{3,2,1,0:T(8,128)(2,1)S(1)} %get-tuple-element.87), channel_id=1, source_target_pairs={{0,4},{1,5},{4,8},{5,9},{6,2},{7,3},{8,12},{9,13},{10,6},{11,7},{1... | collective-permute-start | bytes 1179656 | tf_op jit(solution)/shard_map/near_back0/ppermute | solution.py:420
  66.4 1.4 %collective-permute-start.16 = (bf16[2,2,384,128]{3,2,1,0:T(8,128)(2,1)S(1)}, bf16[2,2,384,128]{3,2,1,0:T(8,128)(2,1)S(1)}, u32[]{:S(2)}, u32[]{:S(2)}) collective-permute-start(bf16[2,2,384,128]{3,2,1,0:T(8,128)(2,1)S(1)} %get-tuple-element.88), channel_id=1, source_target_pairs={{2,6},{3,7},{4,0},{5,1},{6,10},{7,11},{8,4},{9,5},{10,14},{11,15},... | collective-permute-start | bytes 1179656 | tf_op jit(solution)/shard_map/far_back0/ppermute | solution.py:420
  68.0 4.4 %collective-permute-start.13 = (bf16[2,2,384,128]{3,2,1,0:T(8,128)(2,1)S(1)}, bf16[2,2,384,128]{3,2,1,0:T(8,128)(2,1)S(1)}, u32[]{:S(2)}, u32[]{:S(2)}) collective-permute-start(bf16[2,2,384,128]{3,2,1,0:T(8,128)(2,1)S(1)} %gather.4), channel_id=1, source_target_pairs={{0,4},{1,5},{4,8},{5,9},{6,2},{7,3},{8,12},{9,13},{10,6},{11,7},{1... | collective-permute-start | bytes 1179656 | tf_op jit(solution)/shard_map/far2/ppermute | solution.py:420
  72.4 8.0 %attend.4 = (bf16[2,1,384,128]{3,2,1,0:T(8,128)(2,1)S(1)}, bf16[2,1,384,128]{3,2,1,0:T(8,128)(2,1)S(1)}, bf16[2,1,384,128]{3,2,1,0:T(8,128)(2,1)S(1)}, bf16[2,1,...) custom-call(s32[8,128]{1,0:T(8,128)S(1)} %route.1.plan, ...), custom_call_target="tpu_custom_call" | custom-call | flops 9223999488 | tf_op jit(solution)/shard_map/attend/pallas_call | solution.py:347
  80.4 3.4 %collective-permute-start.25 = (bf16[2,1,384,128]{3,2,1,0:T(8,128)(2,1)S(1)}, bf16[2,1,384,128]{3,2,1,0:T(8,128)(2,1)S(1)}, u32[]{:S(2)}, u32[]{:S(2)}) collective-permute-start(bf16[2,1,384,128]{3,2,1,0:T(8,128)(2,1)S(1)} %get-tuple-element.111), channel_id=1, source_target_pairs={{0,4},{1,5},{4,8},{5,9},{6,2},{7,3},{8,12},{9,13},{10,6},{11,7},{1... | collective-permute-start | bytes 589832 | tf_op jit(solution)/shard_map/near_back1/ppermute | solution.py:420
  83.7 1.5 %collective-permute-start.26 = (bf16[2,1,384,128]{3,2,1,0:T(8,128)(2,1)S(1)}, bf16[2,1,384,128]{3,2,1,0:T(8,128)(2,1)S(1)}, u32[]{:S(2)}, u32[]{:S(2)}) collective-permute-start(bf16[2,1,384,128]{3,2,1,0:T(8,128)(2,1)S(1)} %get-tuple-element.112), channel_id=1, source_target_pairs={{2,6},{3,7},{4,0},{5,1},{6,10},{7,11},{8,4},{9,5},{10,14},{11,15},... | collective-permute-start | bytes 589832 | tf_op jit(solution)/shard_map/far_back1/ppermute | solution.py:420
  85.6 3.2 %collective-permute-start.28 = (bf16[2,2,384,128]{3,2,1,0:T(8,128)(2,1)S(1)}, bf16[2,2,384,128]{3,2,1,0:T(8,128)(2,1)S(1)}, u32[]{:S(2)}, u32[]{:S(2)}) collective-permute-start(bf16[2,2,384,128]{3,2,1,0:T(8,128)(2,1)S(1)} %get-tuple-element.118), channel_id=1, source_target_pairs={{0,3},{1,2},{2,1},{3,0},{4,7},{5,6},{6,5},{7,4},{8,11},{9,10},{10,... | collective-permute-start | bytes 1179656 | tf_op jit(solution)/shard_map/sums0/ppermute | solution.py:411
  88.8 15.5 %attend.5 = (bf16[1,2,384,128]{3,2,1,0:T(8,128)(2,1)S(1)}, bf16[1,2,384,128]{3,2,1,0:T(8,128)(2,1)S(1)}, bf16[1,2,384,128]{3,2,1,0:T(8,128)(2,1)S(1)}, bf16[1,2,...) custom-call(s32[8,128]{1,0:T(8,128)S(1)} %route.1.plan, ...), custom_call_target="tpu_custom_call" | custom-call | flops 18447998976 | tf_op jit(solution)/shard_map/attend/pallas_call | solution.py:347
  104.3 4.3 %collective-permute-start.17 = (bf16[2,2,384,128]{3,2,1,0:T(8,128)(2,1)S(1)}, bf16[2,2,384,128]{3,2,1,0:T(8,128)(2,1)S(1)}, u32[]{:S(2)}, u32[]{:S(2)}) collective-permute-start(bf16[2,2,384,128]{3,2,1,0:T(8,128)(2,1)S(1)} %get-tuple-element.98), channel_id=1, source_target_pairs={{0,4},{1,5},{4,8},{5,9},{6,2},{7,3},{8,12},{9,13},{10,6},{11,7},{1... | collective-permute-start | bytes 1179656 | tf_op jit(solution)/shard_map/near_back2/ppermute | solution.py:420
  108.6 1.3 collective-permute-start.18
  110.0 1.0 collective-permute-start.23
  111.1 0.4 collective-permute-start.29
  111.5 4.9 %collective-permute-done.17.refs_4_.refs_1_ = bf16[2,2,384,128]{3,2,1,0:T(8,128)(2,1)S(1)} collective-permute-done((bf16[2,2,384,128]{3,2,1,0:T(8,128)(2,1)S(1)}, bf16[2,2,384,128]{3,2,1,0:T(8,128)(2,1)S(1)}, u32[]{:S(2)}, u32[]{:S(2)}) %collective-permute-start.17) | collective-permute-done | bytes 393248 | tf_op jit(solution)/shard_map/near_back2/ppermute | solution.py:420
  116.4 1.2 collective-permute-start.30
  117.6 3.3 %collective-permute-done.18.refs_5_ = bf16[2,2,384,128]{3,2,1,0:T(8,128)(2,1)S(1)} collective-permute-done((bf16[2,2,384,128]{3,2,1,0:T(8,128)(2,1)S(1)}, bf16[2,2,384,128]{3,2,1,0:T(8,128)(2,1)S(1)}, u32[]{:S(2)}, u32[]{:S(2)}) %collective-permute-start.18) | collective-permute-done | bytes 393248 | tf_op jit(solution)/shard_map/far_back2/ppermute | solution.py:420
  121.1 1.8 %collective-permute-start.24 = (bf16[1,2,384,128]{3,2,1,0:T(8,128)(2,1)S(1)}, bf16[1,2,384,128]{3,2,1,0:T(8,128)(2,1)S(1)}, u32[]{:S(2)}, u32[]{:S(2)}) collective-permute-start(bf16[1,2,384,128]{3,2,1,0:T(8,128)(2,1)S(1)} %get-tuple-element.107), channel_id=1, source_target_pairs={{0,3},{1,2},{2,1},{3,0},{4,7},{5,6},{6,5},{7,4},{8,11},{9,10},{10,... | collective-permute-start | bytes 589832 | tf_op jit(solution)/shard_map/results2/ppermute | solution.py:411
  122.9 0.5 collective-permute-start.19
  123.4 4.9 %collective-permute-done.31.refs_3_.refs_7_ = bf16[2,1,384,128]{3,2,1,0:T(8,128)(2,1)S(1)} collective-permute-done((bf16[2,1,384,128]{3,2,1,0:T(8,128)(2,1)S(1)}, bf16[2,1,384,128]{3,2,1,0:T(8,128)(2,1)S(1)}, u32[]{:S(2)}, u32[]{:S(2)}) %collective-permute-start.31) | collective-permute-done | bytes 196640 | tf_op jit(solution)/shard_map/sums1/ppermute | solution.py:411
  128.3 1.4 %unpack.3 = (bf16[384,1280]{1,0:T(8,128)(2,1)}, bf16[384,1280]{1,0:T(8,128)(2,1)}, bf16[384,1280]{1,0:T(8,128)(2,1)}, bf16[384,1280]{1,0:T(8,128)(2,1)}) custom-call(s32[1]{0:T(128)} %bitcast.place, bf16[2,2,384,128]{3,2,1,0:T(8,128)(2,1)S(1)} %get-tuple-element.93.refs_13_.refs_0_.refs_4_, ...), custom_call_target="tpu_custom_call" | custom-call | flops 1844800000 | tf_op jit(solution)/shard_map/unpack/pallas_call | solution.py:195
  129.7 1.1 unpack.4
  130.8 1.4 %collective-permute-done.24.refs_7_ = bf16[1,2,384,128]{3,2,1,0:T(8,128)(2,1)S(1)} collective-permute-done((bf16[1,2,384,128]{3,2,1,0:T(8,128)(2,1)S(1)}, bf16[1,2,384,128]{3,2,1,0:T(8,128)(2,1)S(1)}, u32[]{:S(2)}, u32[]{:S(2)}) %collective-permute-start.24) | collective-permute-done | bytes 196640 | tf_op jit(solution)/shard_map/results2/ppermute | solution.py:411
  132.2 2.9 %collective-permute-done.20.refs_2_ = bf16[1,2,384,128]{3,2,1,0:T(8,128)(2,1)S(1)} collective-permute-done((bf16[1,2,384,128]{3,2,1,0:T(8,128)(2,1)S(1)}, bf16[1,2,384,128]{3,2,1,0:T(8,128)(2,1)S(1)}, u32[]{:S(2)}, u32[]{:S(2)}) %collective-permute-start.20) | collective-permute-done | bytes 196640 | tf_op jit(solution)/shard_map/sums2/ppermute | solution.py:411
  135.2 4.7 %collective-permute-done.21.refs_3_ = bf16[1,2,384,128]{3,2,1,0:T(8,128)(2,1)S(1)} collective-permute-done((bf16[1,2,384,128]{3,2,1,0:T(8,128)(2,1)S(1)}, bf16[1,2,384,128]{3,2,1,0:T(8,128)(2,1)S(1)}, u32[]{:S(2)}, u32[]{:S(2)}) %collective-permute-start.21) | collective-permute-done | bytes 196640 | tf_op jit(solution)/shard_map/sums2/ppermute | solution.py:411
  139.9 1.4 %unpack.5 = (bf16[384,1280]{1,0:T(8,128)(2,1)}, bf16[384,1280]{1,0:T(8,128)(2,1)}, bf16[384,1280]{1,0:T(8,128)(2,1)}, bf16[384,1280]{1,0:T(8,128)(2,1)}) custom-call(s32[1]{0:T(128)} %bitcast.place, bf16[1,2,384,128]{3,2,1,0:T(8,128)(2,1)S(1)} %get-tuple-element.100.refs_0_, ...), custom_call_target="tpu_custom_call", output_to_operand_aliasing={{0}: (9, {}), {1}: (10, {}), {2}: (11, {}), {3}: (12, {})} | custom-call | flops 1844800000 | tf_op jit(solution)/shard_map/unpack/pallas_call | solution.py:195
  (71 shorter events, 2.2 us)
Async XLA Ops:
  3.8 19.9 %collective-permute-start = (bf16[2,2,400,128]{3,2,1,0:T(8,128)(2,1)}, bf16[2,2,400,128]{3,2,1,0:T(8,128)(2,1)S(1)}, u32[]{:S(2)}, u32[]{:S(2)}) collective-permute-start(bf16[2,2,400,128]{3,2,1,0:T(8,128)(2,1)} %get-tuple-element.70), channel_id=1, source_target_pairs={{0,2},{1,3},{2,0},{3,1},{4,6},{5,7},{6,4},{7,5},{8,10},{9,11},{10,... | collective-permute-start | bytes 1228808 | tf_op jit(solution)/shard_map/facing0/ppermute | solution.py:411
  5.8 19.0 %collective-permute-start.1 = (bf16[2,2,400,128]{3,2,1,0:T(8,128)(2,1)}, bf16[2,2,400,128]{3,2,1,0:T(8,128)(2,1)S(1)}, u32[]{:S(2)}, u32[]{:S(2)}) collective-permute-start(bf16[2,2,400,128]{3,2,1,0:T(8,128)(2,1)} %get-tuple-element.71.refs_8_), channel_id=1, source_target_pairs={{0,3},{1,2},{2,1},{3,0},{4,7},{5,6},{6,5},{7,4},{8,11},{9,10},{10,... | collective-permute-start | bytes 1228808 | tf_op jit(solution)/shard_map/crossing0/ppermute | solution.py:411
  9.6 13.2 %collective-permute-start.10 = (bf16[2,2,384,128]{3,2,1,0:T(8,128)(2,1)}, bf16[2,2,384,128]{3,2,1,0:T(8,128)(2,1)}, u32[]{:S(2)}, u32[]{:S(2)}) collective-permute-start(bf16[2,2,384,128]{3,2,1,0:T(8,128)(2,1)} %get-tuple-element.81.refs_4_), channel_id=1, source_target_pairs={{2,6},{3,7},{4,0},{5,1},{6,10},{7,11},{8,4},{9,5},{10,14},{11,15},... | collective-permute-start | bytes 1179656 | tf_op jit(solution)/shard_map/near0/ppermute | solution.py:420
  10.9 19.0 %collective-permute-start.2 = (bf16[2,2,400,128]{3,2,1,0:T(8,128)(2,1)}, bf16[2,2,400,128]{3,2,1,0:T(8,128)(2,1)S(1)}, u32[]{:S(2)}, u32[]{:S(2)}) collective-permute-start(bf16[2,2,400,128]{3,2,1,0:T(8,128)(2,1)} %get-tuple-element.72.refs_4_), channel_id=1, source_target_pairs={{0,1},{1,0},{2,3},{3,2},{4,5},{5,4},{6,7},{7,6},{8,9},{9,8},{10,11... | collective-permute-start | bytes 1228808 | tf_op jit(solution)/shard_map/partner0/ppermute | solution.py:411
  17.6 18.1 %collective-permute-start.8 = (bf16[2,3,384,128]{3,2,1,0:T(8,128)(2,1)}, bf16[2,3,384,128]{3,2,1,0:T(8,128)(2,1)S(1)}, u32[]{:S(2)}, u32[]{:S(2)}) collective-permute-start(bf16[2,3,384,128]{3,2,1,0:T(8,128)(2,1)} %get-tuple-element.79.refs_4_), channel_id=1, source_target_pairs={{2,6},{3,7},{4,0},{5,1},{6,10},{7,11},{8,4},{9,5},{10,14},{11,15},... | collective-permute-start | bytes 1769480 | tf_op jit(solution)/shard_map/near1/ppermute | solution.py:420
  22.8 19.5 %collective-permute-start.11 = (bf16[2,2,384,128]{3,2,1,0:T(8,128)(2,1)}, bf16[2,2,384,128]{3,2,1,0:T(8,128)(2,1)}, u32[]{:S(2)}, u32[]{:S(2)}) collective-permute-start(bf16[2,2,384,128]{3,2,1,0:T(8,128)(2,1)} %collective-permute-done.10.refs_8_), channel_id=1, source_target_pairs={{0,1},{1,0},{2,3},{3,2},{4,5},{5,4},{6,7},{7,6},{8,9},{9,8},{10,11... | collective-permute-start | bytes 1179656 | tf_op jit(solution)/shard_map/near_partner0/ppermute | solution.py:411
  23.6 2.0 %copy-start = (bf16[2,2,400,128]{3,2,1,0:T(8,128)(2,1)}, bf16[2,2,400,128]{3,2,1,0:T(8,128)(2,1)S(1)}, u32[]{:S(2)}) copy-start(bf16[2,2,400,128]{3,2,1,0:T(8,128)(2,1)S(1)} %collective-permute-done.facing_ref.refs_1_.refs_2_.refs_6_) | copy-start | bytes 1228804
  24.9 0.9 copy-start.2
  25.7 17.8 %collective-permute-start.12 = (bf16[2,2,384,128]{3,2,1,0:T(8,128)(2,1)}, bf16[2,2,384,128]{3,2,1,0:T(8,128)(2,1)}, u32[]{:S(2)}, u32[]{:S(2)}) collective-permute-start(bf16[2,2,384,128]{3,2,1,0:T(8,128)(2,1)} %gather.3), channel_id=1, source_target_pairs={{0,4},{1,5},{4,8},{5,9},{6,2},{7,3},{8,12},{9,13},{10,6},{11,7},{1... | collective-permute-start | bytes 1179656 | tf_op jit(solution)/shard_map/far0/ppermute | solution.py:420
  29.9 11.7 %collective-permute-start.4 = (bf16[2,1,384,128]{3,2,1,0:T(8,128)(2,1)}, bf16[2,1,384,128]{3,2,1,0:T(8,128)(2,1)S(1)}, u32[]{:S(2)}, u32[]{:S(2)}) collective-permute-start(bf16[2,1,384,128]{3,2,1,0:T(8,128)(2,1)} %follow.7), channel_id=1, source_target_pairs={{0,2},{1,3},{2,0},{3,1},{4,6},{5,7},{6,4},{7,5},{8,10},{9,11},{10,... | collective-permute-start | bytes 589832 | tf_op jit(solution)/shard_map/facing1/ppermute | solution.py:411
  29.9 11.1 %collective-permute-start.6 = (bf16[2,1,384,128]{3,2,1,0:T(8,128)(2,1)}, bf16[2,1,384,128]{3,2,1,0:T(8,128)(2,1)S(1)}, u32[]{:S(2)}, u32[]{:S(2)}) collective-permute-start(bf16[2,1,384,128]{3,2,1,0:T(8,128)(2,1)} %follow.9), channel_id=1, source_target_pairs={{0,3},{1,2},{2,1},{3,0},{4,7},{5,6},{6,5},{7,4},{8,11},{9,10},{10,... | collective-permute-start | bytes 589832 | tf_op jit(solution)/shard_map/crossing1/ppermute | solution.py:411
  31.4 3.3 %copy-start.1 = (bf16[2,2,400,128]{3,2,1,0:T(8,128)(2,1)S(1)}, bf16[2,2,400,128]{3,2,1,0:T(8,128)(2,1)}, u32[]{:S(2)}) copy-start(bf16[2,2,400,128]{3,2,1,0:T(8,128)(2,1)} %copy-done) | copy-start | bytes 1228804
  31.4 3.3 %copy-start.3 = (bf16[2,2,400,128]{3,2,1,0:T(8,128)(2,1)S(1)}, bf16[2,2,400,128]{3,2,1,0:T(8,128)(2,1)}, u32[]{:S(2)}) copy-start(bf16[2,2,400,128]{3,2,1,0:T(8,128)(2,1)} %copy-done.2) | copy-start | bytes 1228804
  31.4 3.3 %copy-start.8 = (s32[3,8]{1,0:T(4,128)S(1)}, s32[3,8]{1,0:T(4,128)}, u32[]{:S(2)}) copy-start(s32[3,8]{1,0:T(4,128)} %lists.11) | copy-start | bytes 292
  31.4 3.3 %copy-start.9 = (s32[3]{0:T(128)S(1)}, s32[3]{0:T(128)}, u32[]{:S(2)}) copy-start(s32[3]{0:T(128)} %counts.11) | copy-start | bytes 40
  35.6 32.3 %collective-permute-start.3 = (bf16[2,3,384,128]{3,2,1,0:T(8,128)(2,1)}, bf16[2,3,384,128]{3,2,1,0:T(8,128)(2,1)S(1)}, u32[]{:S(2)}, u32[]{:S(2)}) collective-permute-start(bf16[2,3,384,128]{3,2,1,0:T(8,128)(2,1)} %get-tuple-element.75.refs_8_), channel_id=1, source_target_pairs={{0,1},{1,0},{2,3},{3,2},{4,5},{5,4},{6,7},{7,6},{8,9},{9,8},{10,11... | collective-permute-start | bytes 1769480 | tf_op jit(solution)/shard_map/partner1/ppermute | solution.py:411
  41.0 0.7 copy-start.6
  41.0 31.4 %collective-permute-start.9 = (bf16[2,3,384,128]{3,2,1,0:T(8,128)(2,1)S(1)}, bf16[2,3,384,128]{3,2,1,0:T(8,128)(2,1)S(1)}, u32[]{:S(2)}, u32[]{:S(2)}) collective-permute-start(bf16[2,3,384,128]{3,2,1,0:T(8,128)(2,1)S(1)} %collective-permute-done.8.refs_8_), channel_id=1, source_target_pairs={{0,1},{1,0},{2,3},{3,2},{4,5},{5,4},{6,7},{7,6},{8,9},{9,8},{10,11... | collective-permute-start | bytes 1769480 | tf_op jit(solution)/shard_map/near_partner1/ppermute | solution.py:411
  41.7 0.7 copy-start.4
  41.7 22.0 %collective-permute-start.7 = (bf16[2,2,384,128]{3,2,1,0:T(8,128)(2,1)}, bf16[2,2,384,128]{3,2,1,0:T(8,128)(2,1)S(1)}, u32[]{:S(2)}, u32[]{:S(2)}) collective-permute-start(bf16[2,2,384,128]{3,2,1,0:T(8,128)(2,1)} %follow.10), channel_id=1, source_target_pairs={{0,3},{1,2},{2,1},{3,0},{4,7},{5,6},{6,5},{7,4},{8,11},{9,10},{10,... | collective-permute-start | bytes 1179656 | tf_op jit(solution)/shard_map/crossing2/ppermute | solution.py:411
  42.4 1.2 copy-start.12
  42.4 24.0 %collective-permute-start.5 = (bf16[2,2,384,128]{3,2,1,0:T(8,128)(2,1)}, bf16[2,2,384,128]{3,2,1,0:T(8,128)(2,1)S(1)}, u32[]{:S(2)}, u32[]{:S(2)}) collective-permute-start(bf16[2,2,384,128]{3,2,1,0:T(8,128)(2,1)} %follow.8), channel_id=1, source_target_pairs={{0,2},{1,3},{2,0},{3,1},{4,6},{5,7},{6,4},{7,5},{8,10},{9,11},{10,... | collective-permute-start | bytes 1179656 | tf_op jit(solution)/shard_map/facing2/ppermute | solution.py:411
  43.5 1.0 copy-start.11
  44.5 16.5 %copy-start.5 = (bf16[2,1,384,128]{3,2,1,0:T(8,128)(2,1)S(1)}, bf16[2,1,384,128]{3,2,1,0:T(8,128)(2,1)}, u32[]{:S(2)}) copy-start(bf16[2,1,384,128]{3,2,1,0:T(8,128)(2,1)} %copy-done.4) | copy-start | bytes 589828
  44.5 16.5 %copy-start.7 = (bf16[2,1,384,128]{3,2,1,0:T(8,128)(2,1)S(1)}, bf16[2,1,384,128]{3,2,1,0:T(8,128)(2,1)}, u32[]{:S(2)}) copy-start(bf16[2,1,384,128]{3,2,1,0:T(8,128)(2,1)} %copy-done.6) | copy-start | bytes 589828
  61.1 11.3 %collective-permute-start.14 = (bf16[2,1,384,128]{3,2,1,0:T(8,128)(2,1)S(1)}, bf16[2,1,384,128]{3,2,1,0:T(8,128)(2,1)S(1)}, u32[]{:S(2)}, u32[]{:S(2)}) collective-permute-start(bf16[2,1,384,128]{3,2,1,0:T(8,128)(2,1)S(1)} %gather.5), channel_id=1, source_target_pairs={{0,4},{1,5},{4,8},{5,9},{6,2},{7,3},{8,12},{9,13},{10,6},{11,7},{1... | collective-permute-start | bytes 589832 | tf_op jit(solution)/shard_map/far1/ppermute | solution.py:420
  63.7 21.6 %collective-permute-start.15 = (bf16[2,2,384,128]{3,2,1,0:T(8,128)(2,1)S(1)}, bf16[2,2,384,128]{3,2,1,0:T(8,128)(2,1)S(1)}, u32[]{:S(2)}, u32[]{:S(2)}) collective-permute-start(bf16[2,2,384,128]{3,2,1,0:T(8,128)(2,1)S(1)} %get-tuple-element.87), channel_id=1, source_target_pairs={{0,4},{1,5},{4,8},{5,9},{6,2},{7,3},{8,12},{9,13},{10,6},{11,7},{1... | collective-permute-start | bytes 1179656 | tf_op jit(solution)/shard_map/near_back0/ppermute | solution.py:420
  66.4 6.0 %copy-start.10 = (bf16[2,3,384,128]{3,2,1,0:T(8,128)(2,1)S(1)}, bf16[2,3,384,128]{3,2,1,0:T(8,128)(2,1)}, u32[]{:S(2)}) copy-start(bf16[2,3,384,128]{3,2,1,0:T(8,128)(2,1)} %get-tuple-element.79.refs_4_) | copy-start | bytes 1769476
  66.4 6.0 %copy-start.13 = (bf16[1,3,384,128]{3,2,1,0:T(8,128)(2,1)S(1)}, bf16[1,3,384,128]{3,2,1,0:T(8,128)(2,1)}, u32[]{:S(2)}) copy-start(bf16[1,3,384,128]{3,2,1,0:T(8,128)(2,1)} %get-tuple-element.74.refs_0_) | copy-start | bytes 884740
  66.4 18.8 %collective-permute-start.16 = (bf16[2,2,384,128]{3,2,1,0:T(8,128)(2,1)S(1)}, bf16[2,2,384,128]{3,2,1,0:T(8,128)(2,1)S(1)}, u32[]{:S(2)}, u32[]{:S(2)}) collective-permute-start(bf16[2,2,384,128]{3,2,1,0:T(8,128)(2,1)S(1)} %get-tuple-element.88), channel_id=1, source_target_pairs={{2,6},{3,7},{4,0},{5,1},{6,10},{7,11},{8,4},{9,5},{10,14},{11,15},... | collective-permute-start | bytes 1179656 | tf_op jit(solution)/shard_map/far_back0/ppermute | solution.py:420
  68.0 20.8 %collective-permute-start.13 = (bf16[2,2,384,128]{3,2,1,0:T(8,128)(2,1)S(1)}, bf16[2,2,384,128]{3,2,1,0:T(8,128)(2,1)S(1)}, u32[]{:S(2)}, u32[]{:S(2)}) collective-permute-start(bf16[2,2,384,128]{3,2,1,0:T(8,128)(2,1)S(1)} %gather.4), channel_id=1, source_target_pairs={{0,4},{1,5},{4,8},{5,9},{6,2},{7,3},{8,12},{9,13},{10,6},{11,7},{1... | collective-permute-start | bytes 1179656 | tf_op jit(solution)/shard_map/far2/ppermute | solution.py:420
  80.4 28.2 %collective-permute-start.25 = (bf16[2,1,384,128]{3,2,1,0:T(8,128)(2,1)S(1)}, bf16[2,1,384,128]{3,2,1,0:T(8,128)(2,1)S(1)}, u32[]{:S(2)}, u32[]{:S(2)}) collective-permute-start(bf16[2,1,384,128]{3,2,1,0:T(8,128)(2,1)S(1)} %get-tuple-element.111), channel_id=1, source_target_pairs={{0,4},{1,5},{4,8},{5,9},{6,2},{7,3},{8,12},{9,13},{10,6},{11,7},{1... | collective-permute-start | bytes 589832 | tf_op jit(solution)/shard_map/near_back1/ppermute | solution.py:420
  83.7 26.2 %collective-permute-start.26 = (bf16[2,1,384,128]{3,2,1,0:T(8,128)(2,1)S(1)}, bf16[2,1,384,128]{3,2,1,0:T(8,128)(2,1)S(1)}, u32[]{:S(2)}, u32[]{:S(2)}) collective-permute-start(bf16[2,1,384,128]{3,2,1,0:T(8,128)(2,1)S(1)} %get-tuple-element.112), channel_id=1, source_target_pairs={{2,6},{3,7},{4,0},{5,1},{6,10},{7,11},{8,4},{9,5},{10,14},{11,15},... | collective-permute-start | bytes 589832 | tf_op jit(solution)/shard_map/far_back1/ppermute | solution.py:420
  85.5 24.4 %collective-permute-start.27 = (bf16[2,2,384,128]{3,2,1,0:T(8,128)(2,1)S(1)}, bf16[2,2,384,128]{3,2,1,0:T(8,128)(2,1)S(1)}, u32[]{:S(2)}, u32[]{:S(2)}) collective-permute-start(bf16[2,2,384,128]{3,2,1,0:T(8,128)(2,1)S(1)} %get-tuple-element.117), channel_id=1, source_target_pairs={{0,2},{1,3},{2,0},{3,1},{4,6},{5,7},{6,4},{7,5},{8,10},{9,11},{10,... | collective-permute-start | bytes 1179656 | tf_op jit(solution)/shard_map/sums0/ppermute | solution.py:411
  85.6 25.4 %collective-permute-start.28 = (bf16[2,2,384,128]{3,2,1,0:T(8,128)(2,1)S(1)}, bf16[2,2,384,128]{3,2,1,0:T(8,128)(2,1)S(1)}, u32[]{:S(2)}, u32[]{:S(2)}) collective-permute-start(bf16[2,2,384,128]{3,2,1,0:T(8,128)(2,1)S(1)} %get-tuple-element.118), channel_id=1, source_target_pairs={{0,3},{1,2},{2,1},{3,0},{4,7},{5,6},{6,5},{7,4},{8,11},{9,10},{10,... | collective-permute-start | bytes 1179656 | tf_op jit(solution)/shard_map/sums0/ppermute | solution.py:411
  104.3 12.1 %collective-permute-start.17 = (bf16[2,2,384,128]{3,2,1,0:T(8,128)(2,1)S(1)}, bf16[2,2,384,128]{3,2,1,0:T(8,128)(2,1)S(1)}, u32[]{:S(2)}, u32[]{:S(2)}) collective-permute-start(bf16[2,2,384,128]{3,2,1,0:T(8,128)(2,1)S(1)} %get-tuple-element.98), channel_id=1, source_target_pairs={{0,4},{1,5},{4,8},{5,9},{6,2},{7,3},{8,12},{9,13},{10,6},{11,7},{1... | collective-permute-start | bytes 1179656 | tf_op jit(solution)/shard_map/near_back2/ppermute | solution.py:420
  108.6 12.3 %collective-permute-start.18 = (bf16[2,2,384,128]{3,2,1,0:T(8,128)(2,1)S(1)}, bf16[2,2,384,128]{3,2,1,0:T(8,128)(2,1)S(1)}, u32[]{:S(2)}, u32[]{:S(2)}) collective-permute-start(bf16[2,2,384,128]{3,2,1,0:T(8,128)(2,1)S(1)} %get-tuple-element.99), channel_id=1, source_target_pairs={{2,6},{3,7},{4,0},{5,1},{6,10},{7,11},{8,4},{9,5},{10,14},{11,15},... | collective-permute-start | bytes 1179656 | tf_op jit(solution)/shard_map/far_back2/ppermute | solution.py:420
  109.9 13.0 %collective-permute-start.32 = (bf16[2,2,384,128]{3,2,1,0:T(8,128)(2,1)S(1)}, bf16[2,2,384,128]{3,2,1,0:T(8,128)(2,1)S(1)}, u32[]{:S(2)}, u32[]{:S(2)}) collective-permute-start(bf16[2,2,384,128]{3,2,1,0:T(8,128)(2,1)S(1)} %follow.13), channel_id=1, source_target_pairs={{0,1},{1,0},{2,3},{3,2},{4,5},{5,4},{6,7},{7,6},{8,9},{9,8},{10,11... | collective-permute-start | bytes 1179656 | tf_op jit(solution)/shard_map/sums_partner0/ppermute | solution.py:411
  110.0 11.1 %collective-permute-start.23 = (bf16[1,2,384,128]{3,2,1,0:T(8,128)(2,1)S(1)}, bf16[1,2,384,128]{3,2,1,0:T(8,128)(2,1)S(1)}, u32[]{:S(2)}, u32[]{:S(2)}) collective-permute-start(bf16[1,2,384,128]{3,2,1,0:T(8,128)(2,1)S(1)} %get-tuple-element.106), channel_id=1, source_target_pairs={{0,2},{1,3},{2,0},{3,1},{4,6},{5,7},{6,4},{7,5},{8,10},{9,11},{10,... | collective-permute-start | bytes 589832 | tf_op jit(solution)/shard_map/results2/ppermute | solution.py:411
  111.1 11.8 %collective-permute-start.29 = (bf16[2,1,384,128]{3,2,1,0:T(8,128)(2,1)S(1)}, bf16[2,1,384,128]{3,2,1,0:T(8,128)(2,1)S(1)}, u32[]{:S(2)}, u32[]{:S(2)}) collective-permute-start(bf16[2,1,384,128]{3,2,1,0:T(8,128)(2,1)S(1)} %follow.12), channel_id=1, source_target_pairs={{0,1},{1,0},{2,3},{3,2},{4,5},{5,4},{6,7},{7,6},{8,9},{9,8},{10,11... | collective-permute-start | bytes 589832 | tf_op jit(solution)/shard_map/sums_partner1/ppermute | solution.py:411
  116.4 7.0 %collective-permute-start.30 = (bf16[2,1,384,128]{3,2,1,0:T(8,128)(2,1)S(1)}, bf16[2,1,384,128]{3,2,1,0:T(8,128)(2,1)S(1)}, u32[]{:S(2)}, u32[]{:S(2)}) collective-permute-start(bf16[2,1,384,128]{3,2,1,0:T(8,128)(2,1)S(1)} %get-tuple-element.121), channel_id=1, source_target_pairs={{0,2},{1,3},{2,0},{3,1},{4,6},{5,7},{6,4},{7,5},{8,10},{9,11},{10,... | collective-permute-start | bytes 589832 | tf_op jit(solution)/shard_map/sums1/ppermute | solution.py:411
  120.8 7.5 %collective-permute-start.31 = (bf16[2,1,384,128]{3,2,1,0:T(8,128)(2,1)S(1)}, bf16[2,1,384,128]{3,2,1,0:T(8,128)(2,1)S(1)}, u32[]{:S(2)}, u32[]{:S(2)}) collective-permute-start(bf16[2,1,384,128]{3,2,1,0:T(8,128)(2,1)S(1)} %get-tuple-element.122), channel_id=1, source_target_pairs={{0,3},{1,2},{2,1},{3,0},{4,7},{5,6},{6,5},{7,4},{8,11},{9,10},{10,... | collective-permute-start | bytes 589832 | tf_op jit(solution)/shard_map/sums1/ppermute | solution.py:411
  121.1 11.1 %collective-permute-start.24 = (bf16[1,2,384,128]{3,2,1,0:T(8,128)(2,1)S(1)}, bf16[1,2,384,128]{3,2,1,0:T(8,128)(2,1)S(1)}, u32[]{:S(2)}, u32[]{:S(2)}) collective-permute-start(bf16[1,2,384,128]{3,2,1,0:T(8,128)(2,1)S(1)} %get-tuple-element.107), channel_id=1, source_target_pairs={{0,3},{1,2},{2,1},{3,0},{4,7},{5,6},{6,5},{7,4},{8,11},{9,10},{10,... | collective-permute-start | bytes 589832 | tf_op jit(solution)/shard_map/results2/ppermute | solution.py:411
  122.9 9.3 %collective-permute-start.22 = (bf16[1,2,384,128]{3,2,1,0:T(8,128)(2,1)S(1)}, bf16[1,2,384,128]{3,2,1,0:T(8,128)(2,1)S(1)}, u32[]{:S(2)}, u32[]{:S(2)}) collective-permute-start(bf16[1,2,384,128]{3,2,1,0:T(8,128)(2,1)S(1)} %follow.11), channel_id=1, source_target_pairs={{0,1},{1,0},{2,3},{3,2},{4,5},{5,4},{6,7},{7,6},{8,9},{9,8},{10,11... | collective-permute-start | bytes 589832 | tf_op jit(solution)/shard_map/results2/ppermute | solution.py:411
  122.9 9.3 %collective-permute-start.19 = (bf16[1,2,384,128]{3,2,1,0:T(8,128)(2,1)S(1)}, bf16[1,2,384,128]{3,2,1,0:T(8,128)(2,1)S(1)}, u32[]{:S(2)}, u32[]{:S(2)}) collective-permute-start(bf16[1,2,384,128]{3,2,1,0:T(8,128)(2,1)S(1)} %get-tuple-element.101), channel_id=1, source_target_pairs={{0,1},{1,0},{2,3},{3,2},{4,5},{5,4},{6,7},{7,6},{8,9},{9,8},{10,11... | collective-permute-start | bytes 589832 | tf_op jit(solution)/shard_map/sums_partner2/ppermute | solution.py:411
  123.4 11.7 %collective-permute-start.20 = (bf16[1,2,384,128]{3,2,1,0:T(8,128)(2,1)S(1)}, bf16[1,2,384,128]{3,2,1,0:T(8,128)(2,1)S(1)}, u32[]{:S(2)}, u32[]{:S(2)}) collective-permute-start(bf16[1,2,384,128]{3,2,1,0:T(8,128)(2,1)S(1)} %get-tuple-element.102), channel_id=1, source_target_pairs={{0,2},{1,3},{2,0},{3,1},{4,6},{5,7},{6,4},{7,5},{8,10},{9,11},{10,... | collective-permute-start | bytes 589832 | tf_op jit(solution)/shard_map/sums2/ppermute | solution.py:411
  128.3 11.6 %collective-permute-start.21 = (bf16[1,2,384,128]{3,2,1,0:T(8,128)(2,1)S(1)}, bf16[1,2,384,128]{3,2,1,0:T(8,128)(2,1)S(1)}, u32[]{:S(2)}, u32[]{:S(2)}) collective-permute-start(bf16[1,2,384,128]{3,2,1,0:T(8,128)(2,1)S(1)} %get-tuple-element.103), channel_id=1, source_target_pairs={{0,3},{1,2},{2,1},{3,0},{4,7},{5,6},{6,5},{7,4},{8,11},{9,10},{10,... | collective-permute-start | bytes 589832 | tf_op jit(solution)/shard_map/sums2/ppermute | solution.py:411

commit v4 on v3

--- a/solution.py
+++ b/solution.py
@@ -16,9 +16,9 @@
 MIN_LIVE = 4
 QUAD = 4
 PIECES = 2 * QUAD
-INS = (2, 1, 2)
+INS = (2, 2, 1)
 OWNS = (2, 3)
-OUTS = ((2, False), (1, False), (2, True))
+OUTS = ((2, False), (2, False), (1, False))
 COSTS = {"pack": 1.0, "gather": 0.5, "attend": 8.0, "combine": 0.3, "unpack": 0.8}
 LOG2E = math.log2(math.e)
 PACK_VMEM = 60 * 1024 * 1024

time: 142 us -> 160 us (1.13)
  local copies, waits for them, and re-layouts: 1.51 us -> 8.74 us
  waiting for transfers between devices: 32.3 us -> 37.8 us
  starting transfers between devices: 44.7 us -> 47.6 us
  Pallas kernels: 61.8 us -> 63.6 us
    unnamed x28 -> x50, local copies, waits for them, and re-layouts: 1.51 us -> 8.74 us
    ppermute x22 -> x19, waiting for transfers between devices: 19.9 us -> 25.8 us  [across(): return lax.ppermute(x, 'tm', [(i, i ^ flip) for i in range(shards)])]
    ppermute x22 -> x19, starting transfers between devices: 16.4 us -> 18.4 us  [across(): return lax.ppermute(x, 'tm', [(i, i ^ flip) for i in range(shards)])]
    pallas_call x3, Pallas kernels: 39.9 us -> 41.7 us  [attend(): pl.pallas_call(functools.partial(attend_body, blocks=blocks, after=len(af...]
  transfers between devices with their start and end apart: 33 -> 30, of which waited for: 10 -> 10; matrix products, arithmetic and copies ran while one was open for 0% -> 0% of each run, Pallas kernels for 40% -> 37%
where the time goes in v4:
time: 160 us; the launch traced here: 159 us
  Pallas kernels  63.6 us (40%)
  starting transfers between devices  47.6 us (30%)
  waiting for transfers between devices  37.8 us (24%)
  local copies, waits for them, and re-layouts  8.74 us (5%)
    pallas_call x3, Pallas kernels, attend(): pl.pallas_call(functools.partial(attend_body, blocks=blocks, after=len(af...  41.7 us
    ppermute x11, starting transfers between devices, along(): return lax.ppermute(x, 'tm', route)  29.2 us
    ppermute x19, waiting for transfers between devices, across(): return lax.ppermute(x, 'tm', [(i, i ^ flip) for i in range(shards)])  25.8 us
    ppermute x19, starting transfers between devices, across(): return lax.ppermute(x, 'tm', [(i, i ^ flip) for i in range(shards)])  18.4 us
    pallas_call x5, Pallas kernels, pack(): pl.pallas_call(functools.partial(pack_body, heads=heads, own=own, planned...  15.7 us
    ppermute x11, waiting for transfers between devices, along(): return lax.ppermute(x, 'tm', route)  11.9 us
    unnamed x50, local copies, waits for them, and re-layouts  8.74 us
    pallas_call x3, Pallas kernels, unpack(): pl.pallas_call(unpack_body, grid_spec=pltpu.PrefetchScalarGridSpec(num_sc...  3.94 us
  transfers between devices with their start and end apart: 30, of which 10 were waited for; matrix products, arithmetic and copies ran while one was open for 0% of the time, Pallas kernels for 37%

profile of v4, /device:TPU:1, one launch (start us, length us, event | category | flops | bytes accessed | tf_op | source)
XLA Modules:
  0.0 158.8 jit_solution(7613134580730359429)
XLA Ops:
  0.6 3.1 %pack.5 = (bf16[2,2,400,128]{3,2,1,0:T(8,128)(2,1)}, bf16[2,2,400,128]{3,2,1,0:T(8,128)(2,1)}) custom-call(s32[1]{0:T(128)} %bitcast.place, s32[3,8]{1,0:T(4,128)} %lists.11, s32[3]{0:T(128)} %counts.11, bf16[384,1280]{1,0:T(8,128)(2,1)} %refs_0_.9, bf16[384,1280]{1,0:T(8,128)(2,1)} %refs_1_.9, bf16[384,1280]{1,0:T(8,128)(2,1)} %refs_2_.9, ...), custom_call_target="tpu_custom_call" | custom-call | flops 2305999872 | tf_op jit(solution)/shard_map/pack/pallas_call | solution.py:100
  3.8 2.1 %collective-permute-start = (bf16[2,2,400,128]{3,2,1,0:T(8,128)(2,1)}, bf16[2,2,400,128]{3,2,1,0:T(8,128)(2,1)S(1)}, u32[]{:S(2)}, u32[]{:S(2)}) collective-permute-start(bf16[2,2,400,128]{3,2,1,0:T(8,128)(2,1)} %get-tuple-element.70), channel_id=1, source_target_pairs={{0,2},{1,3},{2,0},{3,1},{4,6},{5,7},{6,4},{7,5},{8,10},{9,11},{10,... | collective-permute-start | bytes 1228808 | tf_op jit(solution)/shard_map/facing0/ppermute | solution.py:411
  6.4 3.2 %pack.6 = (bf16[2,2,384,128]{3,2,1,0:T(8,128)(2,1)}, bf16[2,2,400,128]{3,2,1,0:T(8,128)(2,1)}, bf16[1,2,384,128]{3,2,1,0:T(8,128)(2,1)}) custom-call(s32[1]{0:T(128)} %bitcast.place, s32[3,8]{1,0:T(4,128)} %lists.11, s32[3]{0:T(128)} %counts.11, bf16[384,1280]{1,0:T(8,128)(2,1)} %refs_0_.9, bf16[384,1280]{1,0:T(8,128)(2,1)} %refs_1_.9, ...), custom_call_target="tpu_custom_call" | custom-call | flops 2305999872 | tf_op jit(solution)/shard_map/pack/pallas_call | solution.py:100
  9.6 1.3 collective-permute-start.10
  10.9 3.1 %pack.7 = (bf16[2,2,384,128]{3,2,1,0:T(8,128)(2,1)}, bf16[2,2,384,128]{3,2,1,0:T(8,128)(2,1)}) custom-call(s32[1]{0:T(128)} %bitcast.place, s32[3,8]{1,0:T(4,128)} %lists.11, s32[3]{0:T(128)} %counts.11, bf16[384,1280]{1,0:T(8,128)(2,1)} %refs_0_.9, bf16[384,1280]{1,0:T(8,128)(2,1)} %refs_1_.9, bf16[384,1280]{1,0:T(8,128)(2,1)} %refs_2_.9, ...), custom_call_target="tpu_custom_call" | custom-call | flops 2305999872 | tf_op jit(solution)/shard_map/pack/pallas_call | solution.py:100
  14.0 3.6 %pack.8 = (bf16[2,3,384,128]{3,2,1,0:T(8,128)(2,1)}, bf16[2,3,384,128]{3,2,1,0:T(8,128)(2,1)}, bf16[1,3,384,128]{3,2,1,0:T(8,128)(2,1)}) custom-call(s32[1]{0:T(128)} %bitcast.place, s32[3,8]{1,0:T(4,128)} %lists.11, s32[3]{0:T(128)} %counts.11, bf16[384,1280]{1,0:T(8,128)(2,1)} %refs_0_.9, bf16[384,1280]{1,0:T(8,128)(2,1)} %refs_1_.9, ...), custom_call_target="tpu_custom_call" | custom-call | flops 3459000064 | tf_op jit(solution)/shard_map/pack/pallas_call | solution.py:100
  17.6 1.3 collective-permute-start.8
  19.3 3.4 %collective-permute-done.10.refs_8_ = bf16[2,2,384,128]{3,2,1,0:T(8,128)(2,1)S(1)} collective-permute-done((bf16[2,2,384,128]{3,2,1,0:T(8,128)(2,1)}, bf16[2,2,384,128]{3,2,1,0:T(8,128)(2,1)S(1)}, u32[]{:S(2)}, u32[]{:S(2)}) %collective-permute-start.10) | collective-permute-done | bytes 393248 | tf_op jit(solution)/shard_map/near0/ppermute | solution.py:420
  22.7 0.8 collective-permute-start.11
  23.5 1.4 collective-permute-done.1.crossing_ref.refs_1_.refs_3_.refs_7_
  25.7 3.4 %collective-permute-start.12 = (bf16[2,2,384,128]{3,2,1,0:T(8,128)(2,1)S(1)}, bf16[2,2,384,128]{3,2,1,0:T(8,128)(2,1)S(1)}, u32[]{:S(2)}, u32[]{:S(2)}) collective-permute-start(bf16[2,2,384,128]{3,2,1,0:T(8,128)(2,1)S(1)} %gather.3), channel_id=1, source_target_pairs={{0,4},{1,5},{4,8},{5,9},{6,2},{7,3},{8,12},{9,13},{10,6},{11,7},{1... | collective-permute-start | bytes 1179656 | tf_op jit(solution)/shard_map/far0/ppermute | solution.py:420
  29.4 0.8 copy-done.1
  31.2 4.5 %collective-permute-done.8.refs_8_ = bf16[2,3,384,128]{3,2,1,0:T(8,128)(2,1)} collective-permute-done((bf16[2,3,384,128]{3,2,1,0:T(8,128)(2,1)}, bf16[2,3,384,128]{3,2,1,0:T(8,128)(2,1)}, u32[]{:S(2)}, u32[]{:S(2)}) %collective-permute-start.8) | collective-permute-done | bytes 589856 | tf_op jit(solution)/shard_map/near1/ppermute | solution.py:420
  35.7 2.5 %collective-permute-start.6 = (bf16[2,2,384,128]{3,2,1,0:T(8,128)(2,1)S(1)}, bf16[2,2,384,128]{3,2,1,0:T(8,128)(2,1)S(1)}, u32[]{:S(2)}, u32[]{:S(2)}) collective-permute-start(bf16[2,2,384,128]{3,2,1,0:T(8,128)(2,1)S(1)} %copy-done.24), channel_id=1, source_target_pairs={{0,3},{1,2},{2,1},{3,0},{4,7},{5,6},{6,5},{7,4},{8,11},{9,10},{10,... | collective-permute-start | bytes 1179656 | tf_op jit(solution)/shard_map/crossing1/ppermute | solution.py:411
  38.2 0.7 copy-done.16
  38.9 0.7 copy-done.20
  39.7 1.0 copy-done.12
  40.7 1.0 copy-done.17
  41.7 1.0 copy-done.21
  42.7 16.2 %attend.3 = (bf16[2,2,384,128]{3,2,1,0:T(8,128)(2,1)S(1)}, bf16[2,2,384,128]{3,2,1,0:T(8,128)(2,1)S(1)}, bf16[2,2,384,128]{3,2,1,0:T(8,128)(2,1)S(1)}, bf16[2,2,...) custom-call(s32[8,128]{1,0:T(8,128)S(1)} %route.1.plan, ...), custom_call_target="tpu_custom_call" | custom-call | flops 18447998976 | tf_op jit(solution)/shard_map/attend/pallas_call | solution.py:347
  59.7 4.1 %collective-permute-start.14 = (bf16[2,2,384,128]{3,2,1,0:T(8,128)(2,1)S(1)}, bf16[2,2,384,128]{3,2,1,0:T(8,128)(2,1)S(1)}, u32[]{:S(2)}, u32[]{:S(2)}) collective-permute-start(bf16[2,2,384,128]{3,2,1,0:T(8,128)(2,1)S(1)} %gather.5), channel_id=1, source_target_pairs={{0,4},{1,5},{4,8},{5,9},{6,2},{7,3},{8,12},{9,13},{10,6},{11,7},{1... | collective-permute-start | bytes 1179656 | tf_op jit(solution)/shard_map/far1/ppermute | solution.py:420
  63.8 2.7 %pack.9 = (bf16[2,1,384,128]{3,2,1,0:T(8,128)(2,1)}, bf16[2,1,384,128]{3,2,1,0:T(8,128)(2,1)}) custom-call(s32[1]{0:T(128)} %bitcast.place, s32[3,8]{1,0:T(4,128)} %lists.11, s32[3]{0:T(128)} %counts.11, bf16[384,1280]{1,0:T(8,128)(2,1)} %refs_0_.9, bf16[384,1280]{1,0:T(8,128)(2,1)} %refs_1_.9, bf16[384,1280]{1,0:T(8,128)(2,1)} %refs_2_.9, ...), custom_call_target="tpu_custom_call" | custom-call | flops 1152999936 | tf_op jit(solution)/shard_map/pack/pallas_call | solution.py:100
  66.5 2.4 %collective-permute-start.7 = (bf16[2,1,384,128]{3,2,1,0:T(8,128)(2,1)}, bf16[2,1,384,128]{3,2,1,0:T(8,128)(2,1)S(1)}, u32[]{:S(2)}, u32[]{:S(2)}) collective-permute-start(bf16[2,1,384,128]{3,2,1,0:T(8,128)(2,1)} %follow.9), channel_id=1, source_target_pairs={{0,3},{1,2},{2,1},{3,0},{4,7},{5,6},{6,5},{7,4},{8,11},{9,10},{10,... | collective-permute-start | bytes 589832 | tf_op jit(solution)/shard_map/crossing2/ppermute | solution.py:411
  68.9 3.5 %collective-permute-done.5.facing_ref.refs_2_.refs_6_ = bf16[2,1,384,128]{3,2,1,0:T(8,128)(2,1)} collective-permute-done((bf16[2,1,384,128]{3,2,1,0:T(8,128)(2,1)}, bf16[2,1,384,128]{3,2,1,0:T(8,128)(2,1)}, u32[]{:S(2)}, u32[]{:S(2)}) %collective-permute-start.5) | collective-permute-done | bytes 196640 | tf_op jit(solution)/shard_map/facing2/ppermute | solution.py:411
  72.5 3.2 %collective-permute-start.15 = (bf16[2,2,384,128]{3,2,1,0:T(8,128)(2,1)}, bf16[2,2,384,128]{3,2,1,0:T(8,128)(2,1)S(1)}, u32[]{:S(2)}, u32[]{:S(2)}) collective-permute-start(bf16[2,2,384,128]{3,2,1,0:T(8,128)(2,1)} %get-tuple-element.87), channel_id=1, source_target_pairs={{0,4},{1,5},{4,8},{5,9},{6,2},{7,3},{8,12},{9,13},{10,6},{11,7},{1... | collective-permute-start | bytes 1179656 | tf_op jit(solution)/shard_map/near_back0/ppermute | solution.py:420
  75.7 1.9 %collective-permute-done.7.crossing_ref.refs_3_.refs_7_ = bf16[2,1,384,128]{3,2,1,0:T(8,128)(2,1)S(1)} collective-permute-done((bf16[2,1,384,128]{3,2,1,0:T(8,128)(2,1)}, bf16[2,1,384,128]{3,2,1,0:T(8,128)(2,1)S(1)}, u32[]{:S(2)}, u32[]{:S(2)}) %collective-permute-start.7) | collective-permute-done | bytes 196640 | tf_op jit(solution)/shard_map/crossing2/ppermute | solution.py:411
  77.6 1.4 collective-permute-start.16
  79.0 0.9 gather.4
  79.9 4.2 %collective-permute-start.13 = (bf16[2,1,384,128]{3,2,1,0:T(8,128)(2,1)S(1)}, bf16[2,1,384,128]{3,2,1,0:T(8,128)(2,1)S(1)}, u32[]{:S(2)}, u32[]{:S(2)}) collective-permute-start(bf16[2,1,384,128]{3,2,1,0:T(8,128)(2,1)S(1)} %gather.4), channel_id=1, source_target_pairs={{0,4},{1,5},{4,8},{5,9},{6,2},{7,3},{8,12},{9,13},{10,6},{11,7},{1... | collective-permute-start | bytes 589832 | tf_op jit(solution)/shard_map/far2/ppermute | solution.py:420
  84.9 1.0 copy-done.19
  85.9 16.4 %attend.4 = (bf16[2,2,384,128]{3,2,1,0:T(8,128)(2,1)S(1)}, bf16[2,2,384,128]{3,2,1,0:T(8,128)(2,1)S(1)}, bf16[2,2,384,128]{3,2,1,0:T(8,128)(2,1)S(1)}, bf16[2,2,...) custom-call(s32[8,128]{1,0:T(8,128)S(1)} %route.1.plan, ...), custom_call_target="tpu_custom_call" | custom-call | flops 18447998976 | tf_op jit(solution)/shard_map/attend/pallas_call | solution.py:347
  102.3 3.2 %collective-permute-start.22 = (bf16[2,2,384,128]{3,2,1,0:T(8,128)(2,1)S(1)}, bf16[2,2,384,128]{3,2,1,0:T(8,128)(2,1)S(1)}, u32[]{:S(2)}, u32[]{:S(2)}) collective-permute-start(bf16[2,2,384,128]{3,2,1,0:T(8,128)(2,1)S(1)} %get-tuple-element.111), channel_id=1, source_target_pairs={{0,4},{1,5},{4,8},{5,9},{6,2},{7,3},{8,12},{9,13},{10,6},{11,7},{1... | collective-permute-start | bytes 1179656 | tf_op jit(solution)/shard_map/near_back1/ppermute | solution.py:420
  105.6 1.5 collective-permute-start.23
  108.1 1.9 %collective-permute-start.25 = (bf16[2,2,384,128]{3,2,1,0:T(8,128)(2,1)S(1)}, bf16[2,2,384,128]{3,2,1,0:T(8,128)(2,1)S(1)}, u32[]{:S(2)}, u32[]{:S(2)}) collective-permute-start(bf16[2,2,384,128]{3,2,1,0:T(8,128)(2,1)S(1)} %get-tuple-element.118), channel_id=1, source_target_pairs={{0,3},{1,2},{2,1},{3,0},{4,7},{5,6},{6,5},{7,4},{8,11},{9,10},{10,... | collective-permute-start | bytes 1179656 | tf_op jit(solution)/shard_map/sums0/ppermute | solution.py:411
  110.1 9.1 %attend.5 = (bf16[2,1,384,128]{3,2,1,0:T(8,128)(2,1)S(1)}, bf16[2,1,384,128]{3,2,1,0:T(8,128)(2,1)S(1)}, bf16[2,1,384,128]{3,2,1,0:T(8,128)(2,1)S(1)}, bf16[2,1,...) custom-call(s32[8,128]{1,0:T(8,128)S(1)} %route.1.plan, ...), custom_call_target="tpu_custom_call" | custom-call | flops 9223999488 | tf_op jit(solution)/shard_map/attend/pallas_call | solution.py:347
  119.1 4.3 %collective-permute-start.17 = (bf16[2,1,384,128]{3,2,1,0:T(8,128)(2,1)S(1)}, bf16[2,1,384,128]{3,2,1,0:T(8,128)(2,1)S(1)}, u32[]{:S(2)}, u32[]{:S(2)}) collective-permute-start(bf16[2,1,384,128]{3,2,1,0:T(8,128)(2,1)S(1)} %get-tuple-element.98), channel_id=1, source_target_pairs={{0,4},{1,5},{4,8},{5,9},{6,2},{7,3},{8,12},{9,13},{10,6},{11,7},{1... | collective-permute-start | bytes 589832 | tf_op jit(solution)/shard_map/near_back2/ppermute | solution.py:420
  123.5 3.2 %collective-permute-done.25.refs_12_.refs_3_.refs_7_ = bf16[2,2,384,128]{3,2,1,0:T(8,128)(2,1)S(1)} collective-permute-done((bf16[2,2,384,128]{3,2,1,0:T(8,128)(2,1)S(1)}, bf16[2,2,384,128]{3,2,1,0:T(8,128)(2,1)S(1)}, u32[]{:S(2)}, u32[]{:S(2)}) %collective-permute-start.25) | collective-permute-done | bytes 393248 | tf_op jit(solution)/shard_map/sums0/ppermute | solution.py:411
  127.1 1.3 collective-permute-start.18
  128.4 3.1 %collective-permute-start.27 = (bf16[2,2,384,128]{3,2,1,0:T(8,128)(2,1)S(1)}, bf16[2,2,384,128]{3,2,1,0:T(8,128)(2,1)S(1)}, u32[]{:S(2)}, u32[]{:S(2)}) collective-permute-start(bf16[2,2,384,128]{3,2,1,0:T(8,128)(2,1)S(1)} %get-tuple-element.121), channel_id=1, source_target_pairs={{0,2},{1,3},{2,0},{3,1},{4,6},{5,7},{6,4},{7,5},{8,10},{9,11},{10,... | collective-permute-start | bytes 1179656 | tf_op jit(solution)/shard_map/sums1/ppermute | solution.py:411
  132.2 4.0 %collective-permute-done.18.refs_5_ = bf16[2,1,384,128]{3,2,1,0:T(8,128)(2,1)S(1)} collective-permute-done((bf16[2,1,384,128]{3,2,1,0:T(8,128)(2,1)S(1)}, bf16[2,1,384,128]{3,2,1,0:T(8,128)(2,1)S(1)}, u32[]{:S(2)}, u32[]{:S(2)}) %collective-permute-start.18) | collective-permute-done | bytes 196640 | tf_op jit(solution)/shard_map/far_back2/ppermute | solution.py:420
  136.3 1.1 collective-permute-start.19
  137.4 1.7 %collective-permute-start.21 = (bf16[2,1,384,128]{3,2,1,0:T(8,128)(2,1)S(1)}, bf16[2,1,384,128]{3,2,1,0:T(8,128)(2,1)S(1)}, u32[]{:S(2)}, u32[]{:S(2)}) collective-permute-start(bf16[2,1,384,128]{3,2,1,0:T(8,128)(2,1)S(1)} %get-tuple-element.107), channel_id=1, source_target_pairs={{0,3},{1,2},{2,1},{3,0},{4,7},{5,6},{6,5},{7,4},{8,11},{9,10},{10,... | collective-permute-start | bytes 589832 | tf_op jit(solution)/shard_map/sums2/ppermute | solution.py:411
  139.1 1.4 unpack.3
  140.5 9.7 %collective-permute-done.28.refs_3_.refs_7_ = bf16[2,2,384,128]{3,2,1,0:T(8,128)(2,1)S(1)} collective-permute-done((bf16[2,2,384,128]{3,2,1,0:T(8,128)(2,1)S(1)}, bf16[2,2,384,128]{3,2,1,0:T(8,128)(2,1)S(1)}, u32[]{:S(2)}, u32[]{:S(2)}) %collective-permute-start.28) | collective-permute-done | bytes 393248 | tf_op jit(solution)/shard_map/sums1/ppermute | solution.py:411
  150.2 1.4 unpack.4
  151.7 1.2 collective-permute-done.20.refs_2_.refs_6_
  152.9 4.9 %collective-permute-done.21.refs_3_.refs_7_ = bf16[2,1,384,128]{3,2,1,0:T(8,128)(2,1)S(1)} collective-permute-done((bf16[2,1,384,128]{3,2,1,0:T(8,128)(2,1)S(1)}, bf16[2,1,384,128]{3,2,1,0:T(8,128)(2,1)S(1)}, u32[]{:S(2)}, u32[]{:S(2)}) %collective-permute-start.21) | collective-permute-done | bytes 196640 | tf_op jit(solution)/shard_map/sums2/ppermute | solution.py:411
  157.7 1.1 unpack.5
  (86 shorter events, 6.7 us)
Async XLA Ops:
  3.8 19.8 %collective-permute-start = (bf16[2,2,400,128]{3,2,1,0:T(8,128)(2,1)}, bf16[2,2,400,128]{3,2,1,0:T(8,128)(2,1)S(1)}, u32[]{:S(2)}, u32[]{:S(2)}) collective-permute-start(bf16[2,2,400,128]{3,2,1,0:T(8,128)(2,1)} %get-tuple-element.70), channel_id=1, source_target_pairs={{0,2},{1,3},{2,0},{3,1},{4,6},{5,7},{6,4},{7,5},{8,10},{9,11},{10,... | collective-permute-start | bytes 1228808 | tf_op jit(solution)/shard_map/facing0/ppermute | solution.py:411
  5.8 19.1 %collective-permute-start.1 = (bf16[2,2,400,128]{3,2,1,0:T(8,128)(2,1)}, bf16[2,2,400,128]{3,2,1,0:T(8,128)(2,1)S(1)}, u32[]{:S(2)}, u32[]{:S(2)}) collective-permute-start(bf16[2,2,400,128]{3,2,1,0:T(8,128)(2,1)} %get-tuple-element.71.refs_8_), channel_id=1, source_target_pairs={{0,3},{1,2},{2,1},{3,0},{4,7},{5,6},{6,5},{7,4},{8,11},{9,10},{10,... | collective-permute-start | bytes 1228808 | tf_op jit(solution)/shard_map/crossing0/ppermute | solution.py:411
  9.6 13.1 %collective-permute-start.10 = (bf16[2,2,384,128]{3,2,1,0:T(8,128)(2,1)}, bf16[2,2,384,128]{3,2,1,0:T(8,128)(2,1)S(1)}, u32[]{:S(2)}, u32[]{:S(2)}) collective-permute-start(bf16[2,2,384,128]{3,2,1,0:T(8,128)(2,1)} %get-tuple-element.81.refs_4_), channel_id=1, source_target_pairs={{2,6},{3,7},{4,0},{5,1},{6,10},{7,11},{8,4},{9,5},{10,14},{11,15},... | collective-permute-start | bytes 1179656 | tf_op jit(solution)/shard_map/near0/ppermute | solution.py:420
  17.6 18.1 %collective-permute-start.8 = (bf16[2,3,384,128]{3,2,1,0:T(8,128)(2,1)}, bf16[2,3,384,128]{3,2,1,0:T(8,128)(2,1)}, u32[]{:S(2)}, u32[]{:S(2)}) collective-permute-start(bf16[2,3,384,128]{3,2,1,0:T(8,128)(2,1)} %get-tuple-element.79.refs_4_), channel_id=1, source_target_pairs={{2,6},{3,7},{4,0},{5,1},{6,10},{7,11},{8,4},{9,5},{10,14},{11,15},... | collective-permute-start | bytes 1769480 | tf_op jit(solution)/shard_map/near1/ppermute | solution.py:420
  18.9 10.5 %collective-permute-start.2 = (bf16[2,2,400,128]{3,2,1,0:T(8,128)(2,1)}, bf16[2,2,400,128]{3,2,1,0:T(8,128)(2,1)S(1)}, u32[]{:S(2)}, u32[]{:S(2)}) collective-permute-start(bf16[2,2,400,128]{3,2,1,0:T(8,128)(2,1)} %get-tuple-element.72.refs_8_), channel_id=1, source_target_pairs={{0,1},{1,0},{2,3},{3,2},{4,5},{5,4},{6,7},{7,6},{8,9},{9,8},{10,11... | collective-permute-start | bytes 1228808 | tf_op jit(solution)/shard_map/partner0/ppermute | solution.py:411
  22.7 2.4 %copy-start.14 = (bf16[2,2,384,128]{3,2,1,0:T(8,128)(2,1)}, bf16[2,2,384,128]{3,2,1,0:T(8,128)(2,1)S(1)}, u32[]{:S(2)}) copy-start(bf16[2,2,384,128]{3,2,1,0:T(8,128)(2,1)S(1)} %collective-permute-done.10.refs_8_) | copy-start | bytes 1179652
  22.7 15.5 %collective-permute-start.11 = (bf16[2,2,384,128]{3,2,1,0:T(8,128)(2,1)S(1)}, bf16[2,2,384,128]{3,2,1,0:T(8,128)(2,1)S(1)}, u32[]{:S(2)}, u32[]{:S(2)}) collective-permute-start(bf16[2,2,384,128]{3,2,1,0:T(8,128)(2,1)S(1)} %collective-permute-done.10.refs_8_), channel_id=1, source_target_pairs={{0,1},{1,0},{2,3},{3,2},{4,5},{5,4},{6,7},{7,6},{8,9},{9,8},{10,11... | collective-permute-start | bytes 1179656 | tf_op jit(solution)/shard_map/near_partner0/ppermute | solution.py:411
  23.5 1.5 copy-start
  25.7 13.2 %collective-permute-start.12 = (bf16[2,2,384,128]{3,2,1,0:T(8,128)(2,1)S(1)}, bf16[2,2,384,128]{3,2,1,0:T(8,128)(2,1)S(1)}, u32[]{:S(2)}, u32[]{:S(2)}) collective-permute-start(bf16[2,2,384,128]{3,2,1,0:T(8,128)(2,1)S(1)} %gather.3), channel_id=1, source_target_pairs={{0,4},{1,5},{4,8},{5,9},{6,2},{7,3},{8,12},{9,13},{10,6},{11,7},{1... | collective-permute-start | bytes 1179656 | tf_op jit(solution)/shard_map/far0/ppermute | solution.py:420
  29.2 50.8 %collective-permute-start.3 = (bf16[2,3,384,128]{3,2,1,0:T(8,128)(2,1)}, bf16[2,3,384,128]{3,2,1,0:T(8,128)(2,1)}, u32[]{:S(2)}, u32[]{:S(2)}) collective-permute-start(bf16[2,3,384,128]{3,2,1,0:T(8,128)(2,1)} %get-tuple-element.75.refs_4_), channel_id=1, source_target_pairs={{0,1},{1,0},{2,3},{3,2},{4,5},{5,4},{6,7},{7,6},{8,9},{9,8},{10,11... | collective-permute-start | bytes 1769480 | tf_op jit(solution)/shard_map/partner1/ppermute | solution.py:411
  29.3 1.0 copy-start.1
  29.3 1.3 copy-start.3
  29.3 1.3 copy-start.8
  29.3 1.2 copy-start.9
  29.3 6.3 %copy-start.24 = (bf16[2,2,384,128]{3,2,1,0:T(8,128)(2,1)S(1)}, bf16[2,2,384,128]{3,2,1,0:T(8,128)(2,1)}, u32[]{:S(2)}) copy-start(bf16[2,2,384,128]{3,2,1,0:T(8,128)(2,1)} %follow.8) | copy-start | bytes 1179652
  29.3 10.3 %copy-start.13 = (bf16[2,2,384,128]{3,2,1,0:T(8,128)(2,1)S(1)}, bf16[2,2,384,128]{3,2,1,0:T(8,128)(2,1)}, u32[]{:S(2)}) copy-start(bf16[2,2,384,128]{3,2,1,0:T(8,128)(2,1)} %get-tuple-element.81.refs_4_) | copy-start | bytes 1179652
  29.3 10.3 %copy-start.15 = (bf16[2,2,384,128]{3,2,1,0:T(8,128)(2,1)S(1)}, bf16[2,2,384,128]{3,2,1,0:T(8,128)(2,1)}, u32[]{:S(2)}) copy-start(bf16[2,2,384,128]{3,2,1,0:T(8,128)(2,1)} %copy-done.14) | copy-start | bytes 1179652
  29.3 10.3 %copy-start.22 = (bf16[1,2,384,128]{3,2,1,0:T(8,128)(2,1)S(1)}, bf16[1,2,384,128]{3,2,1,0:T(8,128)(2,1)}, u32[]{:S(2)}) copy-start(bf16[1,2,384,128]{3,2,1,0:T(8,128)(2,1)} %get-tuple-element.80.refs_0_) | copy-start | bytes 589828
  29.4 1.8 %copy-start.11 = (bf16[2,2,400,128]{3,2,1,0:T(8,128)(2,1)}, bf16[2,2,400,128]{3,2,1,0:T(8,128)(2,1)S(1)}, u32[]{:S(2)}) copy-start(bf16[2,2,400,128]{3,2,1,0:T(8,128)(2,1)S(1)} %collective-permute-done.2.partner_ref.refs_1_.refs_5_) | copy-start | bytes 1228804
  29.4 29.5 %collective-permute-start.4 = (bf16[2,2,384,128]{3,2,1,0:T(8,128)(2,1)}, bf16[2,2,384,128]{3,2,1,0:T(8,128)(2,1)S(1)}, u32[]{:S(2)}, u32[]{:S(2)}) collective-permute-start(bf16[2,2,384,128]{3,2,1,0:T(8,128)(2,1)} %follow.6), channel_id=1, source_target_pairs={{0,2},{1,3},{2,0},{3,1},{4,6},{5,7},{6,4},{7,5},{8,10},{9,11},{10,... | collective-permute-start | bytes 1179656 | tf_op jit(solution)/shard_map/facing1/ppermute | solution.py:411
  35.7 23.2 %collective-permute-start.6 = (bf16[2,2,384,128]{3,2,1,0:T(8,128)(2,1)S(1)}, bf16[2,2,384,128]{3,2,1,0:T(8,128)(2,1)S(1)}, u32[]{:S(2)}, u32[]{:S(2)}) collective-permute-start(bf16[2,2,384,128]{3,2,1,0:T(8,128)(2,1)S(1)} %copy-done.24), channel_id=1, source_target_pairs={{0,3},{1,2},{2,1},{3,0},{4,7},{5,6},{6,5},{7,4},{8,11},{9,10},{10,... | collective-permute-start | bytes 1179656 | tf_op jit(solution)/shard_map/crossing1/ppermute | solution.py:411
  38.9 45.2 %collective-permute-start.9 = (bf16[2,3,384,128]{3,2,1,0:T(8,128)(2,1)}, bf16[2,3,384,128]{3,2,1,0:T(8,128)(2,1)}, u32[]{:S(2)}, u32[]{:S(2)}) collective-permute-start(bf16[2,3,384,128]{3,2,1,0:T(8,128)(2,1)} %collective-permute-done.8.refs_8_), channel_id=1, source_target_pairs={{0,1},{1,0},{2,3},{3,2},{4,5},{5,4},{6,7},{7,6},{8,9},{9,8},{10,11... | collective-permute-start | bytes 1769480 | tf_op jit(solution)/shard_map/near_partner1/ppermute | solution.py:411
  39.7 1.0 copy-start.12
  40.7 1.0 copy-start.17
  59.7 24.4 %collective-permute-start.14 = (bf16[2,2,384,128]{3,2,1,0:T(8,128)(2,1)S(1)}, bf16[2,2,384,128]{3,2,1,0:T(8,128)(2,1)S(1)}, u32[]{:S(2)}, u32[]{:S(2)}) collective-permute-start(bf16[2,2,384,128]{3,2,1,0:T(8,128)(2,1)S(1)} %gather.5), channel_id=1, source_target_pairs={{0,4},{1,5},{4,8},{5,9},{6,2},{7,3},{8,12},{9,13},{10,6},{11,7},{1... | collective-permute-start | bytes 1179656 | tf_op jit(solution)/shard_map/far1/ppermute | solution.py:420
  66.5 5.9 %collective-permute-start.5 = (bf16[2,1,384,128]{3,2,1,0:T(8,128)(2,1)}, bf16[2,1,384,128]{3,2,1,0:T(8,128)(2,1)}, u32[]{:S(2)}, u32[]{:S(2)}) collective-permute-start(bf16[2,1,384,128]{3,2,1,0:T(8,128)(2,1)} %follow.7), channel_id=1, source_target_pairs={{0,2},{1,3},{2,0},{3,1},{4,6},{5,7},{6,4},{7,5},{8,10},{9,11},{10,... | collective-permute-start | bytes 589832 | tf_op jit(solution)/shard_map/facing2/ppermute | solution.py:411
  66.5 11.0 %collective-permute-start.7 = (bf16[2,1,384,128]{3,2,1,0:T(8,128)(2,1)}, bf16[2,1,384,128]{3,2,1,0:T(8,128)(2,1)S(1)}, u32[]{:S(2)}, u32[]{:S(2)}) collective-permute-start(bf16[2,1,384,128]{3,2,1,0:T(8,128)(2,1)} %follow.9), channel_id=1, source_target_pairs={{0,3},{1,2},{2,1},{3,0},{4,7},{5,6},{6,5},{7,4},{8,11},{9,10},{10,... | collective-permute-start | bytes 589832 | tf_op jit(solution)/shard_map/crossing2/ppermute | solution.py:411
  72.5 34.6 %collective-permute-start.15 = (bf16[2,2,384,128]{3,2,1,0:T(8,128)(2,1)}, bf16[2,2,384,128]{3,2,1,0:T(8,128)(2,1)S(1)}, u32[]{:S(2)}, u32[]{:S(2)}) collective-permute-start(bf16[2,2,384,128]{3,2,1,0:T(8,128)(2,1)} %get-tuple-element.87), channel_id=1, source_target_pairs={{0,4},{1,5},{4,8},{5,9},{6,2},{7,3},{8,12},{9,13},{10,6},{11,7},{1... | collective-permute-start | bytes 1179656 | tf_op jit(solution)/shard_map/near_back0/ppermute | solution.py:420
  77.6 7.3 %copy-start.5 = (bf16[2,2,384,128]{3,2,1,0:T(8,128)(2,1)S(1)}, bf16[2,2,384,128]{3,2,1,0:T(8,128)(2,1)}, u32[]{:S(2)}) copy-start(bf16[2,2,384,128]{3,2,1,0:T(8,128)(2,1)} %copy-done.4) | copy-start | bytes 1179652
  77.6 7.3 %copy-start.7 = (bf16[2,2,384,128]{3,2,1,0:T(8,128)(2,1)S(1)}, bf16[2,2,384,128]{3,2,1,0:T(8,128)(2,1)}, u32[]{:S(2)}) copy-start(bf16[2,2,384,128]{3,2,1,0:T(8,128)(2,1)} %copy-done.6) | copy-start | bytes 1179652
  77.6 7.3 %copy-start.10 = (bf16[2,3,384,128]{3,2,1,0:T(8,128)(2,1)S(1)}, bf16[2,3,384,128]{3,2,1,0:T(8,128)(2,1)}, u32[]{:S(2)}) copy-start(bf16[2,3,384,128]{3,2,1,0:T(8,128)(2,1)} %get-tuple-element.79.refs_4_) | copy-start | bytes 1769476
  77.6 7.3 %copy-start.23 = (bf16[1,3,384,128]{3,2,1,0:T(8,128)(2,1)S(1)}, bf16[1,3,384,128]{3,2,1,0:T(8,128)(2,1)}, u32[]{:S(2)}) copy-start(bf16[1,3,384,128]{3,2,1,0:T(8,128)(2,1)} %get-tuple-element.74.refs_0_) | copy-start | bytes 884740
  77.6 29.5 %collective-permute-start.16 = (bf16[2,2,384,128]{3,2,1,0:T(8,128)(2,1)}, bf16[2,2,384,128]{3,2,1,0:T(8,128)(2,1)S(1)}, u32[]{:S(2)}, u32[]{:S(2)}) collective-permute-start(bf16[2,2,384,128]{3,2,1,0:T(8,128)(2,1)} %get-tuple-element.88), channel_id=1, source_target_pairs={{2,6},{3,7},{4,0},{5,1},{6,10},{7,11},{8,4},{9,5},{10,14},{11,15},... | collective-permute-start | bytes 1179656 | tf_op jit(solution)/shard_map/far_back0/ppermute | solution.py:420
  79.9 30.1 %collective-permute-start.13 = (bf16[2,1,384,128]{3,2,1,0:T(8,128)(2,1)S(1)}, bf16[2,1,384,128]{3,2,1,0:T(8,128)(2,1)S(1)}, u32[]{:S(2)}, u32[]{:S(2)}) collective-permute-start(bf16[2,1,384,128]{3,2,1,0:T(8,128)(2,1)S(1)} %gather.4), channel_id=1, source_target_pairs={{0,4},{1,5},{4,8},{5,9},{6,2},{7,3},{8,12},{9,13},{10,6},{11,7},{1... | collective-permute-start | bytes 589832 | tf_op jit(solution)/shard_map/far2/ppermute | solution.py:420
  84.9 1.0 copy-start.19
  102.3 21.1 %collective-permute-start.22 = (bf16[2,2,384,128]{3,2,1,0:T(8,128)(2,1)S(1)}, bf16[2,2,384,128]{3,2,1,0:T(8,128)(2,1)S(1)}, u32[]{:S(2)}, u32[]{:S(2)}) collective-permute-start(bf16[2,2,384,128]{3,2,1,0:T(8,128)(2,1)S(1)} %get-tuple-element.111), channel_id=1, source_target_pairs={{0,4},{1,5},{4,8},{5,9},{6,2},{7,3},{8,12},{9,13},{10,6},{11,7},{1... | collective-permute-start | bytes 1179656 | tf_op jit(solution)/shard_map/near_back1/ppermute | solution.py:420
  105.6 17.9 %collective-permute-start.23 = (bf16[2,2,384,128]{3,2,1,0:T(8,128)(2,1)S(1)}, bf16[2,2,384,128]{3,2,1,0:T(8,128)(2,1)S(1)}, u32[]{:S(2)}, u32[]{:S(2)}) collective-permute-start(bf16[2,2,384,128]{3,2,1,0:T(8,128)(2,1)S(1)} %get-tuple-element.112), channel_id=1, source_target_pairs={{2,6},{3,7},{4,0},{5,1},{6,10},{7,11},{8,4},{9,5},{10,14},{11,15},... | collective-permute-start | bytes 1179656 | tf_op jit(solution)/shard_map/far_back1/ppermute | solution.py:420
  107.4 16.1 %collective-permute-start.24 = (bf16[2,2,384,128]{3,2,1,0:T(8,128)(2,1)S(1)}, bf16[2,2,384,128]{3,2,1,0:T(8,128)(2,1)S(1)}, u32[]{:S(2)}, u32[]{:S(2)}) collective-permute-start(bf16[2,2,384,128]{3,2,1,0:T(8,128)(2,1)S(1)} %get-tuple-element.117), channel_id=1, source_target_pairs={{0,2},{1,3},{2,0},{3,1},{4,6},{5,7},{6,4},{7,5},{8,10},{9,11},{10,... | collective-permute-start | bytes 1179656 | tf_op jit(solution)/shard_map/sums0/ppermute | solution.py:411
  108.1 18.7 %collective-permute-start.25 = (bf16[2,2,384,128]{3,2,1,0:T(8,128)(2,1)S(1)}, bf16[2,2,384,128]{3,2,1,0:T(8,128)(2,1)S(1)}, u32[]{:S(2)}, u32[]{:S(2)}) collective-permute-start(bf16[2,2,384,128]{3,2,1,0:T(8,128)(2,1)S(1)} %get-tuple-element.118), channel_id=1, source_target_pairs={{0,3},{1,2},{2,1},{3,0},{4,7},{5,6},{6,5},{7,4},{8,11},{9,10},{10,... | collective-permute-start | bytes 1179656 | tf_op jit(solution)/shard_map/sums0/ppermute | solution.py:411
  119.1 12.3 %collective-permute-start.17 = (bf16[2,1,384,128]{3,2,1,0:T(8,128)(2,1)S(1)}, bf16[2,1,384,128]{3,2,1,0:T(8,128)(2,1)S(1)}, u32[]{:S(2)}, u32[]{:S(2)}) collective-permute-start(bf16[2,1,384,128]{3,2,1,0:T(8,128)(2,1)S(1)} %get-tuple-element.98), channel_id=1, source_target_pairs={{0,4},{1,5},{4,8},{5,9},{6,2},{7,3},{8,12},{9,13},{10,6},{11,7},{1... | collective-permute-start | bytes 589832 | tf_op jit(solution)/shard_map/near_back2/ppermute | solution.py:420
  123.4 13.9 %collective-permute-start.29 = (bf16[2,2,384,128]{3,2,1,0:T(8,128)(2,1)S(1)}, bf16[2,2,384,128]{3,2,1,0:T(8,128)(2,1)S(1)}, u32[]{:S(2)}, u32[]{:S(2)}) collective-permute-start(bf16[2,2,384,128]{3,2,1,0:T(8,128)(2,1)S(1)} %follow.11), channel_id=1, source_target_pairs={{0,1},{1,0},{2,3},{3,2},{4,5},{5,4},{6,7},{7,6},{8,9},{9,8},{10,11... | collective-permute-start | bytes 1179656 | tf_op jit(solution)/shard_map/sums_partner0/ppermute | solution.py:411
  127.0 10.4 %collective-permute-start.26 = (bf16[2,2,384,128]{3,2,1,0:T(8,128)(2,1)S(1)}, bf16[2,2,384,128]{3,2,1,0:T(8,128)(2,1)S(1)}, u32[]{:S(2)}, u32[]{:S(2)}) collective-permute-start(bf16[2,2,384,128]{3,2,1,0:T(8,128)(2,1)S(1)} %follow.10), channel_id=1, source_target_pairs={{0,1},{1,0},{2,3},{3,2},{4,5},{5,4},{6,7},{7,6},{8,9},{9,8},{10,11... | collective-permute-start | bytes 1179656 | tf_op jit(solution)/shard_map/sums_partner1/ppermute | solution.py:411
  127.1 9.1 %collective-permute-start.18 = (bf16[2,1,384,128]{3,2,1,0:T(8,128)(2,1)S(1)}, bf16[2,1,384,128]{3,2,1,0:T(8,128)(2,1)S(1)}, u32[]{:S(2)}, u32[]{:S(2)}) collective-permute-start(bf16[2,1,384,128]{3,2,1,0:T(8,128)(2,1)S(1)} %get-tuple-element.99), channel_id=1, source_target_pairs={{2,6},{3,7},{4,0},{5,1},{6,10},{7,11},{8,4},{9,5},{10,14},{11,15},... | collective-permute-start | bytes 589832 | tf_op jit(solution)/shard_map/far_back2/ppermute | solution.py:420
  128.4 12.1 %collective-permute-start.27 = (bf16[2,2,384,128]{3,2,1,0:T(8,128)(2,1)S(1)}, bf16[2,2,384,128]{3,2,1,0:T(8,128)(2,1)S(1)}, u32[]{:S(2)}, u32[]{:S(2)}) collective-permute-start(bf16[2,2,384,128]{3,2,1,0:T(8,128)(2,1)S(1)} %get-tuple-element.121), channel_id=1, source_target_pairs={{0,2},{1,3},{2,0},{3,1},{4,6},{5,7},{6,4},{7,5},{8,10},{9,11},{10,... | collective-permute-start | bytes 1179656 | tf_op jit(solution)/shard_map/sums1/ppermute | solution.py:411
  131.5 18.7 %collective-permute-start.28 = (bf16[2,2,384,128]{3,2,1,0:T(8,128)(2,1)S(1)}, bf16[2,2,384,128]{3,2,1,0:T(8,128)(2,1)S(1)}, u32[]{:S(2)}, u32[]{:S(2)}) collective-permute-start(bf16[2,2,384,128]{3,2,1,0:T(8,128)(2,1)S(1)} %get-tuple-element.122), channel_id=1, source_target_pairs={{0,3},{1,2},{2,1},{3,0},{4,7},{5,6},{6,5},{7,4},{8,11},{9,10},{10,... | collective-permute-start | bytes 1179656 | tf_op jit(solution)/shard_map/sums1/ppermute | solution.py:411
  136.3 15.4 %collective-permute-start.19 = (bf16[2,1,384,128]{3,2,1,0:T(8,128)(2,1)S(1)}, bf16[2,1,384,128]{3,2,1,0:T(8,128)(2,1)S(1)}, u32[]{:S(2)}, u32[]{:S(2)}) collective-permute-start(bf16[2,1,384,128]{3,2,1,0:T(8,128)(2,1)S(1)} %get-tuple-element.105), channel_id=1, source_target_pairs={{0,1},{1,0},{2,3},{3,2},{4,5},{5,4},{6,7},{7,6},{8,9},{9,8},{10,11... | collective-permute-start | bytes 589832 | tf_op jit(solution)/shard_map/sums_partner2/ppermute | solution.py:411
  137.4 15.5 %collective-permute-start.20 = (bf16[2,1,384,128]{3,2,1,0:T(8,128)(2,1)S(1)}, bf16[2,1,384,128]{3,2,1,0:T(8,128)(2,1)S(1)}, u32[]{:S(2)}, u32[]{:S(2)}) collective-permute-start(bf16[2,1,384,128]{3,2,1,0:T(8,128)(2,1)S(1)} %get-tuple-element.106), channel_id=1, source_target_pairs={{0,2},{1,3},{2,0},{3,1},{4,6},{5,7},{6,4},{7,5},{8,10},{9,11},{10,... | collective-permute-start | bytes 589832 | tf_op jit(solution)/shard_map/sums2/ppermute | solution.py:411
  137.4 20.3 %collective-permute-start.21 = (bf16[2,1,384,128]{3,2,1,0:T(8,128)(2,1)S(1)}, bf16[2,1,384,128]{3,2,1,0:T(8,128)(2,1)S(1)}, u32[]{:S(2)}, u32[]{:S(2)}) collective-permute-start(bf16[2,1,384,128]{3,2,1,0:T(8,128)(2,1)S(1)} %get-tuple-element.107), channel_id=1, source_target_pairs={{0,3},{1,2},{2,1},{3,0},{4,7},{5,6},{6,5},{7,4},{8,11},{9,10},{10,... | collective-permute-start | bytes 589832 | tf_op jit(solution)/shard_map/sums2/ppermute | solution.py:411
  (7 other events, 5.6 us)
